TPU v7x, 32 devices: a whole 2x2x4 slice. The times are simulated.
32 devices in a mesh: seq: 8 (over z, y), head: 4 (over x, core).
Axes of the slice: x: 2, y: 2, z: 4, core: 2. Of those that a mesh axis runs over, the one named last changes fastest.
Arguments:
- tokens: bfloat16 [3072, 4096], P('seq', 'head'), may hold values from -6 to 6
- norm_gain: float32 [4096], replicated, may hold values from 0.25 to 1.75
- w_in: bfloat16 [4096, 8, 2304], P('seq', 'head'), may hold values from -0.09375 to 0.09375
- w_dt: bfloat16 [4096, 128], P('seq', 'head'), may hold values from -0.09375 to 0.09375
- dt_bias: float32 [128], P('head'), may hold values from -3 to -1
- a_log: float32 [128], P('head'), may hold values from -11 to -1
- d_skip: float32 [128], P('head'), may hold values from 0.5 to 1.5
- conv_w: float32 [4, 8, 1280], P(None, 'head'), may hold values from -0.5 to 0.5
- conv_b: float32 [8, 1280], P('head'), may hold values from -0.5 to 0.5
- gate_gain: float32 [8, 1024], P('head'), may hold values from 0.25 to 1.75
- w_out: bfloat16 [8, 1024, 4096], P('head'), may hold values from -0.09375 to 0.09375
Outputs:
- mixed: bfloat16 [3072, 4096], P('seq', 'head')
All inputs are finite; a program needn't handle non-finite values.
Results may differ from a plain program's by a relative error of at most 0.018.
Values may be sent and summed in bfloat16 or wider, within the bound.
No kernel may reach another device: no remote copies, remote signals or barrier semaphores. Data moves between devices by JAX's collectives and lax.ppermute only.
A program may use at most 128 MiB of HBM per device.

v0:
```python
from functools import partial

import jax
import jax.numpy as jnp
from jax import lax
from jax.sharding import PartitionSpec as P

STRETCH = 128


EPS = 1e-05
HIGHEST = lax.Precision.HIGHEST


def from_behind(shard, axis, by):
    count = lax.axis_size(axis)
    pairs = [(i, i + by) for i in range(count) if 0 <= i + by < count]
    return lax.ppermute(shard, axis, pairs)


def carried_in(shard, axis, combine, identity):
    count, index = (lax.axis_size(axis), lax.axis_index(axis))
    everything = jax.tree.map(
        lambda part, kind: lax.all_gather(part.astype(kind), axis),
        shard,
        (jnp.bfloat16, jnp.bfloat16),
    )
    start = jax.tree.map(
        lambda part, zero: jnp.broadcast_to(jnp.asarray(zero, part.dtype), part.shape),
        shard,
        identity,
    )

    def lap(k, before):
        reached = k < index
        new = combine(
            before, jax.tree.map(lambda part, own: part[k].astype(own.dtype), everything, shard)
        )
        return jax.tree.map(lambda a, b: jnp.where(reached, a, b), new, before)

    return lax.fori_loop(0, count, lap, start)


def normalize(values, gain):
    squares = jnp.mean(values * values, axis=-1, keepdims=True)
    return values * lax.rsqrt(squares + EPS) * gain


def state_block(inputs, step_size, log_decay, in_map, out_map, block_len):
    length = inputs.shape[0]
    stretch_count = length // block_len
    head_count = inputs.shape[1]
    head_size = inputs.shape[2]
    state_size = in_map.shape[1]
    shaped = (
        inputs.reshape(stretch_count, block_len, head_count, head_size),
        step_size.reshape(stretch_count, block_len, head_count),
        log_decay.reshape(stretch_count, block_len, head_count),
        in_map.reshape(stretch_count, block_len, state_size),
        out_map.reshape(stretch_count, block_len, state_size),
    )
    causal = jnp.arange(block_len)[:, None] >= jnp.arange(block_len)[None, :]

    def advance(state_now, pieces):
        stretch_in, stretch_step, stretch_log, stretch_b, stretch_c = pieces
        cumulative = jnp.cumsum(stretch_log, axis=0)
        gap_log = cumulative[:, None, :] - cumulative[None, :, :]
        decays = jnp.where(
            causal[:, :, None], jnp.exp(jnp.where(causal[:, :, None], gap_log, 0.0)), 0.0
        )
        scores = jnp.dot(stretch_c, stretch_b.T, preferred_element_type=jnp.float32)
        wide_c = stretch_c.astype(jnp.float32)
        wide_b = stretch_b.astype(jnp.float32)
        weights = scores[:, :, None] * decays * stretch_step[None, :, :]
        within = jnp.einsum("ijh,jhp->ihp", weights, stretch_in, precision=HIGHEST)
        across = jnp.exp(cumulative)[:, :, None] * jnp.einsum(
            "in,hpn->ihp", wide_c, state_now, precision=HIGHEST
        )
        to_end = jnp.exp(cumulative[-1][None, :] - cumulative) * stretch_step
        fresh_state = jnp.einsum("jh,jhp,jn->hpn", to_end, stretch_in, wide_b, precision=HIGHEST)
        state_next = jnp.exp(cumulative[-1])[:, None, None] * state_now + fresh_state
        return (state_next, within + across)

    start_state = jnp.zeros((head_count, head_size, state_size), jnp.float32)
    final, outputs = lax.scan(advance, start_state, shaped)
    return (outputs.reshape(length, head_count, head_size), final)


def link_states(earlier, later):
    return (earlier[0] + later[0], jnp.exp(later[0])[:, :, None, None] * earlier[1] + later[1])


def body(tokens, norm_gain, w_in, w_dt, dt_bias, a_log, d_skip, conv_w, conv_b, gate_gain, w_out):
    local_rows = tokens.shape[0]
    kernel_len = conv_w.shape[0]
    groups, group_width = gate_gain.shape
    head_count = dt_bias.shape[0]
    per_group = head_count // groups
    head_size = group_width // per_group
    state_size = (conv_b.shape[1] - group_width) // 2
    gathered = lax.all_gather(tokens, "head", axis=1, tiled=True)
    normed = normalize(gathered.astype(jnp.float32), norm_gain).astype(jnp.bfloat16)
    span_rows = normed.shape[0]
    flat_in = w_in.reshape(w_in.shape[0], groups * w_in.shape[2])
    proj_sum = jnp.dot(
        normed,
        lax.all_gather(flat_in, "seq", axis=0, tiled=True),
        preferred_element_type=jnp.float32,
    )
    step_sum = jnp.dot(
        normed, lax.all_gather(w_dt, "seq", axis=0, tiled=True), preferred_element_type=jnp.float32
    )
    projected = proj_sum.astype(jnp.bfloat16).reshape(span_rows, groups, w_in.shape[2])
    step_size = jax.nn.softplus(step_sum + dt_bias[None, :])
    gate_raw = projected[span_rows - local_rows :, :, :group_width]
    own_channels = projected[:, :, group_width:]
    rim_rows = from_behind(own_channels[local_rows - kernel_len + 1 :], "seq", 1)
    extended = jnp.concatenate([rim_rows, own_channels], axis=0)
    summed = conv_b[None, :, :]
    for offset in range(kernel_len):
        summed = summed + conv_w[offset][None, :, :] * extended[
            offset : offset + local_rows
        ].astype(jnp.float32)
    narrow = lax.optimization_barrier(jax.nn.silu(summed).astype(jnp.bfloat16))
    convolved = narrow.astype(jnp.float32)
    inputs = convolved[:, :, :group_width].reshape(local_rows, groups, per_group, head_size)
    in_map = narrow[:, :, group_width : group_width + state_size]
    out_map = narrow[:, :, group_width + state_size :]
    step_grouped = step_size.reshape(local_rows, groups, per_group)
    log_decay = -jnp.exp(a_log).reshape(groups, per_group)[None, :, :] * step_grouped
    run_block = jax.vmap(
        partial(state_block, block_len=STRETCH), in_axes=(1, 1, 1, 1, 1), out_axes=(1, 0)
    )
    local_out, ending = run_block(inputs, step_grouped, log_decay, in_map, out_map)
    totals = jnp.sum(log_decay, axis=0)
    identity = (jnp.zeros_like(totals), jnp.zeros_like(ending))
    prior_decay, incoming = carried_in((totals, ending), "seq", link_states, identity)
    cumulative = jnp.exp(jnp.cumsum(log_decay, axis=0))
    carried = (
        jnp.einsum("tgn,ghpn->tghp", out_map.astype(jnp.float32), incoming, precision=HIGHEST)
        * cumulative[:, :, :, None]
    )
    outputs = local_out + carried + d_skip.reshape(groups, per_group)[None, :, :, None] * inputs
    gated = outputs.reshape(local_rows, groups, group_width) * jax.nn.silu(
        gate_raw.astype(jnp.float32)
    )
    normed_out = normalize(gated, gate_gain[None, :, :]).astype(jnp.bfloat16)
    flat_out = normed_out.reshape(local_rows, groups * group_width)
    terms = jnp.dot(
        flat_out,
        w_out.reshape(groups * group_width, w_out.shape[2]),
        preferred_element_type=jnp.float32,
    )
    return lax.psum_scatter(terms.astype(jnp.bfloat16), "head", scatter_dimension=1, tiled=True)


def solution(mesh):
    in_specs = (
        P("seq", "head"),
        P(),
        P("seq", "head", None),
        P("seq", "head"),
        P("head"),
        P("head"),
        P("head"),
        P(None, "head", None),
        P("head", None),
        P("head", None),
        P("head", None, None),
    )
    out_specs = P("seq", "head")
    return jax.shard_map(body, mesh=mesh, in_specs=in_specs, out_specs=out_specs, check_vma=False)
```

profile of v0, /device:TPU:8, one launch (start us, length us, event | category | flops | bytes accessed | tf_op | source)
XLA Modules:
  0.0 1002.8 jit_solution(12846484459356773343)
XLA Ops:
  7.3 5.2 copy.74
  13.3 28.3 %all_gather.20 = bf16[4096,32]{0,1:T(8,128)(2,1)S(1)} all-gather(bf16[512,32]{0,1:T(8,128)(2,1)S(1)} %copy-done.12), channel_id=1, replica_groups=mesh['seq'=8,'head'=4] {'seq'}, dimensions={0}, use_global_device_ids=true | all-gather | bytes 294912 | tf_op jit(solution)/shard_map/all_gather | solution.py:111
  41.7 2.7 fusion.41
  45.7 710.8 %all-gather.7.cloned.1.call-done = bf16[4096,4608]{1,0:T(8,128)(2,1)} async-done(((bf16[512,4608]{1,0:T(8,128)(2,1)}), bf16[4096,4608]{1,0:T(8,128)(2,1)}) %all-gather.7.cloned.1.call-update) | async-done | bytes 37748752 | tf_op jit(solution)/shard_map/all_gather | solution.py:107
  756.6 21.8 %convolution_convert_fusion = bf16[384,4608]{1,0:T(8,128)(2,1)} fusion(bf16[4096,4608]{1,0:T(8,128)(2,1)} %all-gather.7.cloned.1.call-done, bf16[384,4096]{1,0:T(8,128)(2,1)} %all-gather.5.cloned.1.call-done, f32[4096]{0:T(1024)S(1)} %copy-done.14, f32[384]{0:T(512)S(1)} %add_rsqrt_fusion.1), kind=kOutput, calls=%fused_computation.49 | convolution fusion | flops 14503575552 | bytes 44451328 | tf_op jit(solution)/shard_map/dot_general | solution.py:105
  778.3 5.7 reshape.123
  785.0 2.7 collective-permute-start
  788.6 2.9 collective-permute-done
  791.5 2.9 multiply_convert_fusion
  794.5 2.3 slice_convert_fusion
  796.9 3.6 copy.50
  800.5 5.7 reshape.126
  806.3 44.0 %while.29 = (s32[]{:T(128)}, f32[2,16,64,128]{3,2,1,0:T(8,128)S(1)}, f32[3,2,128,16,64]{2,4,3,1,0:T(8,128)}, f32[3,2,128,16]{2,0,3,1:T(4,128)S(1)}, f32[3,2,128,...) while((s32[]{:T(128)}, ...), condition=%wide.region_3.4_spmd.clone.clone, body=%wide.region_1.3_spmd.clone.clone.sunk | while | flops 1221349376 | bytes 15371887 | solution.py:85
  806.3 3.5 constant_dynamic-slice_fusion.5
  810.5 4.2 fusion.95
  816.5 2.5 fusion.96
  819.1 1.9 convolution_add_fusion.3
  821.0 3.5 constant_dynamic-slice_fusion.5
  825.1 4.2 fusion.95
  831.2 2.5 fusion.96
  835.7 3.5 constant_dynamic-slice_fusion.5
  839.8 4.2 fusion.95
  845.8 2.5 fusion.96
  854.1 15.9 %all_gather.22 = bf16[8,2,16]{2,1,0:T(2,128)(2,1)S(1)} all-gather(bf16[1,2,16]{2,1,0:T(2,128)(2,1)S(1)} %convert_element_type.84), channel_id=1, replica_groups=mesh['seq'=8,'head'=4] {'seq'}, dimensions={0}, use_global_device_ids=true | all-gather | bytes 576 | tf_op jit(solution)/shard_map/all_gather | solution.py:24
  870.2 3.7 slice.80
  873.8 50.3 %all-gather.9.cloned.1.call-done = bf16[16,16,64,128]{3,2,1,0:T(8,128)(2,1)} async-done(((bf16[2,16,64,128]{3,2,1,0:T(8,128)(2,1)}), bf16[16,16,64,128]{3,2,1,0:T(8,128)(2,1)}) %all-gather.9.cloned.1.call-update) | async-done | bytes 4194320 | tf_op jit(solution)/shard_map/all_gather | solution.py:24
  924.1 10.7 %while.28 = (s32[]{:T(128)}, f32[2,16,64,128]{3,2,1,0:T(8,128)S(1)}, s32[]{:T(128)}, bf16[8,2,16]{2,1,0:T(2,128)(2,1)S(1)}, bf16[8,2,16,64,128]{4,3,2,1,0:T(8,128)(2,1)}, /*index=5*/s32[]{:T(128)}, s32[]{:T(128)}) while((s32[]{:T(128)}, f32[2,16,64,128]{3,2,1,0:T(8,128)S(1)}, s32[]{:T(128)}, bf16[8,2,16]{2,1,0:T(2,128)(2,1)S(1)}, ...), condition=%wide.region_6.7_spmd.clone, body=%wide.region_5.6_spmd.clone.sunk | while | flops 1310756 | bytes 2621873 | solution.py:41
  934.8 6.3 fusion.49
  941.1 2.4 copy.60
  943.5 2.6 multiply_reduce_fusion
  946.2 13.1 %bitcast_convert_fusion = bf16[384,4096]{1,0:T(8,128)(2,1)} fusion(bf16[2,1024,4096]{2,1,0:T(8,128)(2,1)} %param.25, f32[2,1024]{1,0:T(2,128)S(1)} %copy-done.15, f32[384,2]{0,1:T(2,128)S(1)} %add_rsqrt_fusion, f32[384,2,1024]{2,0,1:T(8,128)S(1)} %copy.60, bf16[384,2,1024]{2,1,0:T(2,128)(2,1)S(1)} %copy-done.1), kind=kOutput, calls=%fused_computation.53 | convolution fusion | flops 6451101696 | bytes 24652800 | tf_op jit(solution)/shard_map/dot_general | solution.py:149
  959.3 37.0 %reduce-scatter.2.cloned.1.call-done = bf16[384,1024]{1,0:T(8,128)(2,1)} async-done(((bf16[384,4096]{1,0:T(8,128)(2,1)}), bf16[384,1024]{1,0:T(8,128)(2,1)}) %reduce-scatter.2.cloned.1.call-update) | async-done | bytes 786448 | tf_op jit(solution)/shard_map/reduce_scatter | solution.py:154
  (161 shorter events, 30.2 us)
Async XLA Ops:
  6.5 35.1 %all-gather.5.cloned.1.call-start = ((), (), s32[]{:S(2)}) async-start(), calls=%async_computation.1 | async-start | bytes 3932160 | tf_op jit(solution)/shard_map/all_gather | solution.py:101
  7.3 749.3 %all-gather.7.cloned.1.call-start = ((), (), s32[]{:S(2)}) async-start(), calls=%async_computation.2 | async-start | bytes 42467328 | tf_op jit(solution)/shard_map/all_gather | solution.py:107
  12.6 29.1 %copy-start.11 = (f32[4,2,1280]{2,1,0:T(2,128)S(1)}, f32[4,2,1280]{2,1,0:T(2,128)}, u32[]{:S(2)}) copy-start(f32[4,2,1280]{2,1,0:T(2,128)} %param.22) | copy-start | bytes 122884
  12.6 31.8 %copy-start.14 = (f32[4096]{0:T(1024)S(1)}, f32[4096]{0:T(1024)}, u32[]{:S(2)}) copy-start(f32[4096]{0:T(1024)} %param.16) | copy-start | bytes 49156
  12.6 31.8 %copy-start.17 = (f32[32]{0:T(128)S(1)}, f32[32]{0:T(128)}, u32[]{:S(2)}) copy-start(f32[32]{0:T(128)} %param.19) | copy-start | bytes 388
  12.6 911.5 %all-gather.9.cloned.1.call-start = ((), (), s32[]{:S(2)}) async-start(), calls=%async_computation.4 | async-start | bytes 4718592 | tf_op jit(solution)/shard_map/all_gather | solution.py:24
  41.6 2.8 copy-start.6
  784.1 4.3 slice-start
  785.0 6.6 collective-permute-start
  788.4 3.1 copy-start.13
  794.5 2.3 copy-start
  806.3 45.0 %copy-start.18 = (f32[32]{0:T(128)S(1)}, f32[32]{0:T(128)}, u32[]{:S(2)}) copy-start(f32[32]{0:T(128)} %param.21) | copy-start | bytes 388
  806.3 4.1 copy-start.2
  806.3 4.1 copy-start.4
  806.3 4.1 copy-start.7
  806.3 4.1 copy-start.9
  819.0 2.0 copy-start.8
  819.0 2.0 copy-start.10
  821.0 4.1 copy-start.2
  821.0 4.1 copy-start.4
  821.0 4.1 copy-start.7
  821.0 4.1 copy-start.9
  833.6 2.0 copy-start.8
  833.6 2.0 copy-start.10
  835.6 4.1 copy-start.2
  835.6 4.1 copy-start.4
  835.7 4.1 copy-start.7
  835.7 4.1 copy-start.9
  848.3 2.0 copy-start.10
  851.2 145.1 %reduce-scatter.2.cloned.1.call-start = ((), (), s32[]{:S(2)}) async-start(), calls=%async_computation.3 | async-start | bytes 3932160 | tf_op jit(solution)/shard_map/reduce_scatter | solution.py:154
  943.5 2.7 copy-start.1
  943.5 2.7 copy-start.15
  (9 other events, 15.0 us)
Sparse Core Ops, SparseCore 0:
  8.9 29.6 all-gather.4
  40.2 716.3 all-gather.6
  851.3 72.7 all-gather.8
  959.4 36.8 reduce-scatter.1
where the time goes:
time: 1010 us; the launch traced here: 1000 us
  waiting for transfers between devices  802 us (79%)
  matrix products  68.7 us (7%)
  blocking collectives  44.2 us (4%)
  local copies, waits for them, and re-layouts  44 us (4%)
  other arithmetic  27.2 us (3%)
  between operations  13.4 us (1%)
    all_gather x1, waiting for transfers between devices, body(): lax.all_gather(flat_in, 'seq', axis=0, tiled=True)  711 us
    all_gather x1, waiting for transfers between devices, carried_in(): lax.all_gather(part.astype(kind), axis)  50.3 us
    reduce_scatter x1, waiting for transfers between devices, body(): lax.psum_scatter(terms.astype(jnp.bfloat16), 'head', scatter_dimension=1,...  37 us
    all_gather x1, blocking collectives, body(): lax.all_gather(w_dt, 'seq', axis=0, tiled=True)  28.3 us
    dot_general x1, matrix products, body(): jnp.dot(normed, lax.all_gather(flat_in, 'seq', axis=0, tiled=True), prefe...  21.8 us
  transfers between devices with their start and end apart: 5, of which 4 were waited for; matrix products, arithmetic and copies ran while one was open for 2% of the time, Pallas kernels for 0%

commit v1 on v0

--- a/solution.py
+++ b/solution.py
@@ -3,6 +3,8 @@
 import jax
 import jax.numpy as jnp
 from jax import lax
+from jax.experimental import pallas as pl
+from jax.experimental.pallas import tpu as pltpu
 from jax.sharding import PartitionSpec as P
 
 STRETCH = 128
@@ -10,6 +12,420 @@
 
 EPS = 1e-05
 HIGHEST = lax.Precision.HIGHEST
+VMEM_LIMIT = 58 * 1024 * 1024
+LANES = 128
+
+
+def swap(value, axis, bit):
+    count = lax.axis_size(axis)
+    return lax.ppermute(value, axis, [(i, i ^ bit) for i in range(count)])
+
+
+def after(values, *gates):
+    return lax.optimization_barrier((values, gates))[0]
+
+
+def silu_of(v):
+    return v * (1.0 / (1.0 + jnp.exp(-v)))
+
+
+def spread(columns, heads, width):
+    rows = columns.shape[0]
+    head_of = lax.broadcasted_iota(jnp.int32, (rows, heads * width), 1) // width
+    out = jnp.broadcast_to(columns[:, heads - 1 : heads], (rows, heads * width))
+    for j in range(heads - 2, -1, -1):
+        out = jnp.where(head_of == j, columns[:, j : j + 1], out)
+    return out
+
+
+def mixer_kernel(
+    cfg,
+    where_ref,
+    *refs,
+):
+    (shards, arrays, blocks, rows, feats, krows, heads, width, state_size, taps, dim) = cfg
+    pieces = [[refs[a * blocks + e] for e in range(blocks)] for a in range(arrays)]
+    at = arrays * blocks
+    mains = refs[at : at + shards]
+    maps = refs[at + shards : at + 2 * shards]
+    (dt_w, conv_w, conv_b, dt_bias, neg_rate, skip, out_ref, wbuf, xbuf, pbuf, cbuf, state, wsem, xsem) = refs[
+        at + 2 * shards :
+    ]
+    i = pl.program_id(0)
+    steps = pl.num_programs(0)
+    me_s, me_h = where_ref[0], where_ref[1]
+    chans = heads * width
+    conv_cols = chans + 2 * state_size
+    main_cols = 2 * chans
+    map_cols = 2 * state_size
+    per = feats // krows
+
+    def fetch(step, slot, start):
+        which = where_ref[2 + step]
+        for a in range(arrays):
+            @pl.when(which == a)
+            def _(a=a):
+                for e in range(blocks):
+                    copy = pltpu.make_async_copy(
+                        pieces[a][e], xbuf.at[slot, :, pl.ds(e * feats, feats)], xsem.at[slot, e]
+                    )
+                    if start:
+                        copy.start()
+                    else:
+                        copy.wait()
+
+    def weights(start):
+        for d in range(shards):
+            kb = me_s ^ d
+            row = ((kb // per) ^ me_h) * feats + (kb % per) * krows
+            row = pl.multiple_of(row, krows)
+            for n, (src, lo, cols) in enumerate(
+                ((mains[d], 0, main_cols), (maps[d], main_cols, map_cols))
+            ):
+                copy = pltpu.make_async_copy(
+                    src, wbuf.at[pl.ds(row, krows), pl.ds(lo, cols)], wsem.at[n, d]
+                )
+                if start:
+                    copy.start()
+                else:
+                    copy.wait()
+        for e in range(blocks):
+            src_row = pl.multiple_of((me_h ^ e) * feats, feats)
+            copy = pltpu.make_async_copy(
+                dt_w.at[pl.ds(src_row, feats), :],
+                wbuf.at[pl.ds(e * feats, feats), pl.ds(main_cols + map_cols, LANES)],
+                wsem.at[2, e],
+            )
+            if start:
+                copy.start()
+            else:
+                copy.wait()
+
+    slot = lax.rem(i, 2)
+
+    @pl.when(i == 0)
+    def _():
+        fetch(0, 0, True)
+        weights(True)
+        state[...] = jnp.zeros_like(state)
+        cbuf[0:8, :] = jnp.zeros((8, conv_cols), jnp.float32)
+
+    @pl.when(i + 1 < steps)
+    def _():
+        fetch(i + 1, 1 - slot, True)
+
+    @pl.when(i == 0)
+    def _():
+        weights(False)
+
+    fetch(i, slot, False)
+
+    total = main_cols + map_cols + LANES
+    squares = jnp.zeros((rows, 1), jnp.float32)
+    for e in range(blocks):
+        part = xbuf[slot, :, e * feats : (e + 1) * feats].astype(jnp.float32)
+        squares = squares + jnp.sum(part * part, axis=1, keepdims=True)
+    factor = lax.rsqrt(squares * (1.0 / dim) + EPS)
+    lo = 0
+    while lo < total:
+        cols = min(256, total - lo)
+        pbuf[:, lo : lo + cols] = (
+            jnp.dot(xbuf[slot], wbuf[:, lo : lo + cols], preferred_element_type=jnp.float32) * factor
+        )
+        lo += cols
+    cbuf[8 : 8 + rows, :] = pbuf[:, chans : chans + conv_cols].astype(jnp.bfloat16).astype(jnp.float32)
+
+    length = STRETCH
+    tri = lax.broadcasted_iota(jnp.int32, (length, length), 0) >= lax.broadcasted_iota(
+        jnp.int32, (length, length), 1
+    )
+    ones = jnp.where(tri, 1.0, 0.0).astype(jnp.float32)
+    lane_head = lax.broadcasted_iota(jnp.int32, (length, chans), 1) // width
+    for st in range(rows // length):
+        r0 = st * length
+        summed = conv_b[...]
+        for k in range(taps):
+            first = 8 - (taps - 1) + k + r0
+            summed = summed + conv_w[k : k + 1, :] * cbuf[first : first + length, :]
+        narrow = silu_of(summed).astype(jnp.bfloat16)
+        xin = narrow[:, :chans]
+        in_map = narrow[:, chans : chans + state_size]
+        out_map = narrow[:, chans + state_size :]
+        xf = xin.astype(jnp.float32)
+        raw = pbuf[r0 : r0 + length, total - LANES :] + dt_bias[...]
+        step = jnp.maximum(raw, 0.0) + jnp.log1p(jnp.exp(-jnp.abs(raw)))
+        logd = neg_rate[...] * step
+        cum = jnp.dot(ones, logd, preferred_element_type=jnp.float32, precision=HIGHEST)
+        last = cum[length - 1 : length, :]
+        cum_t = cum.T
+        step_t = step.T
+        scores = lax.dot_general(
+            out_map, in_map, (((1,), (1,)), ((), ())), preferred_element_type=jnp.float32
+        )
+        weighted, spaced = [], []
+        for j in range(heads):
+            gap = cum[:, j : j + 1] - cum_t[j : j + 1, :]
+            decay = jnp.where(tri, jnp.exp(jnp.where(tri, gap, 0.0)), 0.0)
+            weighted.append((scores * decay * step_t[j : j + 1, :]).astype(jnp.bfloat16))
+            spaced.append(jnp.where(lane_head == j, xf, 0.0).astype(jnp.bfloat16))
+        within = jnp.dot(
+            jnp.concatenate(weighted, axis=1),
+            jnp.concatenate(spaced, axis=0),
+            preferred_element_type=jnp.float32,
+        )
+        now = state[...]
+        across = jnp.dot(out_map, now.astype(jnp.bfloat16), preferred_element_type=jnp.float32)
+        y = within + spread(jnp.exp(cum), heads, width) * across + skip[...] * xf
+        to_end = spread(jnp.exp(last - cum) * step, heads, width)
+        fresh = lax.dot_general(
+            in_map,
+            (xf * to_end).astype(jnp.bfloat16),
+            (((0,), (0,)), ((), ())),
+            preferred_element_type=jnp.float32,
+        )
+        state[...] = spread(jnp.exp(last), heads, width) * now + fresh
+        gate = pbuf[r0 : r0 + length, :chans].astype(jnp.bfloat16).astype(jnp.float32)
+        out_ref[r0 : r0 + length, :] = (y * silu_of(gate)).astype(jnp.bfloat16)
+    cbuf[0:8, :] = cbuf[rows : rows + 8, :]
+
+
+def mixer(where, pieces, mains, maps, dt_w, conv_w, conv_b, dt_bias, neg_rate, skip, rows, heads, width, dim):
+    arrays, blocks, shards = len(pieces), len(pieces[0]), len(mains)
+    feats = pieces[0][0].shape[1]
+    krows = mains[0].shape[0]
+    chans = heads * width
+    state_size = maps[0].shape[1] // 2
+    taps = conv_w.shape[0]
+    total = 2 * chans + 2 * state_size + LANES
+    cfg = (shards, arrays, blocks, rows, feats, krows, heads, width, state_size, taps, dim)
+    hbm = pl.BlockSpec(memory_space=pl.ANY)
+
+    def whole(a):
+        return pl.BlockSpec(a.shape, lambda i, w: (0,) * a.ndim)
+
+    small = (conv_w, conv_b, dt_bias, neg_rate, skip)
+    flat = [p for row in pieces for p in row]
+    return pl.pallas_call(
+        partial(mixer_kernel, cfg),
+        out_shape=jax.ShapeDtypeStruct((rows * shards, chans), jnp.bfloat16),
+        grid_spec=pltpu.PrefetchScalarGridSpec(
+            num_scalar_prefetch=1,
+            grid=(shards,),
+            in_specs=[hbm] * (len(flat) + 2 * shards + 1) + [whole(a) for a in small],
+            out_specs=pl.BlockSpec((rows, chans), lambda i, w: (i, 0)),
+            scratch_shapes=[
+                pltpu.VMEM((dim, total), jnp.bfloat16),
+                pltpu.VMEM((2, rows, dim), jnp.bfloat16),
+                pltpu.VMEM((rows, total), jnp.float32),
+                pltpu.VMEM((8 + rows, chans + 2 * state_size), jnp.float32),
+                pltpu.VMEM((state_size, chans), jnp.float32),
+                pltpu.SemaphoreType.DMA((3, max(shards, blocks))),
+                pltpu.SemaphoreType.DMA((2, blocks)),
+            ],
+        ),
+        compiler_params=pltpu.CompilerParams(vmem_limit_bytes=VMEM_LIMIT, dimension_semantics=("arbitrary",)),
+        cost_estimate=pl.CostEstimate(
+            flops=2 * rows * shards * dim * total, bytes_accessed=2 * rows * shards * dim, transcendentals=0
+        ),
+    )(where, *flat, *mains, *maps, dt_w, *small)
+
+
+def out_kernel(cfg, where_ref, *refs):
+    shards, chans, groups, order = cfg
+    gated = refs[:shards]
+    gain, w_ref, out_ref, flat = refs[shards:]
+    me_s = where_ref[0]
+    per = shards // groups
+
+    @pl.when(pl.program_id(0) == 0)
+    def _():
+        for g in range(groups):
+            squares = 0.0
+            parts = []
+            for d in range(g * per, (g + 1) * per):
+                part = gated[d][...].astype(jnp.float32)
+                parts.append(part)
+                squares = squares + jnp.sum(part * part, axis=1, keepdims=True)
+            factor = lax.rsqrt(squares * (1.0 / (per * chans)) + EPS)
+            for d, part in zip(range(g * per, (g + 1) * per), parts):
+                t = me_s ^ d
+                value = (part * factor * gain[pl.ds(t, 1), :]).astype(jnp.bfloat16)
+                flat[:, pl.ds(pl.multiple_of(t * chans, chans), chans)] = value
+
+    out_ref[...] = jnp.dot(flat[...], w_ref[...], preferred_element_type=jnp.float32).astype(jnp.bfloat16)
+
+
+def out_terms(where, gated, gain, w_flat, groups, blocks, order):
+    shards = len(gated)
+    rows, chans = gated[0].shape
+    depth, dim = w_flat.shape
+    feats = dim // blocks
+    tile = min(512, feats)
+    tiles = feats // tile
+
+    def column(i, w):
+        e = order[-1]
+        for n in range(len(order) - 2, -1, -1):
+            e = jnp.where(i // tiles == n, order[n], e)
+        return (0, (w[1] ^ e) * tiles + lax.rem(i, tiles))
+
+    return pl.pallas_call(
+        partial(out_kernel, (shards, chans, groups, order)),
+        out_shape=jax.ShapeDtypeStruct((rows, feats * len(order)), jnp.bfloat16),
+        grid_spec=pltpu.PrefetchScalarGridSpec(
+            num_scalar_prefetch=1,
+            grid=(tiles * len(order),),
+            in_specs=[pl.BlockSpec((rows, chans), lambda i, w: (0, 0))] * shards
+            + [pl.BlockSpec(gain.shape, lambda i, w: (0, 0)), pl.BlockSpec((depth, tile), column)],
+            out_specs=pl.BlockSpec((rows, tile), lambda i, w: (0, i)),
+            scratch_shapes=[pltpu.VMEM((rows, depth), jnp.bfloat16)],
+        ),
+        compiler_params=pltpu.CompilerParams(vmem_limit_bytes=VMEM_LIMIT, dimension_semantics=("arbitrary",)),
+        cost_estimate=pl.CostEstimate(
+            flops=2 * rows * depth * feats * len(order),
+            bytes_accessed=2 * depth * feats * len(order),
+            transcendentals=0,
+        ),
+    )(where, *gated, gain, w_flat)
+
+
+def gather_tokens(tokens):
+    outer = lax.axis_size("seq") // 2
+    half = outer // 2
+    at = lax.axis_index("seq") // 2
+
+    def line(value, pairs):
+        return lax.ppermute(value, "seq", [(2 * a + y, 2 * b + y) for a, b in pairs for y in (0, 1)])
+
+    near = swap(tokens, "seq", 2)
+    crossing = [line(v, [(1, 2), (2, 1)]) for v in (tokens, near)]
+    outward = [line(v, [(1, 0), (2, 3)]) for v in crossing]
+    middle = (at == 1) | (at == 2)
+    far = [jnp.where(middle, a, b) for a, b in zip(crossing, outward)]
+    rows = [tokens, near, *far]
+    both = []
+    for value in rows:
+        both += [value, swap(value, "seq", 1)]
+    pairs = [(v, swap(v, "head", 2)) for v in both]
+    pieces = [(a, swap(a, "head", 1), b, swap(b, "head", 1)) for a, b in pairs]
+    return pieces, far
+
+
+def piece_table(shards):
+    me = lax.axis_index("seq")
+    shard = jnp.arange(shards)
+    outer = (shard // 2) ^ (me // 2)
+    middle = (me // 2 == 1) | (me // 2 == 2)
+    slot = jnp.where((outer >= 2) & middle, outer ^ 1, outer)
+    return slot * 2 + ((shard ^ me) & 1)
+
+
+def head_split_body(
+    tokens, norm_gain, w_in, w_dt, dt_bias, a_log, d_skip, conv_w, conv_b, gate_gain, w_out
+):
+    shards, blocks = lax.axis_size("seq"), lax.axis_size("head")
+    s, h = lax.axis_index("seq"), lax.axis_index("head")
+    rows = tokens.shape[0]
+    krows, groups, wide = w_in.shape
+    group_width = gate_gain.shape[1]
+    state_size = (conv_b.shape[1] - group_width) // 2
+    local_heads = dt_bias.shape[0]
+    heads = local_heads // shards
+    width = groups * group_width // local_heads
+    chans = heads * width
+    per = shards // groups
+    dim = krows * shards
+
+    pieces, far = gather_tokens(tokens)
+
+    gain = lax.dynamic_slice_in_dim(norm_gain, s * krows, krows, 0)
+
+    def columns(t, first, count):
+        part = lax.dynamic_slice(w_in, (0, t // per, first), (krows, 1, count))[:, 0]
+        return (part.astype(jnp.float32) * gain[:, None]).astype(jnp.bfloat16)
+
+    to_send = []
+    for d in range(shards):
+        t = s ^ d
+        first = (t % per) * chans
+        to_send.append(
+            jnp.concatenate([columns(t, first, chans), columns(t, group_width + first, chans)], axis=1)
+        )
+    far_map = columns(s ^ per, 2 * group_width, 2 * state_size)
+    own_map = columns(s, 2 * group_width, 2 * state_size)
+    dt_w = lax.all_gather(
+        (w_dt.astype(jnp.float32) * gain[:, None]).astype(jnp.bfloat16), "seq", axis=0, tiled=True
+    )
+    dt_w = lax.dynamic_slice_in_dim(dt_w, s * heads, heads, 1)
+    dt_w = jnp.pad(dt_w, ((0, 0), (0, LANES - heads)))
+    to_send, far_map = after((to_send, far_map), *far)
+    maps = [own_map] + [None] * (shards - 1)
+    maps[per] = swap(far_map, "seq", per)
+    bit = per // 2
+    while bit:
+        for d in [d for d in range(shards) if maps[d] is not None]:
+            if not d & bit and maps[d | bit] is None:
+                maps[d | bit] = swap(maps[d], "seq", bit)
+        bit //= 2
+    mains = [to_send[0]] + [None] * (shards - 1)
+    for d in range(shards - 1, 0, -1):
+        mains[d] = swap(to_send[d], "seq", d)
+
+    group = s // per
+    quarter = (s % per) * chans
+
+    def own_channels(a):
+        a = lax.dynamic_index_in_dim(a, group, a.ndim - 2, keepdims=False)
+        inputs = lax.dynamic_slice_in_dim(a, quarter, chans, a.ndim - 1)
+        return jnp.concatenate([inputs, a[..., group_width:]], axis=-1)
+
+    def own_heads(a):
+        return lax.dynamic_slice_in_dim(a, s * heads, heads, 0)
+
+    def lanes(a):
+        return jnp.pad(a, (0, LANES - heads))[None, :]
+
+    where = jnp.concatenate([jnp.stack([s, h]), piece_table(shards)]).astype(jnp.int32)
+    gated = mixer(
+        where,
+        pieces,
+        mains,
+        maps,
+        dt_w,
+        own_channels(conv_w),
+        own_channels(conv_b)[None, :],
+        lanes(own_heads(dt_bias)),
+        lanes(-jnp.exp(own_heads(a_log))),
+        jnp.repeat(own_heads(d_skip), width)[None, :],
+        rows,
+        heads,
+        width,
+        dim,
+    )
+    blocks_out = [
+        lax.dynamic_slice_in_dim(gated, (s ^ d) * rows, rows, 0) for d in range(shards)
+    ]
+    arrived = [blocks_out[0]] + [None] * (shards - 1)
+    for d in range(shards - 1, 0, -1):
+        arrived[d] = swap(blocks_out[d], "seq", d)
+
+    gains = gate_gain.reshape(shards, chans)
+    w_flat = w_out.reshape(groups * group_width, w_out.shape[2])
+    feats = w_flat.shape[1] // blocks
+    lead = out_terms(where, arrived, gains, w_flat, groups, blocks, (3, 1))
+    other = swap(lead, "head", 1)
+    own = out_terms(where, arrived, gains, w_flat, groups, blocks, (2, 0))
+    wide_sum = own.astype(jnp.float32) + other.astype(jnp.float32)
+    beyond = swap(wide_sum[:, :feats].astype(jnp.bfloat16), "head", 2)
+    return (wide_sum[:, feats:] + beyond.astype(jnp.float32)).astype(jnp.bfloat16)
+
+
+def fits_head_split(mesh, w_in, gate_gain, dt_bias):
+    shards, blocks = mesh.shape["seq"], mesh.shape["head"]
+    groups = gate_gain.shape[0] // blocks
+    local_heads = dt_bias.shape[0] // blocks
+    chans = groups * gate_gain.shape[1] // shards
+    return shards == 8 and blocks == 4 and groups == 2 and local_heads % shards == 0 and chans % LANES == 0
 
 
 def from_behind(shard, axis, by):
@@ -90,7 +506,7 @@
     return (earlier[0] + later[0], jnp.exp(later[0])[:, :, None, None] * earlier[1] + later[1])
 
 
-def body(tokens, norm_gain, w_in, w_dt, dt_bias, a_log, d_skip, conv_w, conv_b, gate_gain, w_out):
+def sequence_split_body(tokens, norm_gain, w_in, w_dt, dt_bias, a_log, d_skip, conv_w, conv_b, gate_gain, w_out):
     local_rows = tokens.shape[0]
     kernel_len = conv_w.shape[0]
     groups, group_width = gate_gain.shape
@@ -169,4 +585,13 @@
         P("head", None, None),
     )
     out_specs = P("seq", "head")
-    return jax.shard_map(body, mesh=mesh, in_specs=in_specs, out_specs=out_specs, check_vma=False)
+
+    def mixer_prefill(*args):
+        by_heads = fits_head_split(mesh, args[2], args[9], args[4])
+        body = head_split_body if by_heads else sequence_split_body
+        mapped = jax.shard_map(
+            body, mesh=mesh, in_specs=in_specs, out_specs=out_specs, check_vma=False
+        )
+        return mapped(*args)
+
+    return mixer_prefill

time: 1010 us -> 452 us (0.45)
  waiting for transfers between devices: 802 us -> 224 us
  Pallas kernels: 0 us -> 73.2 us
  matrix products: 68.7 us -> 0 us
  starting transfers between devices: 2.81 us -> 60.4 us
  other arithmetic: 27.2 us -> 13 us
  local copies, waits for them, and re-layouts: 44 us -> 31.5 us
  between operations: 13.4 us -> 0.97 us
    all_gather x3 -> x0, waiting for transfers between devices: 761 us -> none  [the longest x1 711 us: body(): lax.all_gather(flat_in, 'seq', axis=0, tiled=True)]
    ppermute x1 -> x56, waiting for transfers between devices: 2.91 us -> 224 us  [the longest x52 211 us: swap(): return lax.ppermute(value, axis, [(i, i ^ bit) for i in range(count)])]
    pallas_call x0 -> x3, Pallas kernels: none -> 73.2 us  [the longest x1 54.7 us: mixer(): pl.pallas_call(partial(mixer_kernel, cfg), out_shape=jax.ShapeDtypeStruct...]
    dot_general x16 -> x0, matrix products: 68.7 us -> none  [the longest x1 21.8 us: body(): jnp.dot(normed, lax.all_gather(flat_in, 'seq', axis=0, tiled=True), prefe...]
    ppermute x1 -> x56, starting transfers between devices: 2.69 us -> 60.4 us  [the longest x52 50.4 us: swap(): return lax.ppermute(value, axis, [(i, i ^ bit) for i in range(count)])]
    reduce_scatter x1 -> x0, waiting for transfers between devices: 37 us -> none  [body(): lax.psum_scatter(terms.astype(jnp.bfloat16), 'head', scatter_dimension=1,...]
    reshape x7 -> x1, local copies, waits for them, and re-layouts: 18.3 us -> 0.6 us  [head_split_body(): gains = gate_gain.reshape(shards, chans)]
    dynamic_slice x12 -> x10, local copies, waits for them, and re-layouts: 11.1 us -> 22 us  [the longest x2 17.6 us: columns(): lax.dynamic_slice(w_in, (0, t // per, first), (krows, 1, count))[:, 0]]
  transfers between devices with their start and end apart: 5 -> 56, of which waited for: 4 -> 24; matrix products, arithmetic and copies ran while one was open for 2% -> 7% of each run, Pallas kernels for 0% -> 2%
where the time goes in v1:
time: 452 us; the launch traced here: 451 us
  waiting for transfers between devices  224 us (50%)
  Pallas kernels  73.2 us (16%)
  starting transfers between devices  60.4 us (13%)
  blocking collectives  48.6 us (11%)
  local copies, waits for them, and re-layouts  31.5 us (7%)
  other arithmetic  13 us (3%)
    ppermute x52, waiting for transfers between devices, swap(): return lax.ppermute(value, axis, [(i, i ^ bit) for i in range(count)])  211 us
    pallas_call x1, Pallas kernels, mixer(): pl.pallas_call(partial(mixer_kernel, cfg), out_shape=jax.ShapeDtypeStruct...  54.7 us
    ppermute x52, starting transfers between devices, swap(): return lax.ppermute(value, axis, [(i, i ^ bit) for i in range(count)])  50.4 us
    all_gather x1, blocking collectives, head_split_body(): lax.all_gather((w_dt.astype(jnp.float32) * gain[:, None]).astype(jnp.bflo...  48.6 us
    pallas_call x2, Pallas kernels, out_terms(): pl.pallas_call(partial(out_kernel, (shards, chans, groups, order)), out_s...  18.5 us
    dynamic_slice x2, local copies, waits for them, and re-layouts, columns(): lax.dynamic_slice(w_in, (0, t // per, first), (krows, 1, count))[:, 0]  17.6 us
    ppermute x4, waiting for transfers between devices, line(): lax.ppermute(value, 'seq', [(2 * a + y, 2 * b + y) for a, b in pairs for...  13 us
    ppermute x4, starting transfers between devices, line(): lax.ppermute(value, 'seq', [(2 * a + y, 2 * b + y) for a, b in pairs for...  10 us
  transfers between devices with their start and end apart: 56, of which 24 were waited for; matrix products, arithmetic and copies ran while one was open for 7% of the time, Pallas kernels for 2%

profile of v1, /device:TPU:8, one launch (start us, length us, event | category | flops | bytes accessed | tf_op | source)
XLA Modules:
  0.0 451.3 jit_solution(13372674855294768301)
XLA Ops:
  1.2 6.4 %constant_dynamic-slice_fusion.24 = (bf16[512,1,256]{2,1,0:T(2,128)(2,1)S(1)}, bf16[512,1,256]{2,1,0:T(2,128)(2,1)S(1)}, bf16[512,1,256]{2,1,0:T(2,128)(2,1)S(1)...) fusion(bf16[512,2,2304]{2,1,0:T(2,128)(2,1)} %param.13, s32[]{:T(128)S(6)} %select_n.244, s32[]{:T(128)S(6)} %select_n.246, ...), kind=kLoop, calls=%fused_computation.95 | loop fusion | bytes 2621472 | tf_op jit(solution)/shard_map/dynamic_slice | solution.py:344
  7.6 11.2 %constant_dynamic-slice_fusion.11 = (bf16[512,1,256]{2,1,0:T(2,128)(2,1)S(1)}, bf16[512,1,256]{2,1,0:T(2,128)(2,1)S(1)}, bf16[512,1,256]{2,1,0:T(2,128)(2,1)S(1)...) fusion(bf16[512,2,2304]{2,1,0:T(2,128)(2,1)S(1)} %copy-done.2, ...), kind=kLoop, calls=%fused_computation.82 | loop fusion | bytes 6815816 | tf_op jit(solution)/shard_map/dynamic_slice | solution.py:344
  18.8 2.4 fusion.1
  24.3 3.5 collective-permute-start.15
  31.1 2.5 collective-permute-start.42
  33.6 19.3 %collective-permute-done.42.refs_43_ = bf16[512,256]{1,0:T(8,128)(2,1)} collective-permute-done((bf16[512,256]{1,0:T(8,128)(2,1)S(1)}, bf16[512,256]{1,0:T(8,128)(2,1)}, u32[]{:S(2)}, u32[]{:S(2)}) %collective-permute-start.42) | collective-permute-done | bytes 262176 | tf_op jit(solution)/shard_map/ppermute | solution.py:21
  52.9 3.7 collective-permute-start.24
  62.1 13.0 %collective-permute-done.24 = bf16[384,1024]{1,0:T(8,128)(2,1)} collective-permute-done((bf16[384,1024]{1,0:T(8,128)(2,1)}, bf16[384,1024]{1,0:T(8,128)(2,1)}, u32[]{:S(2)}, u32[]{:S(2)}) %collective-permute-start.24) | collective-permute-done | bytes 786464 | tf_op jit(solution)/shard_map/ppermute | solution.py:298
  79.1 2.3 collective-permute-done.9.refs_10_
  85.0 12.2 %collective-permute-done.5.refs_6_ = bf16[384,1024]{1,0:T(8,128)(2,1)} collective-permute-done((bf16[384,1024]{1,0:T(8,128)(2,1)}, bf16[384,1024]{1,0:T(8,128)(2,1)}, u32[]{:S(2)}, u32[]{:S(2)}) %collective-permute-start.5) | collective-permute-done | bytes 786464 | tf_op jit(solution)/shard_map/ppermute | solution.py:21
  104.6 13.2 %collective-permute-done.18.refs_18_ = bf16[384,1024]{1,0:T(8,128)(2,1)} collective-permute-done((bf16[384,1024]{1,0:T(8,128)(2,1)S(1)}, bf16[384,1024]{1,0:T(8,128)(2,1)}, u32[]{:S(2)}, u32[]{:S(2)}) %collective-permute-start.18) | collective-permute-done | bytes 786464 | tf_op jit(solution)/shard_map/ppermute | solution.py:21
  119.2 12.1 %collective-permute-done.43.refs_44_ = bf16[512,256]{1,0:T(8,128)(2,1)S(1)} collective-permute-done((bf16[512,256]{1,0:T(8,128)(2,1)S(1)}, bf16[512,256]{1,0:T(8,128)(2,1)S(1)}, u32[]{:S(2)}, u32[]{:S(2)}) %collective-permute-start.43) | collective-permute-done | bytes 262176 | tf_op jit(solution)/shard_map/ppermute | solution.py:21
  131.3 3.5 collective-permute-start.45
  138.8 3.1 collective-permute-done.45.refs_46_
  143.9 21.3 %collective-permute-done.44.refs_45_ = bf16[512,256]{1,0:T(8,128)(2,1)S(1)} collective-permute-done((bf16[512,256]{1,0:T(8,128)(2,1)S(1)}, bf16[512,256]{1,0:T(8,128)(2,1)S(1)}, u32[]{:S(2)}, u32[]{:S(2)}) %collective-permute-start.44) | collective-permute-done | bytes 262176 | tf_op jit(solution)/shard_map/ppermute | solution.py:21
  166.9 7.3 %collective-permute-done.35.refs_35_ = bf16[512,512]{1,0:T(8,128)(2,1)S(1)} collective-permute-done((bf16[512,512]{1,0:T(8,128)(2,1)S(1)}, bf16[512,512]{1,0:T(8,128)(2,1)S(1)}, u32[]{:S(2)}, u32[]{:S(2)}) %collective-permute-start.35) | collective-permute-done | bytes 524320 | tf_op jit(solution)/shard_map/ppermute | solution.py:21
  176.5 6.3 %collective-permute-start.39 = (bf16[512,512]{1,0:T(8,128)(2,1)}, bf16[512,512]{1,0:T(8,128)(2,1)}, u32[]{:S(2)}, u32[]{:S(2)}) collective-permute-start(bf16[512,512]{1,0:T(8,128)(2,1)} %get-tuple-element.21), channel_id=1, source_target_pairs={{0,28},{4,24},{8,20},{12,16},{16,12},{20,8},{24,4},{28,0},{1,29},{... | collective-permute-start | bytes 1572872 | tf_op jit(solution)/shard_map/ppermute | solution.py:21
  182.9 36.1 %collective-permute-done.37.refs_37_ = bf16[512,512]{1,0:T(8,128)(2,1)} collective-permute-done((bf16[512,512]{1,0:T(8,128)(2,1)}, bf16[512,512]{1,0:T(8,128)(2,1)}, u32[]{:S(2)}, u32[]{:S(2)}) %collective-permute-start.37) | collective-permute-done | bytes 524320 | tf_op jit(solution)/shard_map/ppermute | solution.py:21
  219.5 48.6 %all_gather.3 = bf16[4096,32]{1,0:T(8,128)(2,1)S(1)} all-gather(bf16[512,32]{1,0:T(8,128)(2,1)S(1)} %multiply_convert_fusion), channel_id=1, replica_groups=mesh['seq'=8,'head'=4] {'seq'}, dimensions={0}, use_global_device_ids=true | all-gather | bytes 294912 | tf_op jit(solution)/shard_map/all_gather | solution.py:356
  271.2 17.4 %collective-permute-done.22.refs_22_ = bf16[384,1024]{1,0:T(8,128)(2,1)} collective-permute-done((bf16[384,1024]{1,0:T(8,128)(2,1)S(1)}, bf16[384,1024]{1,0:T(8,128)(2,1)}, u32[]{:S(2)}, u32[]{:S(2)}) %collective-permute-start.22) | collective-permute-done | bytes 786464 | tf_op jit(solution)/shard_map/ppermute | solution.py:21
  290.4 14.6 %collective-permute-done.31.refs_30_ = bf16[384,1024]{1,0:T(8,128)(2,1)} collective-permute-done((bf16[384,1024]{1,0:T(8,128)(2,1)}, bf16[384,1024]{1,0:T(8,128)(2,1)}, u32[]{:S(2)}, u32[]{:S(2)}) %collective-permute-start.31) | collective-permute-done | bytes 786464 | tf_op jit(solution)/shard_map/ppermute | solution.py:21
  311.5 54.7 %shard_map.109 = bf16[3072,256]{1,0:T(8,128)(2,1)} custom-call(s32[10]{0:T(128)} %pad_add_fusion.where_ref, bf16[384,1024]{1,0:T(8,128)(2,1)} %refs_0_.1, bf16[384,1024]{1,0:T(8,128)(2,1)} %copy-done.23, bf16[384,1024]{1,0:T(8,128)(2,1)} %copy-done.22, bf16[384,1024]{1,0:T(8,128)(2,1)} %copy-done.24, bf16[384,1024]{1,0:T(8,128)(2,1)} %collective-permute-done.3.refs_4_, ...), custom_call_target="tpu_custom_call" | custom-call | flops 22548578304 | bytes 25165824 | tf_op jit(solution)/shard_map/pallas_call | solution.py:208
  366.2 2.3 constant_dynamic-slice_fusion
  377.3 3.6 collective-permute-done.48.refs_2_
  380.9 3.6 collective-permute-start.53
  385.6 14.2 %collective-permute-done.51.refs_5_ = bf16[384,256]{1,0:T(8,128)(2,1)S(1)} collective-permute-done((bf16[384,256]{1,0:T(8,128)(2,1)S(1)}, bf16[384,256]{1,0:T(8,128)(2,1)S(1)}, u32[]{:S(2)}, u32[]{:S(2)}) %collective-permute-start.51) | collective-permute-done | bytes 196640 | tf_op jit(solution)/shard_map/ppermute | solution.py:21
  399.9 6.3 %collective-permute-done.52.refs_6_ = bf16[384,256]{1,0:T(8,128)(2,1)S(1)} collective-permute-done((bf16[384,256]{1,0:T(8,128)(2,1)S(1)}, bf16[384,256]{1,0:T(8,128)(2,1)S(1)}, u32[]{:S(2)}, u32[]{:S(2)}) %collective-permute-start.52) | collective-permute-done | bytes 196640 | tf_op jit(solution)/shard_map/ppermute | solution.py:21
  406.1 2.6 collective-permute-done.53.refs_7_
  409.4 9.3 %shard_map.111 = bf16[384,2048]{1,0:T(8,128)(2,1)} custom-call(s32[10]{0:T(128)} %pad_add_fusion.where_ref, bf16[384,256]{1,0:T(8,128)(2,1)} %get-tuple-element.48.refs_0_, bf16[384,256]{1,0:T(8,128)(2,1)} %copy-done.6, bf16[384,256]{1,0:T(8,128)(2,1)} %copy-done.7, bf16[384,256]{1,0:T(8,128)(2,1)} %copy-done.8, bf16[384,256]{1,0:T(8,128)(2,1)} %copy-done.9, ...), custom_call_target="tpu_custom_call" | custom-call | flops 3221225472 | bytes 8388608 | tf_op jit(solution)/shard_map/pallas_call | solution.py:272
  418.7 9.3 %shard_map.110 = bf16[384,2048]{1,0:T(8,128)(2,1)} custom-call(s32[10]{0:T(128)} %pad_add_fusion.where_ref, bf16[384,256]{1,0:T(8,128)(2,1)} %get-tuple-element.48.refs_0_, bf16[384,256]{1,0:T(8,128)(2,1)} %copy-done.6, bf16[384,256]{1,0:T(8,128)(2,1)} %copy-done.7, bf16[384,256]{1,0:T(8,128)(2,1)} %copy-done.8, bf16[384,256]{1,0:T(8,128)(2,1)} %copy-done.9, ...), custom_call_target="tpu_custom_call" | custom-call | flops 3221225472 | bytes 8388608 | tf_op jit(solution)/shard_map/pallas_call | solution.py:272
  428.0 2.0 convert_add_fusion
  431.7 18.5 %collective-permute-done.55 = bf16[384,1024]{1,0:T(8,128)(2,1)S(1)} collective-permute-done((bf16[384,1024]{1,0:T(8,128)(2,1)S(1)}, bf16[384,1024]{1,0:T(8,128)(2,1)S(1)}, u32[]{:S(2)}, u32[]{:S(2)}) %collective-permute-start.55) | collective-permute-done | bytes 786464 | tf_op jit(solution)/shard_map/ppermute | solution.py:21
  (221 shorter events, 64.2 us)
Async XLA Ops:
  0.0 52.9 %collective-permute-start.7 = (bf16[384,1024]{1,0:T(8,128)(2,1)}, bf16[384,1024]{1,0:T(8,128)(2,1)}, u32[]{:S(2)}, u32[]{:S(2)}) collective-permute-start(bf16[384,1024]{1,0:T(8,128)(2,1)} %refs_0_.1), channel_id=1, source_target_pairs={{0,8},{4,12},{8,0},{12,4},{16,24},{20,28},{24,16},{28,20},{1,9},{5... | collective-permute-start | bytes 2359304 | tf_op jit(solution)/shard_map/ppermute | solution.py:21
  24.3 32.3 %collective-permute-start.15 = (bf16[384,1024]{1,0:T(8,128)(2,1)S(1)}, bf16[384,1024]{1,0:T(8,128)(2,1)S(1)}, u32[]{:S(2)}, u32[]{:S(2)}) collective-permute-start(bf16[384,1024]{1,0:T(8,128)(2,1)S(1)} %copy-done.21), channel_id=1, source_target_pairs={{8,16},{12,20},{16,8},{20,12},{9,17},{13,21},{17,9},{21,13},{10,18... | collective-permute-start | bytes 2359304 | tf_op jit(solution)/shard_map/ppermute | solution.py:298
  27.8 31.2 %collective-permute-start.3 = (bf16[384,1024]{1,0:T(8,128)(2,1)S(1)}, bf16[384,1024]{1,0:T(8,128)(2,1)}, u32[]{:S(2)}, u32[]{:S(2)}) collective-permute-start(bf16[384,1024]{1,0:T(8,128)(2,1)S(1)} %copy-done.21), channel_id=1, source_target_pairs={{0,4},{4,0},{8,12},{12,8},{16,20},{20,16},{24,28},{28,24},{1,5},{5... | collective-permute-start | bytes 2359304 | tf_op jit(solution)/shard_map/ppermute | solution.py:21
  29.2 31.4 %collective-permute-start.1 = (bf16[384,1024]{1,0:T(8,128)(2,1)S(1)}, bf16[384,1024]{1,0:T(8,128)(2,1)S(1)}, u32[]{:S(2)}, u32[]{:S(2)}) collective-permute-start(bf16[384,1024]{1,0:T(8,128)(2,1)S(1)} %copy-done.21), channel_id=1, source_target_pairs={{0,2},{1,3},{2,0},{3,1},{4,6},{5,7},{6,4},{7,5},{8,10},{9,11},{10,... | collective-permute-start | bytes 2359304 | tf_op jit(solution)/shard_map/ppermute | solution.py:21
  31.1 21.8 %collective-permute-start.42 = (bf16[512,256]{1,0:T(8,128)(2,1)S(1)}, bf16[512,256]{1,0:T(8,128)(2,1)}, u32[]{:S(2)}, u32[]{:S(2)}) collective-permute-start(bf16[512,256]{1,0:T(8,128)(2,1)S(1)} %collective-permute-done.41.refs_42_), channel_id=1, source_target_pairs={{0,4},{4,0},{8,12},{12,8},{16,20},{20,16},{24,28},{28,24},{1,5},{5... | collective-permute-start | bytes 786440 | tf_op jit(solution)/shard_map/ppermute | solution.py:21
  52.9 22.2 %collective-permute-start.24 = (bf16[384,1024]{1,0:T(8,128)(2,1)}, bf16[384,1024]{1,0:T(8,128)(2,1)}, u32[]{:S(2)}, u32[]{:S(2)}) collective-permute-start(bf16[384,1024]{1,0:T(8,128)(2,1)} %collective-permute-done.7.refs_8_), channel_id=1, source_target_pairs={{8,16},{12,20},{16,8},{20,12},{9,17},{13,21},{17,9},{21,13},{10,18... | collective-permute-start | bytes 2359304 | tf_op jit(solution)/shard_map/ppermute | solution.py:298
  62.1 21.8 %collective-permute-start.8 = (bf16[384,1024]{1,0:T(8,128)(2,1)}, bf16[384,1024]{1,0:T(8,128)(2,1)}, u32[]{:S(2)}, u32[]{:S(2)}) collective-permute-start(bf16[384,1024]{1,0:T(8,128)(2,1)} %collective-permute-done.7.refs_8_), channel_id=1, source_target_pairs={{0,1},{1,0},{2,3},{3,2},{4,5},{5,4},{6,7},{7,6},{8,9},{9,8},{10,11... | collective-permute-start | bytes 2359304 | tf_op jit(solution)/shard_map/ppermute | solution.py:21
  75.1 22.1 %collective-permute-start.5 = (bf16[384,1024]{1,0:T(8,128)(2,1)}, bf16[384,1024]{1,0:T(8,128)(2,1)}, u32[]{:S(2)}, u32[]{:S(2)}) collective-permute-start(bf16[384,1024]{1,0:T(8,128)(2,1)} %collective-permute-done.3.refs_4_), channel_id=1, source_target_pairs={{0,2},{1,3},{2,0},{3,1},{4,6},{5,7},{6,4},{7,5},{8,10},{9,11},{10,... | collective-permute-start | bytes 2359304 | tf_op jit(solution)/shard_map/ppermute | solution.py:21
  77.5 21.1 %collective-permute-start.4 = (bf16[384,1024]{1,0:T(8,128)(2,1)}, bf16[384,1024]{1,0:T(8,128)(2,1)}, u32[]{:S(2)}, u32[]{:S(2)}) collective-permute-start(bf16[384,1024]{1,0:T(8,128)(2,1)} %collective-permute-done.3.refs_4_), channel_id=1, source_target_pairs={{0,1},{1,0},{2,3},{3,2},{4,5},{5,4},{6,7},{7,6},{8,9},{9,8},{10,11... | collective-permute-start | bytes 2359304 | tf_op jit(solution)/shard_map/ppermute | solution.py:21
  79.1 21.6 %collective-permute-start.2 = (bf16[384,1024]{1,0:T(8,128)(2,1)}, bf16[384,1024]{1,0:T(8,128)(2,1)S(1)}, u32[]{:S(2)}, u32[]{:S(2)}) collective-permute-start(bf16[384,1024]{1,0:T(8,128)(2,1)} %copy-done.22), channel_id=1, source_target_pairs={{0,1},{1,0},{2,3},{3,2},{4,5},{5,4},{6,7},{7,6},{8,9},{9,8},{10,11... | collective-permute-start | bytes 2359304 | tf_op jit(solution)/shard_map/ppermute | solution.py:21
  100.7 34.1 %collective-permute-start.13 = (bf16[384,1024]{1,0:T(8,128)(2,1)}, bf16[384,1024]{1,0:T(8,128)(2,1)S(1)}, u32[]{:S(2)}, u32[]{:S(2)}) collective-permute-start(bf16[384,1024]{1,0:T(8,128)(2,1)} %collective-permute-done.11.refs_12_), channel_id=1, source_target_pairs={{0,2},{1,3},{2,0},{3,1},{4,6},{5,7},{6,4},{7,5},{8,10},{9,11},{10,... | collective-permute-start | bytes 2359304 | tf_op jit(solution)/shard_map/ppermute | solution.py:21
  101.3 34.0 %collective-permute-start.12 = (bf16[384,1024]{1,0:T(8,128)(2,1)}, bf16[384,1024]{1,0:T(8,128)(2,1)S(1)}, u32[]{:S(2)}, u32[]{:S(2)}) collective-permute-start(bf16[384,1024]{1,0:T(8,128)(2,1)} %collective-permute-done.11.refs_12_), channel_id=1, source_target_pairs={{0,1},{1,0},{2,3},{3,2},{4,5},{5,4},{6,7},{7,6},{8,9},{9,8},{10,11... | collective-permute-start | bytes 2359304 | tf_op jit(solution)/shard_map/ppermute | solution.py:21
  102.8 32.5 %collective-permute-start.10 = (bf16[384,1024]{1,0:T(8,128)(2,1)}, bf16[384,1024]{1,0:T(8,128)(2,1)S(1)}, u32[]{:S(2)}, u32[]{:S(2)}) collective-permute-start(bf16[384,1024]{1,0:T(8,128)(2,1)} %collective-permute-done.9.refs_10_), channel_id=1, source_target_pairs={{0,1},{1,0},{2,3},{3,2},{4,5},{5,4},{6,7},{7,6},{8,9},{9,8},{10,11... | collective-permute-start | bytes 2359304 | tf_op jit(solution)/shard_map/ppermute | solution.py:21
  134.8 30.3 %collective-permute-start.33 = (bf16[512,512]{1,0:T(8,128)(2,1)S(1)}, bf16[512,512]{1,0:T(8,128)(2,1)S(1)}, u32[]{:S(2)}, u32[]{:S(2)}) collective-permute-start(bf16[512,512]{1,0:T(8,128)(2,1)S(1)} %get-tuple-element.15), channel_id=1, source_target_pairs={{0,4},{4,0},{8,12},{12,8},{16,20},{20,16},{24,28},{28,24},{1,5},{5... | collective-permute-start | bytes 1572872 | tf_op jit(solution)/shard_map/ppermute | solution.py:21
  135.3 30.2 %collective-permute-start.34 = (bf16[512,512]{1,0:T(8,128)(2,1)S(1)}, bf16[512,512]{1,0:T(8,128)(2,1)S(1)}, u32[]{:S(2)}, u32[]{:S(2)}) collective-permute-start(bf16[512,512]{1,0:T(8,128)(2,1)S(1)} %get-tuple-element.16), channel_id=1, source_target_pairs={{0,8},{4,12},{8,0},{12,4},{16,24},{20,28},{24,16},{28,20},{1,9},{5... | collective-permute-start | bytes 1572872 | tf_op jit(solution)/shard_map/ppermute | solution.py:21
  135.4 29.7 %collective-permute-start.44 = (bf16[512,256]{1,0:T(8,128)(2,1)S(1)}, bf16[512,256]{1,0:T(8,128)(2,1)S(1)}, u32[]{:S(2)}, u32[]{:S(2)}) collective-permute-start(bf16[512,256]{1,0:T(8,128)(2,1)S(1)} %collective-permute-done.43.refs_44_), channel_id=1, source_target_pairs={{0,4},{4,0},{8,12},{12,8},{16,20},{20,16},{24,28},{28,24},{1,5},{5... | collective-permute-start | bytes 786440 | tf_op jit(solution)/shard_map/ppermute | solution.py:21
  136.9 37.4 %collective-permute-start.35 = (bf16[512,512]{1,0:T(8,128)(2,1)S(1)}, bf16[512,512]{1,0:T(8,128)(2,1)S(1)}, u32[]{:S(2)}, u32[]{:S(2)}) collective-permute-start(bf16[512,512]{1,0:T(8,128)(2,1)S(1)} %get-tuple-element.17), channel_id=1, source_target_pairs={{0,12},{4,8},{8,4},{12,0},{16,28},{20,24},{24,20},{28,16},{1,13},{... | collective-permute-start | bytes 1572872 | tf_op jit(solution)/shard_map/ppermute | solution.py:21
  141.9 33.7 %collective-permute-start.36 = (bf16[512,512]{1,0:T(8,128)(2,1)S(1)}, bf16[512,512]{1,0:T(8,128)(2,1)S(1)}, u32[]{:S(2)}, u32[]{:S(2)}) collective-permute-start(bf16[512,512]{1,0:T(8,128)(2,1)S(1)} %get-tuple-element.18), channel_id=1, source_target_pairs={{0,16},{4,20},{8,24},{12,28},{16,0},{20,4},{24,8},{28,12},{1,17},{... | collective-permute-start | bytes 1572872 | tf_op jit(solution)/shard_map/ppermute | solution.py:21
  165.1 53.9 %collective-permute-start.37 = (bf16[512,512]{1,0:T(8,128)(2,1)}, bf16[512,512]{1,0:T(8,128)(2,1)}, u32[]{:S(2)}, u32[]{:S(2)}) collective-permute-start(bf16[512,512]{1,0:T(8,128)(2,1)} %get-tuple-element.19), channel_id=1, source_target_pairs={{0,20},{4,16},{8,28},{12,24},{16,4},{20,0},{24,12},{28,8},{1,21},{... | collective-permute-start | bytes 1572872 | tf_op jit(solution)/shard_map/ppermute | solution.py:21
  165.1 104.7 %collective-permute-start.29 = (bf16[384,1024]{1,0:T(8,128)(2,1)S(1)}, bf16[384,1024]{1,0:T(8,128)(2,1)}, u32[]{:S(2)}, u32[]{:S(2)}) collective-permute-start(bf16[384,1024]{1,0:T(8,128)(2,1)S(1)} %broadcast_select_fusion.refs_24_), channel_id=1, source_target_pairs={{0,4},{4,0},{8,12},{12,8},{16,20},{20,16},{24,28},{28,24},{1,5},{5... | collective-permute-start | bytes 2359304 | tf_op jit(solution)/shard_map/ppermute | solution.py:21
  165.4 104.7 %collective-permute-start.27 = (bf16[384,1024]{1,0:T(8,128)(2,1)S(1)}, bf16[384,1024]{1,0:T(8,128)(2,1)}, u32[]{:S(2)}, u32[]{:S(2)}) collective-permute-start(bf16[384,1024]{1,0:T(8,128)(2,1)S(1)} %broadcast_select_fusion.refs_24_), channel_id=1, source_target_pairs={{0,2},{1,3},{2,0},{3,1},{4,6},{5,7},{6,4},{7,5},{8,10},{9,11},{10,... | collective-permute-start | bytes 2359304 | tf_op jit(solution)/shard_map/ppermute | solution.py:21
  174.3 93.8 %collective-permute-start.38 = (bf16[512,512]{1,0:T(8,128)(2,1)}, bf16[512,512]{1,0:T(8,128)(2,1)}, u32[]{:S(2)}, u32[]{:S(2)}) collective-permute-start(bf16[512,512]{1,0:T(8,128)(2,1)} %get-tuple-element.20), channel_id=1, source_target_pairs={{0,24},{4,28},{8,16},{12,20},{16,8},{20,12},{24,0},{28,4},{1,25},{... | collective-permute-start | bytes 1572872 | tf_op jit(solution)/shard_map/ppermute | solution.py:21
  176.5 91.6 %collective-permute-start.39 = (bf16[512,512]{1,0:T(8,128)(2,1)}, bf16[512,512]{1,0:T(8,128)(2,1)}, u32[]{:S(2)}, u32[]{:S(2)}) collective-permute-start(bf16[512,512]{1,0:T(8,128)(2,1)} %get-tuple-element.21), channel_id=1, source_target_pairs={{0,28},{4,24},{8,20},{12,16},{16,12},{20,8},{24,4},{28,0},{1,29},{... | collective-permute-start | bytes 1572872 | tf_op jit(solution)/shard_map/ppermute | solution.py:21
  219.0 50.6 %collective-permute-start.46 = (bf16[512,256]{1,0:T(8,128)(2,1)}, bf16[512,256]{1,0:T(8,128)(2,1)S(1)}, u32[]{:S(2)}, u32[]{:S(2)}) collective-permute-start(bf16[512,256]{1,0:T(8,128)(2,1)} %copy-done.45), channel_id=1, source_target_pairs={{0,4},{4,0},{8,12},{12,8},{16,20},{20,16},{24,28},{28,24},{1,5},{5... | collective-permute-start | bytes 786440 | tf_op jit(solution)/shard_map/ppermute | solution.py:21
  270.2 34.8 %collective-permute-start.31 = (bf16[384,1024]{1,0:T(8,128)(2,1)}, bf16[384,1024]{1,0:T(8,128)(2,1)}, u32[]{:S(2)}, u32[]{:S(2)}) collective-permute-start(bf16[384,1024]{1,0:T(8,128)(2,1)} %collective-permute-done.29.refs_28_), channel_id=1, source_target_pairs={{0,2},{1,3},{2,0},{3,1},{4,6},{5,7},{6,4},{7,5},{8,10},{9,11},{10,... | collective-permute-start | bytes 2359304 | tf_op jit(solution)/shard_map/ppermute | solution.py:21
  288.6 21.8 %collective-permute-start.14 = (bf16[384,1024]{1,0:T(8,128)(2,1)S(1)}, bf16[384,1024]{1,0:T(8,128)(2,1)}, u32[]{:S(2)}, u32[]{:S(2)}) collective-permute-start(bf16[384,1024]{1,0:T(8,128)(2,1)S(1)} %copy-done.29), channel_id=1, source_target_pairs={{0,1},{1,0},{2,3},{3,2},{4,5},{5,4},{6,7},{7,6},{8,9},{9,8},{10,11... | collective-permute-start | bytes 2359304 | tf_op jit(solution)/shard_map/ppermute | solution.py:21
  288.6 21.7 %collective-permute-start.30 = (bf16[384,1024]{1,0:T(8,128)(2,1)}, bf16[384,1024]{1,0:T(8,128)(2,1)S(1)}, u32[]{:S(2)}, u32[]{:S(2)}) collective-permute-start(bf16[384,1024]{1,0:T(8,128)(2,1)} %collective-permute-done.29.refs_28_), channel_id=1, source_target_pairs={{0,1},{1,0},{2,3},{3,2},{4,5},{5,4},{6,7},{7,6},{8,9},{9,8},{10,11... | collective-permute-start | bytes 2359304 | tf_op jit(solution)/shard_map/ppermute | solution.py:21
  289.1 21.2 %collective-permute-start.28 = (bf16[384,1024]{1,0:T(8,128)(2,1)}, bf16[384,1024]{1,0:T(8,128)(2,1)}, u32[]{:S(2)}, u32[]{:S(2)}) collective-permute-start(bf16[384,1024]{1,0:T(8,128)(2,1)} %collective-permute-done.27.refs_26_), channel_id=1, source_target_pairs={{0,1},{1,0},{2,3},{3,2},{4,5},{5,4},{6,7},{7,6},{8,9},{9,8},{10,11... | collective-permute-start | bytes 2359304 | tf_op jit(solution)/shard_map/ppermute | solution.py:21
  289.5 20.9 %collective-permute-start.23 = (bf16[384,1024]{1,0:T(8,128)(2,1)}, bf16[384,1024]{1,0:T(8,128)(2,1)S(1)}, u32[]{:S(2)}, u32[]{:S(2)}) collective-permute-start(bf16[384,1024]{1,0:T(8,128)(2,1)} %collective-permute-done.22.refs_22_), channel_id=1, source_target_pairs={{0,1},{1,0},{2,3},{3,2},{4,5},{5,4},{6,7},{7,6},{8,9},{9,8},{10,11... | collective-permute-start | bytes 2359304 | tf_op jit(solution)/shard_map/ppermute | solution.py:21
  373.5 26.4 %collective-permute-start.51 = (bf16[384,256]{1,0:T(8,128)(2,1)S(1)}, bf16[384,256]{1,0:T(8,128)(2,1)S(1)}, u32[]{:S(2)}, u32[]{:S(2)}) collective-permute-start(bf16[384,256]{1,0:T(8,128)(2,1)S(1)} %get-tuple-element.43), channel_id=1, source_target_pairs={{0,20},{4,16},{8,28},{12,24},{16,4},{20,0},{24,12},{28,8},{1,21},{... | collective-permute-start | bytes 589832 | tf_op jit(solution)/shard_map/ppermute | solution.py:21
  375.8 30.3 %collective-permute-start.52 = (bf16[384,256]{1,0:T(8,128)(2,1)S(1)}, bf16[384,256]{1,0:T(8,128)(2,1)S(1)}, u32[]{:S(2)}, u32[]{:S(2)}) collective-permute-start(bf16[384,256]{1,0:T(8,128)(2,1)S(1)} %get-tuple-element.42), channel_id=1, source_target_pairs={{0,24},{4,28},{8,16},{12,20},{16,8},{20,12},{24,0},{28,4},{1,25},{... | collective-permute-start | bytes 589832 | tf_op jit(solution)/shard_map/ppermute | solution.py:21
  380.9 27.9 %collective-permute-start.53 = (bf16[384,256]{1,0:T(8,128)(2,1)S(1)}, bf16[384,256]{1,0:T(8,128)(2,1)S(1)}, u32[]{:S(2)}, u32[]{:S(2)}) collective-permute-start(bf16[384,256]{1,0:T(8,128)(2,1)S(1)} %get-tuple-element.41), channel_id=1, source_target_pairs={{0,28},{4,24},{8,20},{12,16},{16,12},{20,8},{24,4},{28,0},{1,29},{... | collective-permute-start | bytes 589832 | tf_op jit(solution)/shard_map/ppermute | solution.py:21
  (75 other events, 2168.9 us)

commit v2 on v1

--- a/solution.py
+++ b/solution.py
@@ -13,16 +13,13 @@
 EPS = 1e-05
 HIGHEST = lax.Precision.HIGHEST
 VMEM_LIMIT = 58 * 1024 * 1024
+OUT_VMEM = 58 * 1024 * 1024
 LANES = 128
 
 
 def swap(value, axis, bit):
     count = lax.axis_size(axis)
     return lax.ppermute(value, axis, [(i, i ^ bit) for i in range(count)])
-
-
-def after(values, *gates):
-    return lax.optimization_barrier((values, gates))[0]
 
 
 def silu_of(v):
@@ -43,14 +40,12 @@
     where_ref,
     *refs,
 ):
-    (shards, arrays, blocks, rows, feats, krows, heads, width, state_size, taps, dim) = cfg
-    pieces = [[refs[a * blocks + e] for e in range(blocks)] for a in range(arrays)]
-    at = arrays * blocks
-    mains = refs[at : at + shards]
-    maps = refs[at + shards : at + 2 * shards]
-    (dt_w, conv_w, conv_b, dt_bias, neg_rate, skip, out_ref, wbuf, xbuf, pbuf, cbuf, state, wsem, xsem) = refs[
-        at + 2 * shards :
-    ]
+    (shards, maps_of, blocks, rows, feats, krows, heads, width, state_size, taps, dim) = cfg
+    many = shards - 1
+    gathered, last = refs[:many], refs[many : many + 2]
+    mains = refs[many + 2 : many + 2 + shards]
+    (map_a, map_b, dt_w, conv_w, conv_b, dt_bias, neg_rate, skip) = refs[many + 2 + shards : many + 10 + shards]
+    (out_ref, wbuf, xbuf, pbuf, pnext, cbuf, state, wsem, xsem) = refs[many + 10 + shards :]
     i = pl.program_id(0)
     steps = pl.num_programs(0)
     me_s, me_h = where_ref[0], where_ref[1]
@@ -59,49 +54,51 @@
     main_cols = 2 * chans
     map_cols = 2 * state_size
     per = feats // krows
+    dt_order = range(shards)
+
+    def move(copy, start):
+        if start:
+            copy.start()
+        else:
+            copy.wait()
 
     def fetch(step, slot, start):
         which = where_ref[2 + step]
-        for a in range(arrays):
-            @pl.when(which == a)
-            def _(a=a):
-                for e in range(blocks):
-                    copy = pltpu.make_async_copy(
-                        pieces[a][e], xbuf.at[slot, :, pl.ds(e * feats, feats)], xsem.at[slot, e]
-                    )
-                    if start:
-                        copy.start()
-                    else:
-                        copy.wait()
+        for k in range(shards // 2):
+            for inner in (0, 1):
+                @pl.when(which == 2 * k + inner)
+                def _(k=k, inner=inner):
+                    part = pl.ds(inner * rows, rows)
+                    for e in range(blocks):
+                        beyond, core = divmod(e, 2)
+                        array = k + beyond * (shards // 2)
+                        if array < many:
+                            src, block = gathered[array].at[core, part, :], e
+                        else:
+                            src, block = last[core].at[part, :], (e & ~1) + ((me_h & 1) ^ core)
+                        dst = xbuf.at[slot, :, pl.ds(pl.multiple_of(block * feats, feats), feats)]
+                        move(pltpu.make_async_copy(src, dst, xsem.at[slot, e]), start)
 
     def weights(start):
         for d in range(shards):
             kb = me_s ^ d
-            row = ((kb // per) ^ me_h) * feats + (kb % per) * krows
-            row = pl.multiple_of(row, krows)
+            block = kb // per
+            place = ((block // 2) ^ (me_h // 2)) * 2 + (block % 2)
+            row = pl.multiple_of(place * feats + (kb % per) * krows, krows)
+            source, lo_row = maps_of[d]
+            map_src = (map_a, map_b)[source].at[pl.ds(lo_row, krows), :]
             for n, (src, lo, cols) in enumerate(
-                ((mains[d], 0, main_cols), (maps[d], main_cols, map_cols))
+                (
+                    (mains[d], 0, main_cols),
+                    (map_src, main_cols, map_cols),
+                    (dt_w.at[dt_order[d]], main_cols + map_cols, LANES),
+                )
             ):
-                copy = pltpu.make_async_copy(
-                    src, wbuf.at[pl.ds(row, krows), pl.ds(lo, cols)], wsem.at[n, d]
-                )
-                if start:
-                    copy.start()
-                else:
-                    copy.wait()
-        for e in range(blocks):
-            src_row = pl.multiple_of((me_h ^ e) * feats, feats)
-            copy = pltpu.make_async_copy(
-                dt_w.at[pl.ds(src_row, feats), :],
-                wbuf.at[pl.ds(e * feats, feats), pl.ds(main_cols + map_cols, LANES)],
-                wsem.at[2, e],
-            )
-            if start:
-                copy.start()
-            else:
-                copy.wait()
+                dst = wbuf.at[pl.ds(row, krows), pl.ds(lo, cols)]
+                move(pltpu.make_async_copy(src, dst, wsem.at[n, d]), start)
 
     slot = lax.rem(i, 2)
+    shard_count = steps - 1
 
     @pl.when(i == 0)
     def _():
@@ -110,7 +107,7 @@
         state[...] = jnp.zeros_like(state)
         cbuf[0:8, :] = jnp.zeros((8, conv_cols), jnp.float32)
 
-    @pl.when(i + 1 < steps)
+    @pl.when(i + 1 < shard_count)
     def _():
         fetch(i + 1, 1 - slot, True)
 
@@ -118,30 +115,41 @@
     def _():
         weights(False)
 
-    fetch(i, slot, False)
+    @pl.when(i < shard_count)
+    def _():
+        fetch(i, slot, False)
 
     total = main_cols + map_cols + LANES
-    squares = jnp.zeros((rows, 1), jnp.float32)
-    for e in range(blocks):
-        part = xbuf[slot, :, e * feats : (e + 1) * feats].astype(jnp.float32)
-        squares = squares + jnp.sum(part * part, axis=1, keepdims=True)
-    factor = lax.rsqrt(squares * (1.0 / dim) + EPS)
-    lo = 0
-    while lo < total:
-        cols = min(256, total - lo)
-        pbuf[:, lo : lo + cols] = (
+    tiles = [(lo, min(256, total - lo)) for lo in range(0, total, 256)]
+    length = STRETCH
+    stretches = rows // length
+
+    def row_factor():
+        squares = jnp.zeros((rows, 1), jnp.float32)
+        for e in range(blocks):
+            part = xbuf[slot, :, e * feats : (e + 1) * feats].astype(jnp.float32)
+            squares = squares + jnp.sum(part * part, axis=1, keepdims=True)
+        return lax.rsqrt(squares * (1.0 / dim) + EPS)
+
+    def project(tile, factor):
+        lo, cols = tile
+        pnext[:, lo : lo + cols] = (
             jnp.dot(xbuf[slot], wbuf[:, lo : lo + cols], preferred_element_type=jnp.float32) * factor
         )
-        lo += cols
-    cbuf[8 : 8 + rows, :] = pbuf[:, chans : chans + conv_cols].astype(jnp.bfloat16).astype(jnp.float32)
-
-    length = STRETCH
-    tri = lax.broadcasted_iota(jnp.int32, (length, length), 0) >= lax.broadcasted_iota(
-        jnp.int32, (length, length), 1
-    )
-    ones = jnp.where(tri, 1.0, 0.0).astype(jnp.float32)
-    lane_head = lax.broadcasted_iota(jnp.int32, (length, chans), 1) // width
-    for st in range(rows // length):
+
+    def hand_over():
+        pbuf[...] = pnext[...]
+        cbuf[8 : 8 + rows, :] = pnext[:, chans : chans + conv_cols].astype(jnp.bfloat16).astype(jnp.float32)
+
+    def constants():
+        tri = lax.broadcasted_iota(jnp.int32, (length, length), 0) >= lax.broadcasted_iota(
+            jnp.int32, (length, length), 1
+        )
+        ones = jnp.where(tri, 1.0, 0.0).astype(jnp.float32)
+        lane_head = lax.broadcasted_iota(jnp.int32, (length, chans), 1) // width
+        return tri, ones, lane_head
+
+    def scan(st, tri, ones, lane_head):
         r0 = st * length
         summed = conv_b[...]
         for k in range(taps):
@@ -156,7 +164,7 @@
         step = jnp.maximum(raw, 0.0) + jnp.log1p(jnp.exp(-jnp.abs(raw)))
         logd = neg_rate[...] * step
         cum = jnp.dot(ones, logd, preferred_element_type=jnp.float32, precision=HIGHEST)
-        last = cum[length - 1 : length, :]
+        last_row = cum[length - 1 : length, :]
         cum_t = cum.T
         step_t = step.T
         scores = lax.dot_general(
@@ -176,46 +184,77 @@
         now = state[...]
         across = jnp.dot(out_map, now.astype(jnp.bfloat16), preferred_element_type=jnp.float32)
         y = within + spread(jnp.exp(cum), heads, width) * across + skip[...] * xf
-        to_end = spread(jnp.exp(last - cum) * step, heads, width)
+        to_end = spread(jnp.exp(last_row - cum) * step, heads, width)
         fresh = lax.dot_general(
             in_map,
             (xf * to_end).astype(jnp.bfloat16),
             (((0,), (0,)), ((), ())),
             preferred_element_type=jnp.float32,
         )
-        state[...] = spread(jnp.exp(last), heads, width) * now + fresh
+        state[...] = spread(jnp.exp(last_row), heads, width) * now + fresh
         gate = pbuf[r0 : r0 + length, :chans].astype(jnp.bfloat16).astype(jnp.float32)
         out_ref[r0 : r0 + length, :] = (y * silu_of(gate)).astype(jnp.bfloat16)
-    cbuf[0:8, :] = cbuf[rows : rows + 8, :]
-
-
-def mixer(where, pieces, mains, maps, dt_w, conv_w, conv_b, dt_bias, neg_rate, skip, rows, heads, width, dim):
-    arrays, blocks, shards = len(pieces), len(pieces[0]), len(mains)
-    feats = pieces[0][0].shape[1]
+
+    def keep_tail():
+        cbuf[0:8, :] = cbuf[rows : rows + 8, :]
+
+    @pl.when(i == 0)
+    def _():
+        factor = row_factor()
+        for tile in tiles:
+            project(tile, factor)
+        hand_over()
+
+    @pl.when((i > 0) & (i < shard_count))
+    def _():
+        held = constants()
+        factor = row_factor()
+        for n in range(max(len(tiles), stretches)):
+            if n < len(tiles):
+                project(tiles[n], factor)
+            if n < stretches:
+                scan(n, *held)
+        keep_tail()
+        hand_over()
+
+    @pl.when(i == shard_count)
+    def _():
+        held = constants()
+        for n in range(stretches):
+            scan(n, *held)
+
+
+def mixer(
+    where, gathered, last, mains, maps, maps_of, dt_w, conv_w, conv_b, dt_bias, neg_rate, skip, rows, heads, width, dim
+):
+    shards = len(mains)
+    feats = last[0].shape[1]
+    blocks = dim // feats
     krows = mains[0].shape[0]
     chans = heads * width
     state_size = maps[0].shape[1] // 2
     taps = conv_w.shape[0]
     total = 2 * chans + 2 * state_size + LANES
-    cfg = (shards, arrays, blocks, rows, feats, krows, heads, width, state_size, taps, dim)
+    cfg = (shards, tuple(maps_of), blocks, rows, feats, krows, heads, width, state_size, taps, dim)
     hbm = pl.BlockSpec(memory_space=pl.ANY)
 
     def whole(a):
         return pl.BlockSpec(a.shape, lambda i, w: (0,) * a.ndim)
 
     small = (conv_w, conv_b, dt_bias, neg_rate, skip)
-    flat = [p for row in pieces for p in row]
+    large = (*gathered, *last, *mains, *maps, dt_w)
     return pl.pallas_call(
         partial(mixer_kernel, cfg),
         out_shape=jax.ShapeDtypeStruct((rows * shards, chans), jnp.bfloat16),
         grid_spec=pltpu.PrefetchScalarGridSpec(
             num_scalar_prefetch=1,
-            grid=(shards,),
-            in_specs=[hbm] * (len(flat) + 2 * shards + 1) + [whole(a) for a in small],
-            out_specs=pl.BlockSpec((rows, chans), lambda i, w: (i, 0)),
+            grid=(shards + 1,),
+            in_specs=[hbm] * len(large) + [whole(a) for a in small],
+            out_specs=pl.BlockSpec((rows, chans), lambda i, w: (jnp.maximum(i - 1, 0), 0)),
             scratch_shapes=[
                 pltpu.VMEM((dim, total), jnp.bfloat16),
                 pltpu.VMEM((2, rows, dim), jnp.bfloat16),
+                pltpu.VMEM((rows, total), jnp.float32),
                 pltpu.VMEM((rows, total), jnp.float32),
                 pltpu.VMEM((8 + rows, chans + 2 * state_size), jnp.float32),
                 pltpu.VMEM((state_size, chans), jnp.float32),
@@ -227,11 +266,11 @@
         cost_estimate=pl.CostEstimate(
             flops=2 * rows * shards * dim * total, bytes_accessed=2 * rows * shards * dim, transcendentals=0
         ),
-    )(where, *flat, *mains, *maps, dt_w, *small)
-
-
-def out_kernel(cfg, where_ref, *refs):
-    shards, chans, groups, order = cfg
+    )(where, *large, *small)
+
+
+def normed_terms_kernel(cfg, where_ref, *refs):
+    shards, chans, groups = cfg
     gated = refs[:shards]
     gain, w_ref, out_ref, flat = refs[shards:]
     me_s = where_ref[0]
@@ -255,60 +294,115 @@
     out_ref[...] = jnp.dot(flat[...], w_ref[...], preferred_element_type=jnp.float32).astype(jnp.bfloat16)
 
 
-def out_terms(where, gated, gain, w_flat, groups, blocks, order):
-    shards = len(gated)
-    rows, chans = gated[0].shape
+def terms_kernel(where_ref, flat, w_ref, out_ref):
+    out_ref[...] = jnp.dot(flat[...], w_ref[...], preferred_element_type=jnp.float32).astype(jnp.bfloat16)
+
+
+def out_terms(kernel, where, values, w_flat, rows, blocks, e, keep):
     depth, dim = w_flat.shape
     feats = dim // blocks
-    tile = min(512, feats)
+    tile = min(256, feats)
     tiles = feats // tile
-
-    def column(i, w):
-        e = order[-1]
-        for n in range(len(order) - 2, -1, -1):
-            e = jnp.where(i // tiles == n, order[n], e)
-        return (0, (w[1] ^ e) * tiles + lax.rem(i, tiles))
-
+    out_shape = jax.ShapeDtypeStruct((rows, feats), jnp.bfloat16)
+    out_spec = pl.BlockSpec((rows, tile), lambda i, w: (0, i))
+    if keep:
+        out_shape = (out_shape, jax.ShapeDtypeStruct((rows, depth), jnp.bfloat16))
+        out_spec = (out_spec, pl.BlockSpec((rows, depth), lambda i, w: (0, 0)))
     return pl.pallas_call(
-        partial(out_kernel, (shards, chans, groups, order)),
-        out_shape=jax.ShapeDtypeStruct((rows, feats * len(order)), jnp.bfloat16),
+        kernel,
+        out_shape=out_shape,
         grid_spec=pltpu.PrefetchScalarGridSpec(
             num_scalar_prefetch=1,
-            grid=(tiles * len(order),),
-            in_specs=[pl.BlockSpec((rows, chans), lambda i, w: (0, 0))] * shards
-            + [pl.BlockSpec(gain.shape, lambda i, w: (0, 0)), pl.BlockSpec((depth, tile), column)],
-            out_specs=pl.BlockSpec((rows, tile), lambda i, w: (0, i)),
-            scratch_shapes=[pltpu.VMEM((rows, depth), jnp.bfloat16)],
+            grid=(tiles,),
+            in_specs=[pl.BlockSpec(v.shape, lambda i, w: (0, 0)) for v in values]
+            + [pl.BlockSpec((depth, tile), lambda i, w: (0, (w[1] ^ e) * tiles + i))],
+            out_specs=out_spec,
         ),
-        compiler_params=pltpu.CompilerParams(vmem_limit_bytes=VMEM_LIMIT, dimension_semantics=("arbitrary",)),
+        compiler_params=pltpu.CompilerParams(vmem_limit_bytes=OUT_VMEM, dimension_semantics=("arbitrary",)),
         cost_estimate=pl.CostEstimate(
-            flops=2 * rows * depth * feats * len(order),
-            bytes_accessed=2 * depth * feats * len(order),
-            transcendentals=0,
+            flops=2 * rows * depth * feats, bytes_accessed=2 * depth * feats, transcendentals=0
         ),
-    )(where, *gated, gain, w_flat)
-
-
-def gather_tokens(tokens):
-    outer = lax.axis_size("seq") // 2
-    half = outer // 2
+    )(where, *values, w_flat)
+
+
+def line(value, pairs):
+    return lax.ppermute(value, "seq", [(2 * a + y, 2 * b + y) for a, b in pairs for y in (0, 1)])
+
+
+def stack(*parts):
+    return jnp.concatenate(parts, axis=0)
+
+
+def both_cores(value):
+    pairs = [[i, i + 1] for i in range(0, lax.axis_size("head"), 2)]
+    return lax.all_gather(value, "head", axis=0, axis_index_groups=pairs)
+
+
+def together(*values):
+    return lax.optimization_barrier(values)
+
+
+def exchange(tokens, main, far_map, own_map, dt_rows):
     at = lax.axis_index("seq") // 2
-
-    def line(value, pairs):
-        return lax.ppermute(value, "seq", [(2 * a + y, 2 * b + y) for a, b in pairs for y in (0, 1)])
-
-    near = swap(tokens, "seq", 2)
-    crossing = [line(v, [(1, 2), (2, 1)]) for v in (tokens, near)]
-    outward = [line(v, [(1, 0), (2, 3)]) for v in crossing]
     middle = (at == 1) | (at == 2)
-    far = [jnp.where(middle, a, b) for a, b in zip(crossing, outward)]
-    rows = [tokens, near, *far]
-    both = []
-    for value in rows:
-        both += [value, swap(value, "seq", 1)]
-    pairs = [(v, swap(v, "head", 2)) for v in both]
-    pieces = [(a, swap(a, "head", 1), b, swap(b, "head", 1)) for a, b in pairs]
-    return pieces, far
+    cross, outward = [(1, 2), (2, 1)], [(1, 0), (2, 3)]
+
+    def x_swap(v):
+        return swap(v, "head", 2)
+
+    def s_swap(v, bit):
+        return swap(v, "seq", bit)
+
+    xp, y0, z1, c0, dt_y, main, far_map, own_map = together(
+        x_swap(tokens),
+        s_swap(tokens, 1),
+        s_swap(tokens, 2),
+        line(tokens, cross),
+        s_swap(dt_rows, 1),
+        main,
+        far_map,
+        own_map,
+    )
+    dt_rows = stack(dt_rows, dt_y)
+    xy, yz1, c1, o0, dt_z = together(
+        x_swap(y0), s_swap(z1, 1), line(z1, cross), line(c0, outward), s_swap(dt_rows, 2)
+    )
+    dt_rows = stack(dt_rows, dt_z)
+    q1 = jnp.where(middle, c0, o0)
+    q1, z1, yz1, c1, far_map, dt_rows, m7 = together(q1, z1, yz1, c1, far_map, dt_rows, main[7])
+    a1 = stack(z1, yz1)
+    xa1, w7, yq1, o1, far_map, dt_far = together(
+        x_swap(a1), s_swap(m7, 7), s_swap(q1, 1), line(c1, outward), s_swap(far_map, 4), s_swap(dt_rows, 4)
+    )
+    own = [stack(tokens, y0), a1]
+    across = [stack(xp, xy), xa1]
+    dt_rows = stack(dt_rows, dt_far)
+    q2 = jnp.where(middle, c1, o1)
+    a2 = stack(q1, yq1)
+    maps = stack(own_map, far_map)
+    half = main[6].shape[0] // 2
+    q2, a2, maps, m5, m6, m1 = together(q2, a2, maps, main[5], main[6][:half], main[1])
+    xa2, w6a, w5, yq2, maps_z, w1 = together(
+        x_swap(a2), s_swap(m6, 6), s_swap(m5, 5), s_swap(q2, 1), s_swap(maps, 2), s_swap(m1, 1)
+    )
+    a3 = stack(q2, yq2)
+    a3, maps, maps_z, m4, m6, m3, m2 = together(
+        a3, maps, maps_z, main[4], main[6][half:], main[3], main[2]
+    )
+    maps = stack(maps, maps_z)
+    xa3, w4, maps_y, w6b, w3, w2 = together(
+        x_swap(a3), s_swap(m4, 4), s_swap(maps, 1), s_swap(m6, 6), s_swap(m3, 3), s_swap(m2, 2)
+    )
+    own += [a2, a3]
+    across += [xa2]
+    gathered = [both_cores(v) for v in own + across]
+    last = (xa3, swap(xa3, "head", 1))
+    mains = [main[0], w1, w2, w3, w4, w5, stack(w6a, w6b), w7]
+    krows = far_map.shape[0]
+    place = {0: (maps, 0), 4: (maps, 1), 2: (maps, 2), 6: (maps, 3)}
+    place.update({d | 1: (maps_y, n) for d, (_, n) in list(place.items())})
+    maps_of = [(0 if place[d][0] is maps else 1, place[d][1] * krows) for d in range(8)]
+    return gathered, last, mains, (maps, maps_y), maps_of, dt_rows
 
 
 def piece_table(shards):
@@ -336,40 +430,25 @@
     per = shards // groups
     dim = krows * shards
 
-    pieces, far = gather_tokens(tokens)
-
     gain = lax.dynamic_slice_in_dim(norm_gain, s * krows, krows, 0)
 
     def columns(t, first, count):
         part = lax.dynamic_slice(w_in, (0, t // per, first), (krows, 1, count))[:, 0]
         return (part.astype(jnp.float32) * gain[:, None]).astype(jnp.bfloat16)
 
-    to_send = []
+    main = []
     for d in range(shards):
         t = s ^ d
         first = (t % per) * chans
-        to_send.append(
+        main.append(
             jnp.concatenate([columns(t, first, chans), columns(t, group_width + first, chans)], axis=1)
         )
     far_map = columns(s ^ per, 2 * group_width, 2 * state_size)
     own_map = columns(s, 2 * group_width, 2 * state_size)
-    dt_w = lax.all_gather(
-        (w_dt.astype(jnp.float32) * gain[:, None]).astype(jnp.bfloat16), "seq", axis=0, tiled=True
-    )
-    dt_w = lax.dynamic_slice_in_dim(dt_w, s * heads, heads, 1)
-    dt_w = jnp.pad(dt_w, ((0, 0), (0, LANES - heads)))
-    to_send, far_map = after((to_send, far_map), *far)
-    maps = [own_map] + [None] * (shards - 1)
-    maps[per] = swap(far_map, "seq", per)
-    bit = per // 2
-    while bit:
-        for d in [d for d in range(shards) if maps[d] is not None]:
-            if not d & bit and maps[d | bit] is None:
-                maps[d | bit] = swap(maps[d], "seq", bit)
-        bit //= 2
-    mains = [to_send[0]] + [None] * (shards - 1)
-    for d in range(shards - 1, 0, -1):
-        mains[d] = swap(to_send[d], "seq", d)
+    dt_rows = (w_dt.T.astype(jnp.float32) * gain[None, :]).astype(jnp.bfloat16)
+    gathered, last, mains, maps, maps_of, dt_rows = exchange(tokens, main, far_map, own_map, dt_rows)
+    dt_rows = lax.dynamic_slice_in_dim(dt_rows.reshape(shards, local_heads, krows), s * heads, heads, 1)
+    dt_w = jnp.pad(jnp.swapaxes(dt_rows, 1, 2), ((0, 0), (0, 0), (0, LANES - heads)))
 
     group = s // per
     quarter = (s % per) * chans
@@ -388,9 +467,11 @@
     where = jnp.concatenate([jnp.stack([s, h]), piece_table(shards)]).astype(jnp.int32)
     gated = mixer(
         where,
-        pieces,
+        gathered,
+        last,
         mains,
         maps,
+        maps_of,
         dt_w,
         own_channels(conv_w),
         own_channels(conv_b)[None, :],
@@ -411,13 +492,17 @@
 
     gains = gate_gain.reshape(shards, chans)
     w_flat = w_out.reshape(groups * group_width, w_out.shape[2])
-    feats = w_flat.shape[1] // blocks
-    lead = out_terms(where, arrived, gains, w_flat, groups, blocks, (3, 1))
-    other = swap(lead, "head", 1)
-    own = out_terms(where, arrived, gains, w_flat, groups, blocks, (2, 0))
-    wide_sum = own.astype(jnp.float32) + other.astype(jnp.float32)
-    beyond = swap(wide_sum[:, :feats].astype(jnp.bfloat16), "head", 2)
-    return (wide_sum[:, feats:] + beyond.astype(jnp.float32)).astype(jnp.bfloat16)
+    wide = jnp.float32
+    first, flat = out_terms(
+        partial(normed_terms_kernel, (shards, chans, groups)), where, [*arrived, gains], w_flat, rows, blocks, 3, True
+    )
+    via_core = swap(first, "head", 1)
+    second = out_terms(terms_kernel, where, [flat], w_flat, rows, blocks, 2, False)
+    beyond = swap((second.astype(wide) + via_core.astype(wide)).astype(jnp.bfloat16), "head", 2)
+    third = out_terms(terms_kernel, where, [flat], w_flat, rows, blocks, 1, False)
+    from_core = swap(third, "head", 1)
+    own = out_terms(terms_kernel, where, [flat], w_flat, rows, blocks, 0, False)
+    return (own.astype(wide) + from_core.astype(wide) + beyond.astype(wide)).astype(jnp.bfloat16)
 
 
 def fits_head_split(mesh, w_in, gate_gain, dt_bias):

time: 452 us -> 377 us (0.83)
  waiting for transfers between devices: 224 us -> 167 us
  blocking collectives: 48.6 us -> 0 us
  between operations: 0.97 us -> 14 us
  other arithmetic: 13 us -> 25.5 us
  starting transfers between devices: 60.4 us -> 54.1 us
  Pallas kernels: 73.2 us -> 78.6 us
  local copies, waits for them, and re-layouts: 31.5 us -> 36.5 us
    all_gather x1 -> x0, blocking collectives: 48.6 us -> none  [head_split_body(): lax.all_gather((w_dt.astype(jnp.float32) * gain[:, None]).astype(jnp.bflo...]
    ppermute x52 -> x35, waiting for transfers between devices: 211 us -> 167 us  [swap(): return lax.ppermute(value, axis, [(i, i ^ bit) for i in range(count)])]
    ppermute x4, waiting for transfers between devices: 13 us -> 0.01 us  [line(): lax.ppermute(value, 'seq', [(2 * a + y, 2 * b + y) for a, b in pairs for...]
    concatenate x0 -> x9, other arithmetic: none -> 12.4 us  [stack(): return jnp.concatenate(parts, axis=0)]
    ppermute x52 -> x35, starting transfers between devices: 50.4 us -> 41.4 us  [swap(): return lax.ppermute(value, axis, [(i, i ^ bit) for i in range(count)])]
    pallas_call x2 -> x4, Pallas kernels: 18.5 us -> 26.2 us  [out_terms(): pl.pallas_call(kernel, out_shape=out_shape, grid_spec=pltpu.PrefetchScala...]
    unnamed x104 -> x85, local copies, waits for them, and re-layouts: 6.19 us -> 10.8 us
  transfers between devices with their start and end apart: 56 -> 46, of which waited for: 24 -> 17; matrix products, arithmetic and copies ran while one was open for 7% -> 12% of each run, Pallas kernels for 2% -> 5%
where the time goes in v2:
time: 377 us; the launch traced here: 376 us
  waiting for transfers between devices  167 us (44%)
  Pallas kernels  78.6 us (21%)
  starting transfers between devices  54.1 us (14%)
  local copies, waits for them, and re-layouts  36.5 us (10%)
  other arithmetic  25.5 us (7%)
  between operations  14 us (4%)
    ppermute x35, waiting for transfers between devices, swap(): return lax.ppermute(value, axis, [(i, i ^ bit) for i in range(count)])  167 us
    pallas_call x1, Pallas kernels, mixer(): pl.pallas_call(partial(mixer_kernel, cfg), out_shape=jax.ShapeDtypeStruct...  52.4 us
    ppermute x35, starting transfers between devices, swap(): return lax.ppermute(value, axis, [(i, i ^ bit) for i in range(count)])  41.4 us
    pallas_call x4, Pallas kernels, out_terms(): pl.pallas_call(kernel, out_shape=out_shape, grid_spec=pltpu.PrefetchScala...  26.2 us
    dynamic_slice x2, local copies, waits for them, and re-layouts, columns(): lax.dynamic_slice(w_in, (0, t // per, first), (krows, 1, count))[:, 0]  17.6 us
    ppermute x4, starting transfers between devices, line(): lax.ppermute(value, 'seq', [(2 * a + y, 2 * b + y) for a, b in pairs for...  12.5 us
    concatenate x9, other arithmetic, stack(): return jnp.concatenate(parts, axis=0)  12.4 us
    unnamed x85, local copies, waits for them, and re-layouts  10.8 us
  transfers between devices with their start and end apart: 46, of which 17 were waited for; matrix products, arithmetic and copies ran while one was open for 12% of the time, Pallas kernels for 5%

profile of v2, /device:TPU:8, one launch (start us, length us, event | category | flops | bytes accessed | tf_op | source)
XLA Modules:
  0.0 376.2 jit_solution(1593662877190358870)
XLA Ops:
  10.0 4.6 %collective-permute-start.3 = (bf16[384,1024]{1,0:T(8,128)(2,1)}, bf16[384,1024]{1,0:T(8,128)(2,1)S(1)}, u32[]{:S(2)}, u32[]{:S(2)}) collective-permute-start(bf16[384,1024]{1,0:T(8,128)(2,1)} %param.11), channel_id=1, source_target_pairs={{8,16},{12,20},{16,8},{20,12},{9,17},{13,21},{17,9},{21,13},{10,18... | collective-permute-start | bytes 2359304 | tf_op jit(solution)/shard_map/ppermute | solution.py:329
  16.7 6.4 %constant_dynamic-slice_fusion.24 = (bf16[512,1,256]{2,1,0:T(2,128)(2,1)S(1)}, bf16[512,1,256]{2,1,0:T(2,128)(2,1)S(1)}, bf16[512,1,256]{2,1,0:T(2,128)(2,1)S(1)...) fusion(bf16[512,2,2304]{2,1,0:T(2,128)(2,1)} %param.13, s32[]{:T(128)S(6)} %select_n.241, s32[]{:T(128)S(6)} %select_n.243, ...), kind=kLoop, calls=%fused_computation.107 | loop fusion | bytes 2621472 | tf_op jit(solution)/shard_map/dynamic_slice | solution.py:436
  23.1 11.2 %constant_dynamic-slice_fusion.11 = (bf16[512,1,256]{2,1,0:T(2,128)(2,1)S(1)}, bf16[512,1,256]{2,1,0:T(2,128)(2,1)S(1)}, bf16[512,1,256]{2,1,0:T(2,128)(2,1)S(1)...) fusion(bf16[512,2,2304]{2,1,0:T(2,128)(2,1)S(1)} %copy-done.2, ...), kind=kLoop, calls=%fused_computation.94 | loop fusion | bytes 6815816 | tf_op jit(solution)/shard_map/dynamic_slice | solution.py:436
  41.1 2.5 pad_maximum_fusion
  49.3 16.2 %collective-permute-done.9 = bf16[64,512]{1,0:T(8,128)(2,1)S(1)} collective-permute-done((bf16[64,512]{1,0:T(8,128)(2,1)S(1)}, bf16[64,512]{1,0:T(8,128)(2,1)S(1)}, u32[]{:S(2)}, u32[]{:S(2)}) %collective-permute-start.9) | collective-permute-done | bytes 65568 | tf_op jit(solution)/shard_map/ppermute | solution.py:22
  66.4 2.9 pad_maximum_fusion.3
  74.4 4.4 %collective-permute-start.13 = (bf16[384,1024]{1,0:T(8,128)(2,1)}, bf16[384,1024]{1,0:T(8,128)(2,1)S(1)}, u32[]{:S(2)}, u32[]{:S(2)}) collective-permute-start(bf16[384,1024]{1,0:T(8,128)(2,1)} %copy-done.6), channel_id=1, source_target_pairs={{8,0},{12,4},{16,24},{20,28},{9,1},{13,5},{17,25},{21,29},{10,2},{... | collective-permute-start | bytes 2359304 | tf_op jit(solution)/shard_map/ppermute | solution.py:329
  78.8 2.5 collective-permute-start.11
  81.3 24.5 %collective-permute-done.15 = bf16[128,512]{1,0:T(8,128)(2,1)S(1)} collective-permute-done((bf16[128,512]{1,0:T(8,128)(2,1)S(1)}, bf16[128,512]{1,0:T(8,128)(2,1)S(1)}, u32[]{:S(2)}, u32[]{:S(2)}) %collective-permute-start.15) | collective-permute-done | bytes 131104 | tf_op jit(solution)/shard_map/ppermute | solution.py:22
  105.9 3.4 collective-permute-start.14
  110.1 9.6 %collective-permute-done.14 = bf16[512,256]{1,0:T(8,128)(2,1)S(1)} collective-permute-done((bf16[512,256]{1,0:T(8,128)(2,1)}, bf16[512,256]{1,0:T(8,128)(2,1)S(1)}, u32[]{:S(2)}, u32[]{:S(2)}) %collective-permute-start.14) | collective-permute-done | bytes 262176 | tf_op jit(solution)/shard_map/ppermute | solution.py:22
  121.9 2.6 pad_maximum_fusion.1
  128.9 4.7 %collective-permute-start.18 = (bf16[512,512]{1,0:T(8,128)(2,1)}, bf16[512,512]{1,0:T(8,128)(2,1)S(1)}, u32[]{:S(2)}, u32[]{:S(2)}) collective-permute-start(bf16[512,512]{1,0:T(8,128)(2,1)} %get-tuple-element.92), channel_id=1, source_target_pairs={{0,20},{4,16},{8,28},{12,24},{16,4},{20,0},{24,12},{28,8},{1,21},{... | collective-permute-start | bytes 1572872 | tf_op jit(solution)/shard_map/ppermute | solution.py:22
  133.6 19.0 %collective-permute-done.17 = bf16[256,512]{1,0:T(8,128)(2,1)S(1)} collective-permute-done((bf16[256,512]{1,0:T(8,128)(2,1)S(1)}, bf16[256,512]{1,0:T(8,128)(2,1)S(1)}, u32[]{:S(2)}, u32[]{:S(2)}) %collective-permute-start.17) | collective-permute-done | bytes 262176 | tf_op jit(solution)/shard_map/ppermute | solution.py:22
  153.5 8.1 %collective-permute-done.18.refs_14_ = bf16[512,512]{1,0:T(8,128)(2,1)S(1)} collective-permute-done((bf16[512,512]{1,0:T(8,128)(2,1)}, bf16[512,512]{1,0:T(8,128)(2,1)S(1)}, u32[]{:S(2)}, u32[]{:S(2)}) %collective-permute-start.18) | collective-permute-done | bytes 524320 | tf_op jit(solution)/shard_map/ppermute | solution.py:22
  161.6 7.7 %collective-permute-done.21.refs_10_ = bf16[512,512]{1,0:T(8,128)(2,1)S(1)} collective-permute-done((bf16[512,512]{1,0:T(8,128)(2,1)}, bf16[512,512]{1,0:T(8,128)(2,1)S(1)}, u32[]{:S(2)}, u32[]{:S(2)}) %collective-permute-start.21) | collective-permute-done | bytes 524320 | tf_op jit(solution)/shard_map/ppermute | solution.py:22
  171.0 2.5 pad_maximum_fusion.2
  178.1 5.1 %collective-permute-start.23 = (bf16[512,512]{1,0:T(8,128)(2,1)}, bf16[512,512]{1,0:T(8,128)(2,1)S(1)}, u32[]{:S(2)}, u32[]{:S(2)}) collective-permute-start(bf16[512,512]{1,0:T(8,128)(2,1)} %get-tuple-element.105), channel_id=1, source_target_pairs={{0,16},{4,20},{8,24},{12,28},{16,0},{20,4},{24,8},{28,12},{1,17},{... | collective-permute-start | bytes 1572872 | tf_op jit(solution)/shard_map/ppermute | solution.py:22
  183.7 19.1 %collective-permute-done.25 = bf16[256,512]{1,0:T(8,128)(2,1)S(1)} collective-permute-done((bf16[256,512]{1,0:T(8,128)(2,1)S(1)}, bf16[256,512]{1,0:T(8,128)(2,1)S(1)}, u32[]{:S(2)}, u32[]{:S(2)}) %collective-permute-start.25) | collective-permute-done | bytes 262176 | tf_op jit(solution)/shard_map/ppermute | solution.py:22
  202.8 7.5 %collective-permute-done.23.refs_13_ = bf16[512,512]{1,0:T(8,128)(2,1)S(1)} collective-permute-done((bf16[512,512]{1,0:T(8,128)(2,1)}, bf16[512,512]{1,0:T(8,128)(2,1)S(1)}, u32[]{:S(2)}, u32[]{:S(2)}) %collective-permute-start.23) | collective-permute-done | bytes 524320 | tf_op jit(solution)/shard_map/ppermute | solution.py:22
  210.3 3.2 collective-permute-done.26.refs_12_
  213.5 7.7 %collective-permute-done.27.refs_11_ = bf16[512,512]{1,0:T(8,128)(2,1)S(1)} collective-permute-done((bf16[512,512]{1,0:T(8,128)(2,1)}, bf16[512,512]{1,0:T(8,128)(2,1)S(1)}, u32[]{:S(2)}, u32[]{:S(2)}) %collective-permute-start.27) | collective-permute-done | bytes 524320 | tf_op jit(solution)/shard_map/ppermute | solution.py:22
  229.4 52.4 %shard_map.109 = bf16[3072,256]{1,0:T(8,128)(2,1)} custom-call(s32[10]{0:T(128)} %pad_add_fusion.where_ref, bf16[2,768,1024]{2,1,0:T(8,128)(2,1)} %bitcast.128, bf16[2,768,1024]{2,1,0:T(8,128)(2,1)} %bitcast.130, bf16[2,768,1024]{2,1,0:T(8,128)(2,1)} %bitcast.131, bf16[2,768,1024]{2,1,0:T(8,128)(2,1)} %bitcast.133, bf16[2,768,1024]{2,1,0:T(8,128)(2,1)} %bitcast.129, ...), custom_call_target="tpu_custom_call" | custom-call | flops 22548578304 | bytes 25165824 | tf_op jit(solution)/shard_map/pallas_call | solution.py:246
  291.9 6.3 %collective-permute-done.30.refs_2_ = bf16[384,256]{1,0:T(8,128)(2,1)S(1)} collective-permute-done((bf16[384,256]{1,0:T(8,128)(2,1)S(1)}, bf16[384,256]{1,0:T(8,128)(2,1)S(1)}, u32[]{:S(2)}, u32[]{:S(2)}) %collective-permute-start.30) | collective-permute-done | bytes 196640 | tf_op jit(solution)/shard_map/ppermute | solution.py:22
  301.7 14.5 %collective-permute-done.33.refs_5_ = bf16[384,256]{1,0:T(8,128)(2,1)S(1)} collective-permute-done((bf16[384,256]{1,0:T(8,128)(2,1)S(1)}, bf16[384,256]{1,0:T(8,128)(2,1)S(1)}, u32[]{:S(2)}, u32[]{:S(2)}) %collective-permute-start.33) | collective-permute-done | bytes 196640 | tf_op jit(solution)/shard_map/ppermute | solution.py:22
  316.3 5.2 %collective-permute-done.34.refs_6_ = bf16[384,256]{1,0:T(8,128)(2,1)S(1)} collective-permute-done((bf16[384,256]{1,0:T(8,128)(2,1)S(1)}, bf16[384,256]{1,0:T(8,128)(2,1)S(1)}, u32[]{:S(2)}, u32[]{:S(2)}) %collective-permute-start.34) | collective-permute-done | bytes 196640 | tf_op jit(solution)/shard_map/ppermute | solution.py:22
  321.5 3.4 collective-permute-done.35.refs_7_
  325.6 7.3 %shard_map.110 = (bf16[384,1024]{1,0:T(8,128)(2,1)}, bf16[384,2048]{1,0:T(8,128)(2,1)}) custom-call(s32[10]{0:T(128)} %pad_add_fusion.where_ref, bf16[384,256]{1,0:T(8,128)(2,1)} %get-tuple-element.150.refs_0_, bf16[384,256]{1,0:T(8,128)(2,1)} %copy-done.22, bf16[384,256]{1,0:T(8,128)(2,1)} %copy-done.23, bf16[384,256]{1,0:T(8,128)(2,1)} %copy-done.24, ...), custom_call_target="tpu_custom_call" | custom-call | flops 1610612736 | bytes 4194304 | tf_op jit(solution)/shard_map/pallas_call | solution.py:311
  332.9 6.3 %shard_map.112 = bf16[384,1024]{1,0:T(8,128)(2,1)} custom-call(s32[10]{0:T(128)} %pad_add_fusion.where_ref, bf16[384,2048]{1,0:T(8,128)(2,1)} %get-tuple-element.123.flat, bf16[2048,4096]{1,0:T(8,128)(2,1)} %bitcast.118), custom_call_target="tpu_custom_call" | custom-call | flops 1610612736 | bytes 4194304 | tf_op jit(solution)/shard_map/pallas_call | solution.py:311
  339.7 6.3 %shard_map.113 = bf16[384,1024]{1,0:T(8,128)(2,1)} custom-call(s32[10]{0:T(128)} %pad_add_fusion.where_ref, bf16[384,2048]{1,0:T(8,128)(2,1)} %get-tuple-element.123.flat, bf16[2048,4096]{1,0:T(8,128)(2,1)} %bitcast.119), custom_call_target="tpu_custom_call" | custom-call | flops 1610612736 | bytes 4194304 | tf_op jit(solution)/shard_map/pallas_call | solution.py:311
  348.0 6.4 %shard_map.111 = bf16[384,1024]{1,0:T(8,128)(2,1)} custom-call(s32[10]{0:T(128)} %pad_add_fusion.where_ref, bf16[384,2048]{1,0:T(8,128)(2,1)} %get-tuple-element.123.flat, bf16[2048,4096]{1,0:T(8,128)(2,1)} %bitcast.120), custom_call_target="tpu_custom_call" | custom-call | flops 1610612736 | bytes 4194304 | tf_op jit(solution)/shard_map/pallas_call | solution.py:311
  354.4 12.5 %collective-permute-done.38 = bf16[384,1024]{1,0:T(8,128)(2,1)S(1)} collective-permute-done((bf16[384,1024]{1,0:T(8,128)(2,1)S(1)}, bf16[384,1024]{1,0:T(8,128)(2,1)S(1)}, u32[]{:S(2)}, u32[]{:S(2)}) %collective-permute-start.38) | collective-permute-done | bytes 786464 | tf_op jit(solution)/shard_map/ppermute | solution.py:22
  (200 shorter events, 66.2 us)
Async XLA Ops:
  6.5 222.8 %all-gather.15.cloned.1.call-start = ((), (), s32[]{:S(2)}) async-start(), calls=%async_computation | async-start | bytes 4718592 | tf_op jit(solution)/shard_map/all_gather | solution.py:338
  6.5 34.2 %collective-permute-start = (bf16[384,1024]{1,0:T(8,128)(2,1)}, bf16[384,1024]{1,0:T(8,128)(2,1)S(1)}, u32[]{:S(2)}, u32[]{:S(2)}) collective-permute-start(bf16[384,1024]{1,0:T(8,128)(2,1)} %param.11), channel_id=1, source_target_pairs={{0,2},{1,3},{2,0},{3,1},{4,6},{5,7},{6,4},{7,5},{8,10},{9,11},{10,... | collective-permute-start | bytes 2359304 | tf_op jit(solution)/shard_map/ppermute | solution.py:22
  8.0 32.7 %collective-permute-start.1 = (bf16[384,1024]{1,0:T(8,128)(2,1)}, bf16[384,1024]{1,0:T(8,128)(2,1)}, u32[]{:S(2)}, u32[]{:S(2)}) collective-permute-start(bf16[384,1024]{1,0:T(8,128)(2,1)} %param.11), channel_id=1, source_target_pairs={{0,4},{4,0},{8,12},{12,8},{16,20},{20,16},{24,28},{28,24},{1,5},{5... | collective-permute-start | bytes 2359304 | tf_op jit(solution)/shard_map/ppermute | solution.py:22
  9.6 31.2 %collective-permute-start.2 = (bf16[384,1024]{1,0:T(8,128)(2,1)}, bf16[384,1024]{1,0:T(8,128)(2,1)}, u32[]{:S(2)}, u32[]{:S(2)}) collective-permute-start(bf16[384,1024]{1,0:T(8,128)(2,1)} %param.11), channel_id=1, source_target_pairs={{0,8},{4,12},{8,0},{12,4},{16,24},{20,28},{24,16},{28,20},{1,9},{5... | collective-permute-start | bytes 2359304 | tf_op jit(solution)/shard_map/ppermute | solution.py:22
  10.0 30.7 %collective-permute-start.3 = (bf16[384,1024]{1,0:T(8,128)(2,1)}, bf16[384,1024]{1,0:T(8,128)(2,1)S(1)}, u32[]{:S(2)}, u32[]{:S(2)}) collective-permute-start(bf16[384,1024]{1,0:T(8,128)(2,1)} %param.11), channel_id=1, source_target_pairs={{8,16},{12,20},{16,8},{20,12},{9,17},{13,21},{17,9},{21,13},{10,18... | collective-permute-start | bytes 2359304 | tf_op jit(solution)/shard_map/ppermute | solution.py:329
  16.1 24.5 %collective-permute-start.4 = (bf16[32,512]{1,0:T(8,128)(2,1)S(1)}, bf16[32,512]{1,0:T(8,128)(2,1)S(1)}, u32[]{:S(2)}, u32[]{:S(2)}) collective-permute-start(bf16[32,512]{1,0:T(8,128)(2,1)S(1)} %fusion.18), channel_id=1, source_target_pairs={{0,4},{4,0},{8,12},{12,8},{16,20},{20,16},{24,28},{28,24},{1,5},{5... | collective-permute-start | bytes 98312 | tf_op jit(solution)/shard_map/ppermute | solution.py:22
  43.6 185.7 %all-gather.23.cloned.1.call-start = ((), (), s32[]{:S(2)}) async-start(), calls=%async_computation.4 | async-start | bytes 4718592 | tf_op jit(solution)/shard_map/all_gather | solution.py:338
  43.7 21.8 %collective-permute-start.5 = (bf16[384,1024]{1,0:T(8,128)(2,1)}, bf16[384,1024]{1,0:T(8,128)(2,1)S(1)}, u32[]{:S(2)}, u32[]{:S(2)}) collective-permute-start(bf16[384,1024]{1,0:T(8,128)(2,1)} %collective-permute-done.1), channel_id=1, source_target_pairs={{0,2},{1,3},{2,0},{3,1},{4,6},{5,7},{6,4},{7,5},{8,10},{9,11},{10,... | collective-permute-start | bytes 2359304 | tf_op jit(solution)/shard_map/ppermute | solution.py:22
  44.3 21.2 %collective-permute-start.6 = (bf16[384,1024]{1,0:T(8,128)(2,1)}, bf16[384,1024]{1,0:T(8,128)(2,1)S(1)}, u32[]{:S(2)}, u32[]{:S(2)}) collective-permute-start(bf16[384,1024]{1,0:T(8,128)(2,1)} %collective-permute-done.2), channel_id=1, source_target_pairs={{0,4},{4,0},{8,12},{12,8},{16,20},{20,16},{24,28},{28,24},{1,5},{5... | collective-permute-start | bytes 2359304 | tf_op jit(solution)/shard_map/ppermute | solution.py:22
  69.3 160.0 %all-gather.17.cloned.1.call-start = ((), (), s32[]{:S(2)}) async-start(), calls=%async_computation.1 | async-start | bytes 4718592 | tf_op jit(solution)/shard_map/all_gather | solution.py:338
  72.0 157.3 %all-gather.19.cloned.1.call-start = ((), (), s32[]{:S(2)}) async-start(), calls=%async_computation.2 | async-start | bytes 4718592 | tf_op jit(solution)/shard_map/all_gather | solution.py:338
  72.1 48.6 %collective-permute-start.10 = (bf16[768,1024]{1,0:T(8,128)(2,1)}, bf16[768,1024]{1,0:T(8,128)(2,1)}, u32[]{:S(2)}, u32[]{:S(2)}) collective-permute-start(bf16[768,1024]{1,0:T(8,128)(2,1)} %copy-done.5), channel_id=1, source_target_pairs={{0,2},{1,3},{2,0},{3,1},{4,6},{5,7},{6,4},{7,5},{8,10},{9,11},{10,... | collective-permute-start | bytes 4718600 | tf_op jit(solution)/shard_map/ppermute | solution.py:22
  73.7 46.1 %collective-permute-start.12 = (bf16[384,1024]{1,0:T(8,128)(2,1)S(1)}, bf16[384,1024]{1,0:T(8,128)(2,1)S(1)}, u32[]{:S(2)}, u32[]{:S(2)}) collective-permute-start(bf16[384,1024]{1,0:T(8,128)(2,1)S(1)} %broadcast_select_fusion.1), channel_id=1, source_target_pairs={{0,4},{4,0},{8,12},{12,8},{16,20},{20,16},{24,28},{28,24},{1,5},{5... | collective-permute-start | bytes 2359304 | tf_op jit(solution)/shard_map/ppermute | solution.py:22
  74.4 45.4 %collective-permute-start.13 = (bf16[384,1024]{1,0:T(8,128)(2,1)}, bf16[384,1024]{1,0:T(8,128)(2,1)S(1)}, u32[]{:S(2)}, u32[]{:S(2)}) collective-permute-start(bf16[384,1024]{1,0:T(8,128)(2,1)} %copy-done.6), channel_id=1, source_target_pairs={{8,0},{12,4},{16,24},{20,28},{9,1},{13,5},{17,25},{21,29},{10,2},{... | collective-permute-start | bytes 2359304 | tf_op jit(solution)/shard_map/ppermute | solution.py:329
  78.8 41.0 %collective-permute-start.11 = (bf16[512,512]{1,0:T(8,128)(2,1)}, bf16[512,512]{1,0:T(8,128)(2,1)S(1)}, u32[]{:S(2)}, u32[]{:S(2)}) collective-permute-start(bf16[512,512]{1,0:T(8,128)(2,1)} %get-tuple-element.78), channel_id=1, source_target_pairs={{0,28},{4,24},{8,20},{12,16},{16,12},{20,8},{24,4},{28,0},{1,29},{... | collective-permute-start | bytes 1572872 | tf_op jit(solution)/shard_map/ppermute | solution.py:22
  81.3 24.5 %collective-permute-start.15 = (bf16[128,512]{1,0:T(8,128)(2,1)S(1)}, bf16[128,512]{1,0:T(8,128)(2,1)S(1)}, u32[]{:S(2)}, u32[]{:S(2)}) collective-permute-start(bf16[128,512]{1,0:T(8,128)(2,1)S(1)} %pad_maximum_fusion.15), channel_id=1, source_target_pairs={{0,16},{4,20},{8,24},{12,28},{16,0},{20,4},{24,8},{28,12},{1,17},{... | collective-permute-start | bytes 393224 | tf_op jit(solution)/shard_map/ppermute | solution.py:22
  124.6 104.7 %all-gather.25.cloned.1.call-start = ((), (), s32[]{:S(2)}) async-start(), calls=%async_computation.5 | async-start | bytes 4718592 | tf_op jit(solution)/shard_map/all_gather | solution.py:338
  125.2 104.2 %all-gather.21.cloned.1.call-start = ((), (), s32[]{:S(2)}) async-start(), calls=%async_computation.3 | async-start | bytes 4718592 | tf_op jit(solution)/shard_map/all_gather | solution.py:338
  125.9 45.1 %collective-permute-start.16 = (bf16[768,1024]{1,0:T(8,128)(2,1)S(1)}, bf16[768,1024]{1,0:T(8,128)(2,1)}, u32[]{:S(2)}, u32[]{:S(2)}) collective-permute-start(bf16[768,1024]{1,0:T(8,128)(2,1)S(1)} %copy-done.3), channel_id=1, source_target_pairs={{0,2},{1,3},{2,0},{3,1},{4,6},{5,7},{6,4},{7,5},{8,10},{9,11},{10,... | collective-permute-start | bytes 4718600 | tf_op jit(solution)/shard_map/ppermute | solution.py:22
  126.5 26.1 %collective-permute-start.17 = (bf16[256,512]{1,0:T(8,128)(2,1)S(1)}, bf16[256,512]{1,0:T(8,128)(2,1)S(1)}, u32[]{:S(2)}, u32[]{:S(2)}) collective-permute-start(bf16[256,512]{1,0:T(8,128)(2,1)S(1)} %copy-done.20), channel_id=1, source_target_pairs={{0,24},{4,28},{8,16},{12,20},{16,8},{20,12},{24,0},{28,4},{1,25},{... | collective-permute-start | bytes 786440 | tf_op jit(solution)/shard_map/ppermute | solution.py:22
  127.9 41.4 %collective-permute-start.19 = (bf16[384,1024]{1,0:T(8,128)(2,1)S(1)}, bf16[384,1024]{1,0:T(8,128)(2,1)S(1)}, u32[]{:S(2)}, u32[]{:S(2)}) collective-permute-start(bf16[384,1024]{1,0:T(8,128)(2,1)S(1)} %broadcast_select_fusion), channel_id=1, source_target_pairs={{0,4},{4,0},{8,12},{12,8},{16,20},{20,16},{24,28},{28,24},{1,5},{5... | collective-permute-start | bytes 2359304 | tf_op jit(solution)/shard_map/ppermute | solution.py:22
  128.9 32.7 %collective-permute-start.18 = (bf16[512,512]{1,0:T(8,128)(2,1)}, bf16[512,512]{1,0:T(8,128)(2,1)S(1)}, u32[]{:S(2)}, u32[]{:S(2)}) collective-permute-start(bf16[512,512]{1,0:T(8,128)(2,1)} %get-tuple-element.92), channel_id=1, source_target_pairs={{0,20},{4,16},{8,28},{12,24},{16,4},{20,0},{24,12},{28,8},{1,21},{... | collective-permute-start | bytes 1572872 | tf_op jit(solution)/shard_map/ppermute | solution.py:22
  133.6 28.0 %collective-permute-start.20 = (bf16[1024,256]{1,0:T(8,128)(2,1)S(1)}, bf16[1024,256]{1,0:T(8,128)(2,1)S(1)}, u32[]{:S(2)}, u32[]{:S(2)}) collective-permute-start(bf16[1024,256]{1,0:T(8,128)(2,1)S(1)} %pad_maximum_fusion.12), channel_id=1, source_target_pairs={{0,8},{4,12},{8,0},{12,4},{16,24},{20,28},{24,16},{28,20},{1,9},{5... | collective-permute-start | bytes 1572872 | tf_op jit(solution)/shard_map/ppermute | solution.py:22
  173.6 55.8 %all-gather.27.cloned.1.call-start = ((), (), s32[]{:S(2)}) async-start(), calls=%async_computation.6 | async-start | bytes 4718592 | tf_op jit(solution)/shard_map/all_gather | solution.py:338
  174.9 46.3 %collective-permute-start.22 = (bf16[768,1024]{1,0:T(8,128)(2,1)S(1)}, bf16[768,1024]{1,0:T(8,128)(2,1)}, u32[]{:S(2)}, u32[]{:S(2)}) collective-permute-start(bf16[768,1024]{1,0:T(8,128)(2,1)S(1)} %copy-done.4), channel_id=1, source_target_pairs={{0,2},{1,3},{2,0},{3,1},{4,6},{5,7},{6,4},{7,5},{8,10},{9,11},{10,... | collective-permute-start | bytes 4718600 | tf_op jit(solution)/shard_map/ppermute | solution.py:22
  176.6 44.7 %collective-permute-start.24 = (bf16[2048,256]{1,0:T(8,128)(2,1)S(1)}, bf16[2048,256]{1,0:T(8,128)(2,1)S(1)}, u32[]{:S(2)}, u32[]{:S(2)}) collective-permute-start(bf16[2048,256]{1,0:T(8,128)(2,1)S(1)} %constant_dynamic-update-slice_fusion.2.refs_17_), channel_id=1, source_target_pairs={{0,4},{4,0},{8,12},{12,8},{16,20},{20,16},{24,28},{28,24},{1,5},{5... | collective-permute-start | bytes 3145736 | tf_op jit(solution)/shard_map/ppermute | solution.py:22
  177.6 25.2 %collective-permute-start.25 = (bf16[256,512]{1,0:T(8,128)(2,1)S(1)}, bf16[256,512]{1,0:T(8,128)(2,1)S(1)}, u32[]{:S(2)}, u32[]{:S(2)}) collective-permute-start(bf16[256,512]{1,0:T(8,128)(2,1)S(1)} %copy-done.19), channel_id=1, source_target_pairs={{0,24},{4,28},{8,16},{12,20},{16,8},{20,12},{24,0},{28,4},{1,25},{... | collective-permute-start | bytes 786440 | tf_op jit(solution)/shard_map/ppermute | solution.py:22
  178.1 32.1 %collective-permute-start.23 = (bf16[512,512]{1,0:T(8,128)(2,1)}, bf16[512,512]{1,0:T(8,128)(2,1)S(1)}, u32[]{:S(2)}, u32[]{:S(2)}) collective-permute-start(bf16[512,512]{1,0:T(8,128)(2,1)} %get-tuple-element.105), channel_id=1, source_target_pairs={{0,16},{4,20},{8,24},{12,28},{16,0},{20,4},{24,8},{28,12},{1,17},{... | collective-permute-start | bytes 1572872 | tf_op jit(solution)/shard_map/ppermute | solution.py:22
  183.2 30.3 %collective-permute-start.26 = (bf16[512,512]{1,0:T(8,128)(2,1)}, bf16[512,512]{1,0:T(8,128)(2,1)S(1)}, u32[]{:S(2)}, u32[]{:S(2)}) collective-permute-start(bf16[512,512]{1,0:T(8,128)(2,1)} %get-tuple-element.109), channel_id=1, source_target_pairs={{0,12},{4,8},{8,4},{12,0},{16,28},{20,24},{24,20},{28,16},{1,13},{... | collective-permute-start | bytes 1572872 | tf_op jit(solution)/shard_map/ppermute | solution.py:22
  289.9 26.4 %collective-permute-start.33 = (bf16[384,256]{1,0:T(8,128)(2,1)S(1)}, bf16[384,256]{1,0:T(8,128)(2,1)S(1)}, u32[]{:S(2)}, u32[]{:S(2)}) collective-permute-start(bf16[384,256]{1,0:T(8,128)(2,1)S(1)} %get-tuple-element.145), channel_id=1, source_target_pairs={{0,20},{4,16},{8,28},{12,24},{16,4},{20,0},{24,12},{28,8},{1,21},{... | collective-permute-start | bytes 589832 | tf_op jit(solution)/shard_map/ppermute | solution.py:22
  291.3 30.1 %collective-permute-start.34 = (bf16[384,256]{1,0:T(8,128)(2,1)S(1)}, bf16[384,256]{1,0:T(8,128)(2,1)S(1)}, u32[]{:S(2)}, u32[]{:S(2)}) collective-permute-start(bf16[384,256]{1,0:T(8,128)(2,1)S(1)} %get-tuple-element.144), channel_id=1, source_target_pairs={{0,24},{4,28},{8,16},{12,20},{16,8},{20,12},{24,0},{28,4},{1,25},{... | collective-permute-start | bytes 589832 | tf_op jit(solution)/shard_map/ppermute | solution.py:22
  298.2 26.7 %collective-permute-start.35 = (bf16[384,256]{1,0:T(8,128)(2,1)S(1)}, bf16[384,256]{1,0:T(8,128)(2,1)S(1)}, u32[]{:S(2)}, u32[]{:S(2)}) collective-permute-start(bf16[384,256]{1,0:T(8,128)(2,1)S(1)} %get-tuple-element.143), channel_id=1, source_target_pairs={{0,28},{4,24},{8,20},{12,16},{16,12},{20,8},{24,4},{28,0},{1,29},{... | collective-permute-start | bytes 589832 | tf_op jit(solution)/shard_map/ppermute | solution.py:22
  (54 other events, 871.7 us)
Sparse Core Ops, SparseCore 0:
  43.7 10.5 all-gather.14
  69.5 13.8 all-gather.22
  84.9 13.2 all-gather.16
  124.7 12.7 all-gather.18
  138.9 13.2 all-gather.24
  173.7 14.5 all-gather.20
  189.8 13.2 all-gather.26

commit v3 on v2

--- a/solution.py
+++ b/solution.py
@@ -13,7 +13,6 @@
 EPS = 1e-05
 HIGHEST = lax.Precision.HIGHEST
 VMEM_LIMIT = 58 * 1024 * 1024
-OUT_VMEM = 58 * 1024 * 1024
 LANES = 128
 
 
@@ -23,16 +22,8 @@
 
 
 def silu_of(v):
-    return v * (1.0 / (1.0 + jnp.exp(-v)))
-
-
-def spread(columns, heads, width):
-    rows = columns.shape[0]
-    head_of = lax.broadcasted_iota(jnp.int32, (rows, heads * width), 1) // width
-    out = jnp.broadcast_to(columns[:, heads - 1 : heads], (rows, heads * width))
-    for j in range(heads - 2, -1, -1):
-        out = jnp.where(head_of == j, columns[:, j : j + 1], out)
-    return out
+    half = 0.5 * v
+    return half + half * jnp.tanh(half)
 
 
 def mixer_kernel(
@@ -40,12 +31,16 @@
     where_ref,
     *refs,
 ):
-    (shards, maps_of, blocks, rows, feats, krows, heads, width, state_size, taps, dim) = cfg
+    (shards, maps_of, parts, dt_rows, blocks, rows, feats, krows, heads, width, state_size, taps, dim) = cfg
     many = shards - 1
     gathered, last = refs[:many], refs[many : many + 2]
-    mains = refs[many + 2 : many + 2 + shards]
-    (map_a, map_b, dt_w, conv_w, conv_b, dt_bias, neg_rate, skip) = refs[many + 2 + shards : many + 10 + shards]
-    (out_ref, wbuf, xbuf, pbuf, pnext, cbuf, state, wsem, xsem) = refs[many + 10 + shards :]
+    at = many + 2
+    mains = []
+    for n in parts:
+        mains.append(refs[at : at + n])
+        at += n
+    (map_a, map_b, conv_w, conv_b, dt_bias, neg_rate, skip) = refs[at : at + 7]
+    (out_ref, wbuf, dt_all, dt_own, xbuf, pbuf, pnext, cbuf, state, wsem, dsem, xsem) = refs[at + 7 :]
     i = pl.program_id(0)
     steps = pl.num_programs(0)
     me_s, me_h = where_ref[0], where_ref[1]
@@ -54,7 +49,8 @@
     main_cols = 2 * chans
     map_cols = 2 * state_size
     per = feats // krows
-    dt_order = range(shards)
+    map_rows = krows + dt_rows * (krows // (2 * state_size))
+    me_q = me_s % (shards // 2)
 
     def move(copy, start):
         if start:
@@ -85,17 +81,19 @@
             block = kb // per
             place = ((block // 2) ^ (me_h // 2)) * 2 + (block % 2)
             row = pl.multiple_of(place * feats + (kb % per) * krows, krows)
-            source, lo_row = maps_of[d]
-            map_src = (map_a, map_b)[source].at[pl.ds(lo_row, krows), :]
-            for n, (src, lo, cols) in enumerate(
-                (
-                    (mains[d], 0, main_cols),
-                    (map_src, main_cols, map_cols),
-                    (dt_w.at[dt_order[d]], main_cols + map_cols, LANES),
-                )
-            ):
-                dst = wbuf.at[pl.ds(row, krows), pl.ds(lo, cols)]
+            source, place_row = maps_of[d]
+            map_src = (map_a, map_b)[source]
+            lo_row = place_row * map_rows
+            depth = krows // len(mains[d])
+            for n, src in enumerate(mains[d]):
+                dst = wbuf.at[pl.ds(row + n * depth, depth), pl.ds(0, main_cols)]
                 move(pltpu.make_async_copy(src, dst, wsem.at[n, d]), start)
+            dst = wbuf.at[pl.ds(row, krows), pl.ds(main_cols, map_cols)]
+            move(pltpu.make_async_copy(map_src.at[pl.ds(lo_row, krows), :], dst, wsem.at[2, d]), start)
+            for n in range(krows // map_cols):
+                src = map_src.at[pl.ds(lo_row + krows + n * dt_rows, dt_rows), :]
+                dst = dt_all.at[:, pl.ds(pl.multiple_of(row + n * map_cols, map_cols), map_cols)]
+                move(pltpu.make_async_copy(src, dst, dsem.at[n, d]), start)
 
     slot = lax.rem(i, 2)
     shard_count = steps - 1
@@ -114,6 +112,14 @@
     @pl.when(i == 0)
     def _():
         weights(False)
+        own_row = lax.broadcasted_iota(jnp.int32, (LANES, dt_rows), 0)
+        group_row = lax.broadcasted_iota(jnp.int32, (LANES, dt_rows), 1)
+        mine = (group_row == own_row + me_q * heads) & (own_row < heads)
+        pick = jnp.where(mine, 1.0, 0.0).astype(jnp.bfloat16)
+        for lo in range(0, dim, feats):
+            dt_own[:, lo : lo + feats] = jnp.dot(
+                pick, dt_all[:, lo : lo + feats], preferred_element_type=jnp.float32
+            ).astype(jnp.bfloat16)
 
     @pl.when(i < shard_count)
     def _():
@@ -133,49 +139,62 @@
 
     def project(tile, factor):
         lo, cols = tile
-        pnext[:, lo : lo + cols] = (
-            jnp.dot(xbuf[slot], wbuf[:, lo : lo + cols], preferred_element_type=jnp.float32) * factor
-        )
+        if lo < total - LANES:
+            part = jnp.dot(xbuf[slot], wbuf[:, lo : lo + cols], preferred_element_type=jnp.float32)
+        else:
+            part = lax.dot_general(
+                xbuf[slot], dt_own[...], (((1,), (1,)), ((), ())), preferred_element_type=jnp.float32
+            )
+        pnext[:, lo : lo + cols] = part * factor
 
     def hand_over():
-        pbuf[...] = pnext[...]
-        cbuf[8 : 8 + rows, :] = pnext[:, chans : chans + conv_cols].astype(jnp.bfloat16).astype(jnp.float32)
+        pbuf[:, :chans] = pnext[:, :chans]
+        pbuf[:, chans:] = pnext[:, total - LANES :]
+        cbuf[8 : 8 + rows, :] = pnext[:, chans : chans + conv_cols]
 
     def constants():
         tri = lax.broadcasted_iota(jnp.int32, (length, length), 0) >= lax.broadcasted_iota(
             jnp.int32, (length, length), 1
         )
         ones = jnp.where(tri, 1.0, 0.0).astype(jnp.float32)
-        lane_head = lax.broadcasted_iota(jnp.int32, (length, chans), 1) // width
-        return tri, ones, lane_head
-
-    def scan(st, tri, ones, lane_head):
+        row = lax.broadcasted_iota(jnp.int32, (2 * LANES, chans), 0) % LANES
+        lane = lax.broadcasted_iota(jnp.int32, (2 * LANES, chans), 1) // width
+        widen = jnp.where(row == lane, 1.0, 0.0).astype(jnp.bfloat16)
+        lane_head = lax.broadcasted_iota(jnp.int32, (1, chans), 1) // width
+        masks = [jnp.where(lane_head == j, 1.0, 0.0).astype(jnp.bfloat16) for j in range(heads)]
+        return tri, ones, widen, masks
+
+    def scan(st, tri, ones, widen, masks):
         r0 = st * length
         summed = conv_b[...]
         for k in range(taps):
             first = 8 - (taps - 1) + k + r0
             summed = summed + conv_w[k : k + 1, :] * cbuf[first : first + length, :]
         narrow = silu_of(summed).astype(jnp.bfloat16)
-        xin = narrow[:, :chans]
         in_map = narrow[:, chans : chans + state_size]
         out_map = narrow[:, chans + state_size :]
-        xf = xin.astype(jnp.float32)
-        raw = pbuf[r0 : r0 + length, total - LANES :] + dt_bias[...]
+        xf = narrow[:, :chans].astype(jnp.float32)
+        raw = pbuf[r0 : r0 + length, chans:] + dt_bias[...]
         step = jnp.maximum(raw, 0.0) + jnp.log1p(jnp.exp(-jnp.abs(raw)))
         logd = neg_rate[...] * step
         cum = jnp.dot(ones, logd, preferred_element_type=jnp.float32, precision=HIGHEST)
-        last_row = cum[length - 1 : length, :]
         cum_t = cum.T
-        step_t = step.T
+        columns = jnp.concatenate([jnp.exp(cum), step, jnp.exp(cum[length - 1 :, :] - cum)], axis=0)
+        high = columns.astype(jnp.bfloat16)
+        low = (columns - high.astype(jnp.float32)).astype(jnp.bfloat16)
+        wide = jnp.dot(jnp.concatenate([high, low], axis=1), widen, preferred_element_type=jnp.float32)
+        since, stepped, to_end = wide[:length], wide[length : 2 * length], wide[2 * length :]
         scores = lax.dot_general(
             out_map, in_map, (((1,), (1,)), ((), ())), preferred_element_type=jnp.float32
         )
+        scores = jnp.where(tri, scores, 0.0)
+        taken = xf * stepped
+        taken_low = taken.astype(jnp.bfloat16)
         weighted, spaced = [], []
         for j in range(heads):
-            gap = cum[:, j : j + 1] - cum_t[j : j + 1, :]
-            decay = jnp.where(tri, jnp.exp(jnp.where(tri, gap, 0.0)), 0.0)
-            weighted.append((scores * decay * step_t[j : j + 1, :]).astype(jnp.bfloat16))
-            spaced.append(jnp.where(lane_head == j, xf, 0.0).astype(jnp.bfloat16))
+            gap = jnp.minimum(cum[:, j : j + 1] - cum_t[j : j + 1, :], 0.0)
+            weighted.append((scores * jnp.exp(gap)).astype(jnp.bfloat16))
+            spaced.append(taken_low * masks[j])
         within = jnp.dot(
             jnp.concatenate(weighted, axis=1),
             jnp.concatenate(spaced, axis=0),
@@ -183,16 +202,12 @@
         )
         now = state[...]
         across = jnp.dot(out_map, now.astype(jnp.bfloat16), preferred_element_type=jnp.float32)
-        y = within + spread(jnp.exp(cum), heads, width) * across + skip[...] * xf
-        to_end = spread(jnp.exp(last_row - cum) * step, heads, width)
+        y = within + since * across + skip[...] * xf
         fresh = lax.dot_general(
-            in_map,
-            (xf * to_end).astype(jnp.bfloat16),
-            (((0,), (0,)), ((), ())),
-            preferred_element_type=jnp.float32,
-        )
-        state[...] = spread(jnp.exp(last_row), heads, width) * now + fresh
-        gate = pbuf[r0 : r0 + length, :chans].astype(jnp.bfloat16).astype(jnp.float32)
+            in_map, (taken * to_end).astype(jnp.bfloat16), (((0,), (0,)), ((), ())), preferred_element_type=jnp.float32
+        )
+        state[...] = since[length - 1 :, :] * now + fresh
+        gate = pbuf[r0 : r0 + length, :chans]
         out_ref[r0 : r0 + length, :] = (y * silu_of(gate)).astype(jnp.bfloat16)
 
     def keep_tail():
@@ -225,7 +240,7 @@
 
 
 def mixer(
-    where, gathered, last, mains, maps, maps_of, dt_w, conv_w, conv_b, dt_bias, neg_rate, skip, rows, heads, width, dim
+    where, gathered, last, mains, maps, maps_of, conv_w, conv_b, dt_bias, neg_rate, skip, rows, heads, width, dim
 ):
     shards = len(mains)
     feats = last[0].shape[1]
@@ -233,16 +248,19 @@
     krows = mains[0].shape[0]
     chans = heads * width
     state_size = maps[0].shape[1] // 2
+    parts = tuple(len(m) if isinstance(m, tuple) else 1 for m in mains)
+    dt_rows = heads * shards // 2
     taps = conv_w.shape[0]
     total = 2 * chans + 2 * state_size + LANES
-    cfg = (shards, tuple(maps_of), blocks, rows, feats, krows, heads, width, state_size, taps, dim)
+    cfg = (shards, tuple(maps_of), parts, dt_rows, blocks, rows, feats, krows, heads, width, state_size, taps, dim)
     hbm = pl.BlockSpec(memory_space=pl.ANY)
 
     def whole(a):
         return pl.BlockSpec(a.shape, lambda i, w: (0,) * a.ndim)
 
     small = (conv_w, conv_b, dt_bias, neg_rate, skip)
-    large = (*gathered, *last, *mains, *maps, dt_w)
+    flat_mains = [part for m in mains for part in (m if isinstance(m, tuple) else (m,))]
+    large = (*gathered, *last, *flat_mains, *maps)
     return pl.pallas_call(
         partial(mixer_kernel, cfg),
         out_shape=jax.ShapeDtypeStruct((rows * shards, chans), jnp.bfloat16),
@@ -252,13 +270,16 @@
             in_specs=[hbm] * len(large) + [whole(a) for a in small],
             out_specs=pl.BlockSpec((rows, chans), lambda i, w: (jnp.maximum(i - 1, 0), 0)),
             scratch_shapes=[
-                pltpu.VMEM((dim, total), jnp.bfloat16),
+                pltpu.VMEM((dim, total - LANES), jnp.bfloat16),
+                pltpu.VMEM((dt_rows, dim), jnp.bfloat16),
+                pltpu.VMEM((LANES, dim), jnp.bfloat16),
                 pltpu.VMEM((2, rows, dim), jnp.bfloat16),
-                pltpu.VMEM((rows, total), jnp.float32),
+                pltpu.VMEM((rows, chans + LANES), jnp.float32),
                 pltpu.VMEM((rows, total), jnp.float32),
                 pltpu.VMEM((8 + rows, chans + 2 * state_size), jnp.float32),
                 pltpu.VMEM((state_size, chans), jnp.float32),
-                pltpu.SemaphoreType.DMA((3, max(shards, blocks))),
+                pltpu.SemaphoreType.DMA((3, shards)),
+                pltpu.SemaphoreType.DMA((krows // (2 * state_size), shards)),
                 pltpu.SemaphoreType.DMA((2, blocks)),
             ],
         ),
@@ -269,15 +290,30 @@
     )(where, *large, *small)
 
 
-def normed_terms_kernel(cfg, where_ref, *refs):
-    shards, chans, groups = cfg
-    gated = refs[:shards]
-    gain, w_ref, out_ref, flat = refs[shards:]
+def terms_kernel(cfg, where_ref, *refs):
+    shards, chans, groups, order, keep = cfg
+    count = shards + 1 if keep else 1
+    values, w_hbm, outs = refs[:count], refs[count], refs[count + 1 : count + 1 + len(order)]
+    w_buf, sem = refs[-2], refs[-1]
+    flat = refs[count + 1 + len(order)] if keep else values[0]
+    depth, feats = w_buf.shape[1:]
+    chunks = sem.shape[1]
+    part_rows = depth // chunks
     me_s = where_ref[0]
-    per = shards // groups
-
-    @pl.when(pl.program_id(0) == 0)
-    def _():
+
+    def copy(block, n):
+        part = pl.ds(n * part_rows, part_rows)
+        lane = pl.multiple_of((where_ref[1] ^ order[block]) * feats, feats)
+        return pltpu.make_async_copy(
+            w_hbm.at[part, pl.ds(lane, feats)], w_buf.at[block, part, :], sem.at[block, n]
+        )
+
+    for block in range(len(order)):
+        for n in range(chunks):
+            copy(block, n).start()
+    if keep:
+        gated, gain = values[:shards], values[shards]
+        per = shards // groups
         for g in range(groups):
             squares = 0.0
             parts = []
@@ -290,37 +326,37 @@
                 t = me_s ^ d
                 value = (part * factor * gain[pl.ds(t, 1), :]).astype(jnp.bfloat16)
                 flat[:, pl.ds(pl.multiple_of(t * chans, chans), chans)] = value
-
-    out_ref[...] = jnp.dot(flat[...], w_ref[...], preferred_element_type=jnp.float32).astype(jnp.bfloat16)
-
-
-def terms_kernel(where_ref, flat, w_ref, out_ref):
-    out_ref[...] = jnp.dot(flat[...], w_ref[...], preferred_element_type=jnp.float32).astype(jnp.bfloat16)
-
-
-def out_terms(kernel, where, values, w_flat, rows, blocks, e, keep):
+    for block, out_ref in enumerate(outs):
+        for n in range(chunks):
+            copy(block, n).wait()
+        for lo in range(0, feats, 256):
+            cols = min(256, feats - lo)
+            out_ref[:, lo : lo + cols] = jnp.dot(
+                flat[...], w_buf[block, :, lo : lo + cols], preferred_element_type=jnp.float32
+            ).astype(jnp.bfloat16)
+
+
+def out_terms(where, values, w_flat, shape, order, keep):
+    shards, groups, rows, chans, blocks = shape
     depth, dim = w_flat.shape
     feats = dim // blocks
-    tile = min(256, feats)
-    tiles = feats // tile
-    out_shape = jax.ShapeDtypeStruct((rows, feats), jnp.bfloat16)
-    out_spec = pl.BlockSpec((rows, tile), lambda i, w: (0, i))
-    if keep:
-        out_shape = (out_shape, jax.ShapeDtypeStruct((rows, depth), jnp.bfloat16))
-        out_spec = (out_spec, pl.BlockSpec((rows, depth), lambda i, w: (0, 0)))
+    vmem = pl.BlockSpec(memory_space=pltpu.VMEM)
+    widths = [feats] * len(order) + ([depth] if keep else [])
+    out_shape = tuple(jax.ShapeDtypeStruct((rows, n), jnp.bfloat16) for n in widths)
     return pl.pallas_call(
-        kernel,
+        partial(terms_kernel, (shards, chans, groups, order, keep)),
         out_shape=out_shape,
-        grid_spec=pltpu.PrefetchScalarGridSpec(
-            num_scalar_prefetch=1,
-            grid=(tiles,),
-            in_specs=[pl.BlockSpec(v.shape, lambda i, w: (0, 0)) for v in values]
-            + [pl.BlockSpec((depth, tile), lambda i, w: (0, (w[1] ^ e) * tiles + i))],
-            out_specs=out_spec,
-        ),
-        compiler_params=pltpu.CompilerParams(vmem_limit_bytes=OUT_VMEM, dimension_semantics=("arbitrary",)),
+        in_specs=[pl.BlockSpec(memory_space=pltpu.SMEM)] + [vmem] * len(values) + [pl.BlockSpec(memory_space=pl.ANY)],
+        out_specs=(vmem,) * len(widths),
+        scratch_shapes=[
+            pltpu.VMEM((len(order), depth, feats), jnp.bfloat16),
+            pltpu.SemaphoreType.DMA((len(order), 8)),
+        ],
+        compiler_params=pltpu.CompilerParams(vmem_limit_bytes=VMEM_LIMIT),
         cost_estimate=pl.CostEstimate(
-            flops=2 * rows * depth * feats, bytes_accessed=2 * depth * feats, transcendentals=0
+            flops=rows * feats,
+            bytes_accessed=rows * feats,
+            transcendentals=0,
         ),
     )(where, *values, w_flat)
 
@@ -342,7 +378,7 @@
     return lax.optimization_barrier(values)
 
 
-def exchange(tokens, main, far_map, own_map, dt_rows):
+def exchange(tokens, w_in, weights_of):
     at = lax.axis_index("seq") // 2
     middle = (at == 1) | (at == 2)
     cross, outward = [(1, 2), (2, 1)], [(1, 0), (2, 3)]
@@ -353,56 +389,53 @@
     def s_swap(v, bit):
         return swap(v, "seq", bit)
 
-    xp, y0, z1, c0, dt_y, main, far_map, own_map = together(
+    xp, y0, z1, c0, (m1, m7, far_map), w_in = together(
         x_swap(tokens),
         s_swap(tokens, 1),
         s_swap(tokens, 2),
         line(tokens, cross),
-        s_swap(dt_rows, 1),
-        main,
-        far_map,
-        own_map,
-    )
-    dt_rows = stack(dt_rows, dt_y)
-    xy, yz1, c1, o0, dt_z = together(
-        x_swap(y0), s_swap(z1, 1), line(z1, cross), line(c0, outward), s_swap(dt_rows, 2)
-    )
-    dt_rows = stack(dt_rows, dt_z)
+        weights_of(w_in, (1, 7, "far")),
+        w_in,
+    )
+    xy, yz1, c1, o0, (m2, m6, m5, m4, m3, m0, own_map) = together(
+        x_swap(y0),
+        s_swap(z1, 1),
+        line(z1, cross),
+        line(c0, outward),
+        weights_of(w_in, (2, 6, 5, 4, 3, 0, "own")),
+    )
     q1 = jnp.where(middle, c0, o0)
-    q1, z1, yz1, c1, far_map, dt_rows, m7 = together(q1, z1, yz1, c1, far_map, dt_rows, main[7])
+    q1, z1, yz1, c1, m7, far_map = together(q1, z1, yz1, c1, m7, far_map)
     a1 = stack(z1, yz1)
-    xa1, w7, yq1, o1, far_map, dt_far = together(
-        x_swap(a1), s_swap(m7, 7), s_swap(q1, 1), line(c1, outward), s_swap(far_map, 4), s_swap(dt_rows, 4)
+    xa1, w7, yq1, o1, far_map = together(
+        x_swap(a1), s_swap(m7, 7), s_swap(q1, 1), line(c1, outward), s_swap(far_map, 4)
     )
     own = [stack(tokens, y0), a1]
     across = [stack(xp, xy), xa1]
-    dt_rows = stack(dt_rows, dt_far)
     q2 = jnp.where(middle, c1, o1)
     a2 = stack(q1, yq1)
     maps = stack(own_map, far_map)
-    half = main[6].shape[0] // 2
-    q2, a2, maps, m5, m6, m1 = together(q2, a2, maps, main[5], main[6][:half], main[1])
-    xa2, w6a, w5, yq2, maps_z, w1 = together(
-        x_swap(a2), s_swap(m6, 6), s_swap(m5, 5), s_swap(q2, 1), s_swap(maps, 2), s_swap(m1, 1)
+    half = m6.shape[0] // 2
+    q2, a2, maps, m5, m6a, m6b = together(q2, a2, maps, m5, m6[:half], m6[half:])
+    xa2, w5, w6a, yq2, maps_z = together(
+        x_swap(a2), s_swap(m5, 5), s_swap(m6a, 6), s_swap(q2, 1), s_swap(maps, 2)
     )
     a3 = stack(q2, yq2)
-    a3, maps, maps_z, m4, m6, m3, m2 = together(
-        a3, maps, maps_z, main[4], main[6][half:], main[3], main[2]
-    )
     maps = stack(maps, maps_z)
-    xa3, w4, maps_y, w6b, w3, w2 = together(
-        x_swap(a3), s_swap(m4, 4), s_swap(maps, 1), s_swap(m6, 6), s_swap(m3, 3), s_swap(m2, 2)
+    a3, maps, m4, m6b, m3 = together(a3, maps, m4, m6b, m3)
+    xa3, w4, w6b, maps_y, w3 = together(
+        x_swap(a3), s_swap(m4, 4), s_swap(m6b, 6), s_swap(maps, 1), s_swap(m3, 3)
     )
     own += [a2, a3]
     across += [xa2]
     gathered = [both_cores(v) for v in own + across]
+    m1, m2, xa3, w3 = together(m1, m2, xa3, w3)
+    w1, w2 = s_swap(m1, 1), s_swap(m2, 2)
     last = (xa3, swap(xa3, "head", 1))
-    mains = [main[0], w1, w2, w3, w4, w5, stack(w6a, w6b), w7]
-    krows = far_map.shape[0]
-    place = {0: (maps, 0), 4: (maps, 1), 2: (maps, 2), 6: (maps, 3)}
-    place.update({d | 1: (maps_y, n) for d, (_, n) in list(place.items())})
-    maps_of = [(0 if place[d][0] is maps else 1, place[d][1] * krows) for d in range(8)]
-    return gathered, last, mains, (maps, maps_y), maps_of, dt_rows
+    mains = [m0, w1, w2, w3, w4, w5, (w6a, w6b), w7]
+    place = {0: 0, 4: 1, 2: 2, 6: 3}
+    maps_of = [(d & 1, place[d & ~1]) for d in range(8)]
+    return gathered, last, mains, (maps, maps_y), maps_of
 
 
 def piece_table(shards):
@@ -432,23 +465,30 @@
 
     gain = lax.dynamic_slice_in_dim(norm_gain, s * krows, krows, 0)
 
-    def columns(t, first, count):
-        part = lax.dynamic_slice(w_in, (0, t // per, first), (krows, 1, count))[:, 0]
-        return (part.astype(jnp.float32) * gain[:, None]).astype(jnp.bfloat16)
-
-    main = []
-    for d in range(shards):
-        t = s ^ d
-        first = (t % per) * chans
-        main.append(
-            jnp.concatenate([columns(t, first, chans), columns(t, group_width + first, chans)], axis=1)
-        )
-    far_map = columns(s ^ per, 2 * group_width, 2 * state_size)
-    own_map = columns(s, 2 * group_width, 2 * state_size)
-    dt_rows = (w_dt.T.astype(jnp.float32) * gain[None, :]).astype(jnp.bfloat16)
-    gathered, last, mains, maps, maps_of, dt_rows = exchange(tokens, main, far_map, own_map, dt_rows)
-    dt_rows = lax.dynamic_slice_in_dim(dt_rows.reshape(shards, local_heads, krows), s * heads, heads, 1)
-    dt_w = jnp.pad(jnp.swapaxes(dt_rows, 1, 2), ((0, 0), (0, 0), (0, LANES - heads)))
+    dt_cols = local_heads // groups
+
+    def weights_of(w_in, names):
+        def columns(t, first, count):
+            part = lax.dynamic_slice(w_in, (0, t // per, first), (krows, 1, count))[:, 0]
+            return (part.astype(jnp.float32) * gain[:, None]).astype(jnp.bfloat16)
+
+        def one(name):
+            if name in ("far", "own"):
+                t = s ^ per if name == "far" else s
+                dt = lax.dynamic_slice_in_dim(w_dt, (t // per) * dt_cols, dt_cols, 1).T
+                dt = (dt.astype(jnp.float32) * gain[None, :]).astype(jnp.bfloat16)
+                cols = 2 * state_size
+                rows_of_dt = [dt[:, lo : lo + cols] for lo in range(0, krows, cols)]
+                return jnp.concatenate([columns(t, 2 * group_width, cols), *rows_of_dt], axis=0)
+            t = s ^ name
+            first = (t % per) * chans
+            return jnp.concatenate(
+                [columns(t, first, chans), columns(t, group_width + first, chans)], axis=1
+            )
+
+        return tuple(one(name) for name in names)
+
+    gathered, last, mains, maps, maps_of = exchange(tokens, w_in, weights_of)
 
     group = s // per
     quarter = (s % per) * chans
@@ -472,7 +512,6 @@
         mains,
         maps,
         maps_of,
-        dt_w,
         own_channels(conv_w),
         own_channels(conv_b)[None, :],
         lanes(own_heads(dt_bias)),
@@ -493,15 +532,15 @@
     gains = gate_gain.reshape(shards, chans)
     w_flat = w_out.reshape(groups * group_width, w_out.shape[2])
     wide = jnp.float32
-    first, flat = out_terms(
-        partial(normed_terms_kernel, (shards, chans, groups)), where, [*arrived, gains], w_flat, rows, blocks, 3, True
-    )
+    shape = (shards, groups, rows, chans, blocks)
+    shape = (shards, groups, rows, chans, blocks)
+    first, flat = out_terms(where, [*arrived, gains], w_flat, shape, (3,), True)
     via_core = swap(first, "head", 1)
-    second = out_terms(terms_kernel, where, [flat], w_flat, rows, blocks, 2, False)
-    beyond = swap((second.astype(wide) + via_core.astype(wide)).astype(jnp.bfloat16), "head", 2)
-    third = out_terms(terms_kernel, where, [flat], w_flat, rows, blocks, 1, False)
+    (second,) = out_terms(where, [flat], w_flat, shape, (2,), False)
+    to_pair, flat = together((second.astype(wide) + via_core.astype(wide)).astype(jnp.bfloat16), flat)
+    beyond = swap(to_pair, "head", 2)
+    third, own = out_terms(where, [flat], w_flat, shape, (1, 0), False)
     from_core = swap(third, "head", 1)
-    own = out_terms(terms_kernel, where, [flat], w_flat, rows, blocks, 0, False)
     return (own.astype(wide) + from_core.astype(wide) + beyond.astype(wide)).astype(jnp.bfloat16)
 
 

time: 377 us -> 357 us (0.947)
  local copies, waits for them, and re-layouts: 36.5 us -> 25.2 us
  Pallas kernels: 78.6 us -> 73.8 us
  starting transfers between devices: 54.1 us -> 49.6 us
    dynamic_slice x2 -> x1, local copies, waits for them, and re-layouts: 17.6 us -> 5.88 us  [columns(): lax.dynamic_slice(w_in, (0, t // per, first), (krows, 1, count))[:, 0]]
    ppermute x35 -> x32, waiting for transfers between devices: 167 us -> 158 us  [swap(): return lax.ppermute(value, axis, [(i, i ^ bit) for i in range(count)])]
    ppermute x4, waiting for transfers between devices: 0.01 us -> 8.32 us  [line(): lax.ppermute(value, 'seq', [(2 * a + y, 2 * b + y) for a, b in pairs for...]
    ppermute x35 -> x32, starting transfers between devices: 41.4 us -> 34.2 us  [swap(): return lax.ppermute(value, axis, [(i, i ^ bit) for i in range(count)])]
    pallas_call x4 -> x3, Pallas kernels: 26.2 us -> 21.3 us  [out_terms(): pl.pallas_call(partial(terms_kernel, (shards, chans, groups, order, keep)...]
    unnamed x85 -> x69, local copies, waits for them, and re-layouts: 10.8 us -> 7.83 us
    concatenate x9 -> x6, other arithmetic: 12.4 us -> 10.2 us  [stack(): return jnp.concatenate(parts, axis=0)]
  transfers between devices with their start and end apart: 46 -> 43, of which waited for: 17 -> 22; matrix products, arithmetic and copies ran while one was open for 12% -> 10% of each run, Pallas kernels for 5% -> 2%
where the time goes in v3:
time: 357 us; the launch traced here: 356 us
  waiting for transfers between devices  167 us (47%)
  Pallas kernels  73.8 us (21%)
  starting transfers between devices  49.6 us (14%)
  other arithmetic  26.4 us (7%)
  local copies, waits for them, and re-layouts  25.2 us (7%)
  between operations  14.3 us (4%)
    ppermute x32, waiting for transfers between devices, swap(): return lax.ppermute(value, axis, [(i, i ^ bit) for i in range(count)])  158 us
    pallas_call x1, Pallas kernels, mixer(): pl.pallas_call(partial(mixer_kernel, cfg), out_shape=jax.ShapeDtypeStruct...  52.5 us
    ppermute x32, starting transfers between devices, swap(): return lax.ppermute(value, axis, [(i, i ^ bit) for i in range(count)])  34.2 us
    pallas_call x3, Pallas kernels, out_terms(): pl.pallas_call(partial(terms_kernel, (shards, chans, groups, order, keep)...  21.3 us
    ppermute x4, starting transfers between devices, line(): lax.ppermute(value, 'seq', [(2 * a + y, 2 * b + y) for a, b in pairs for...  14.9 us
    concatenate x6, other arithmetic, stack(): return jnp.concatenate(parts, axis=0)  10.2 us
    ppermute x4, waiting for transfers between devices, line(): lax.ppermute(value, 'seq', [(2 * a + y, 2 * b + y) for a, b in pairs for...  8.32 us
    unnamed x69, local copies, waits for them, and re-layouts  7.83 us
  transfers between devices with their start and end apart: 43, of which 22 were waited for; matrix products, arithmetic and copies ran while one was open for 10% of the time, Pallas kernels for 2%

profile of v3, /device:TPU:8, one launch (start us, length us, event | category | flops | bytes accessed | tf_op | source)
XLA Modules:
  0.0 356.4 jit_solution(13684682167824226707)
XLA Ops:
  10.0 4.6 %collective-permute-start.3 = (bf16[384,1024]{1,0:T(8,128)(2,1)}, bf16[384,1024]{1,0:T(8,128)(2,1)}, u32[]{:S(2)}, u32[]{:S(2)}) collective-permute-start(bf16[384,1024]{1,0:T(8,128)(2,1)} %param.11), channel_id=1, source_target_pairs={{8,16},{12,20},{16,8},{20,12},{9,17},{13,21},{17,9},{21,13},{10,18... | collective-permute-start | bytes 2359304 | tf_op jit(solution)/shard_map/ppermute | solution.py:365
  16.3 5.9 %constant_dynamic-slice_fusion.10 = (bf16[512,1,256]{2,1,0:T(2,128)(2,1)S(1)}, bf16[512,1,256]{2,1,0:T(2,128)(2,1)S(1)}, bf16[512,1,256]{2,1,0:T(2,128)(2,1)S(1)...) fusion(bf16[512,2,2304]{2,1,0:T(2,128)(2,1)} %param.13, s32[]{:T(128)S(6)} %select_n.248, s32[]{:T(128)S(6)} %select_n.243, ...), kind=kLoop, calls=%fused_computation.77 | loop fusion | bytes 2621468 | tf_op jit(solution)/shard_map/dynamic_slice | solution.py:472
  23.5 2.5 collective-permute-done
  28.6 3.0 collective-permute-done.3
  31.6 2.6 pad_maximum_fusion
  35.6 3.6 %collective-permute-start.6 = (bf16[384,1024]{1,0:T(8,128)(2,1)}, bf16[384,1024]{1,0:T(8,128)(2,1)}, u32[]{:S(2)}, u32[]{:S(2)}) collective-permute-start(bf16[384,1024]{1,0:T(8,128)(2,1)} %collective-permute-done.2), channel_id=1, source_target_pairs={{8,16},{12,20},{16,8},{20,12},{9,17},{13,21},{17,9},{21,13},{10,18... | collective-permute-start | bytes 2359304 | tf_op jit(solution)/shard_map/ppermute | solution.py:365
  39.3 3.5 copy.35
  42.8 2.2 collective-permute-start.7
  50.3 2.3 collective-permute-done.4
  55.0 3.2 collective-permute-done.7
  67.6 4.4 %collective-permute-start.11 = (bf16[384,1024]{1,0:T(8,128)(2,1)}, bf16[384,1024]{1,0:T(8,128)(2,1)S(1)}, u32[]{:S(2)}, u32[]{:S(2)}) collective-permute-start(bf16[384,1024]{1,0:T(8,128)(2,1)} %collective-permute-done.6), channel_id=1, source_target_pairs={{8,0},{12,4},{16,24},{20,28},{9,1},{13,5},{17,25},{21,29},{10,2},{... | collective-permute-start | bytes 2359304 | tf_op jit(solution)/shard_map/ppermute | solution.py:365
  74.6 28.2 %collective-permute-done.12 = bf16[544,256]{1,0:T(8,128)(2,1)S(1)} collective-permute-done((bf16[544,256]{1,0:T(8,128)(2,1)S(1)}, bf16[544,256]{1,0:T(8,128)(2,1)S(1)}, u32[]{:S(2)}, u32[]{:S(2)}) %collective-permute-start.12) | collective-permute-done | bytes 278560 | tf_op jit(solution)/shard_map/ppermute | solution.py:21
  103.6 2.5 pad_maximum_fusion.1
  114.3 33.6 %collective-permute-done.15.refs_15_ = bf16[256,512]{1,0:T(8,128)(2,1)S(1)} collective-permute-done((bf16[256,512]{1,0:T(8,128)(2,1)}, bf16[256,512]{1,0:T(8,128)(2,1)S(1)}, u32[]{:S(2)}, u32[]{:S(2)}) %collective-permute-start.15) | collective-permute-done | bytes 262176 | tf_op jit(solution)/shard_map/ppermute | solution.py:21
  149.0 2.5 pad_maximum_fusion.2
  156.2 2.4 collective-permute-start.22
  159.7 30.0 %collective-permute-done.20.refs_16_ = bf16[256,512]{1,0:T(8,128)(2,1)S(1)} collective-permute-done((bf16[256,512]{1,0:T(8,128)(2,1)S(1)}, bf16[256,512]{1,0:T(8,128)(2,1)S(1)}, u32[]{:S(2)}, u32[]{:S(2)}) %collective-permute-start.20) | collective-permute-done | bytes 262176 | tf_op jit(solution)/shard_map/ppermute | solution.py:21
  198.1 9.8 %collective-permute-done.24.refs_10_ = bf16[512,512]{1,0:T(8,128)(2,1)S(1)} collective-permute-done((bf16[512,512]{1,0:T(8,128)(2,1)}, bf16[512,512]{1,0:T(8,128)(2,1)S(1)}, u32[]{:S(2)}, u32[]{:S(2)}) %collective-permute-start.24) | collective-permute-done | bytes 524320 | tf_op jit(solution)/shard_map/ppermute | solution.py:21
  210.2 52.5 %shard_map.109 = bf16[3072,256]{1,0:T(8,128)(2,1)} custom-call(s32[10]{0:T(128)} %pad_add_fusion.where_ref, bf16[2,768,1024]{2,1,0:T(8,128)(2,1)} %bitcast.99, bf16[2,768,1024]{2,1,0:T(8,128)(2,1)} %bitcast.101, bf16[2,768,1024]{2,1,0:T(8,128)(2,1)} %bitcast.102, bf16[2,768,1024]{2,1,0:T(8,128)(2,1)} %bitcast.104, bf16[2,768,1024]{2,1,0:T(8,128)(2,1)} %bitcast.100, ...), custom_call_target="tpu_custom_call" | custom-call | flops 22548578304 | bytes 25165824 | tf_op jit(solution)/shard_map/pallas_call | solution.py:264
  262.8 2.3 constant_dynamic-slice_fusion
  265.8 2.7 collective-permute-start.28
  269.1 2.5 collective-permute-start.30
  272.8 4.7 %collective-permute-done.27.refs_2_ = bf16[384,256]{1,0:T(8,128)(2,1)S(1)} collective-permute-done((bf16[384,256]{1,0:T(8,128)(2,1)S(1)}, bf16[384,256]{1,0:T(8,128)(2,1)S(1)}, u32[]{:S(2)}, u32[]{:S(2)}) %collective-permute-start.27) | collective-permute-done | bytes 196640 | tf_op jit(solution)/shard_map/ppermute | solution.py:21
  277.6 2.5 collective-permute-start.32
  282.3 13.1 %collective-permute-done.30.refs_5_ = bf16[384,256]{1,0:T(8,128)(2,1)S(1)} collective-permute-done((bf16[384,256]{1,0:T(8,128)(2,1)S(1)}, bf16[384,256]{1,0:T(8,128)(2,1)S(1)}, u32[]{:S(2)}, u32[]{:S(2)}) %collective-permute-start.30) | collective-permute-done | bytes 196640 | tf_op jit(solution)/shard_map/ppermute | solution.py:21
  295.4 5.9 %collective-permute-done.31.refs_6_ = bf16[384,256]{1,0:T(8,128)(2,1)S(1)} collective-permute-done((bf16[384,256]{1,0:T(8,128)(2,1)S(1)}, bf16[384,256]{1,0:T(8,128)(2,1)S(1)}, u32[]{:S(2)}, u32[]{:S(2)}) %collective-permute-start.31) | collective-permute-done | bytes 196640 | tf_op jit(solution)/shard_map/ppermute | solution.py:21
  301.3 2.2 collective-permute-done.32.refs_7_
  304.3 6.8 %shard_map.110 = (bf16[384,1024]{1,0:T(8,128)(2,1)}, bf16[384,2048]{1,0:T(8,128)(2,1)}) custom-call(s32[10]{0:T(128)} %pad_add_fusion.where_ref, bf16[384,256]{1,0:T(8,128)(2,1)} %get-tuple-element.151.refs_0_, bf16[384,256]{1,0:T(8,128)(2,1)} %copy-done.13, bf16[384,256]{1,0:T(8,128)(2,1)} %copy-done.14, bf16[384,256]{1,0:T(8,128)(2,1)} %copy-done.15, ...), custom_call_target="tpu_custom_call" | custom-call | flops 393216 | bytes 393216 | tf_op jit(solution)/shard_map/pallas_call | solution.py:346
  311.2 6.3 %shard_map.111 = bf16[384,1024]{1,0:T(8,128)(2,1)} custom-call(s32[10]{0:T(128)} %pad_add_fusion.where_ref, bf16[384,2048]{1,0:T(8,128)(2,1)} %get-tuple-element.123.refs_0_, bf16[2048,4096]{1,0:T(8,128)(2,1)} %bitcast.92), custom_call_target="tpu_custom_call" | custom-call | flops 393216 | bytes 393216 | tf_op jit(solution)/shard_map/pallas_call | solution.py:346
  318.9 8.2 %shard_map.112 = (bf16[384,1024]{1,0:T(8,128)(2,1)}, bf16[384,1024]{1,0:T(8,128)(2,1)}) custom-call(s32[10]{0:T(128)} %pad_add_fusion.where_ref, bf16[384,2048]{1,0:T(8,128)(2,1)} %get-tuple-element.123.refs_0_, bf16[2048,4096]{1,0:T(8,128)(2,1)} %bitcast.93), custom_call_target="tpu_custom_call" | custom-call | flops 393216 | bytes 393216 | tf_op jit(solution)/shard_map/pallas_call | solution.py:346
  329.8 17.4 %collective-permute-done.35 = bf16[384,1024]{1,0:T(8,128)(2,1)S(1)} collective-permute-done((bf16[384,1024]{1,0:T(8,128)(2,1)S(1)}, bf16[384,1024]{1,0:T(8,128)(2,1)S(1)}, u32[]{:S(2)}, u32[]{:S(2)}) %collective-permute-start.35) | collective-permute-done | bytes 786464 | tf_op jit(solution)/shard_map/ppermute | solution.py:21
  347.2 2.3 add_convert_fusion
  (179 shorter events, 65.7 us)
Async XLA Ops:
  6.5 191.5 %all-gather.15.cloned.1.call-start = ((), (), s32[]{:S(2)}) async-start(), calls=%async_computation | async-start | bytes 4718592 | tf_op jit(solution)/shard_map/all_gather | solution.py:374
  6.5 19.5 %collective-permute-start = (bf16[384,1024]{1,0:T(8,128)(2,1)}, bf16[384,1024]{1,0:T(8,128)(2,1)S(1)}, u32[]{:S(2)}, u32[]{:S(2)}) collective-permute-start(bf16[384,1024]{1,0:T(8,128)(2,1)} %param.11), channel_id=1, source_target_pairs={{0,2},{1,3},{2,0},{3,1},{4,6},{5,7},{6,4},{7,5},{8,10},{9,11},{10,... | collective-permute-start | bytes 2359304 | tf_op jit(solution)/shard_map/ppermute | solution.py:21
  8.0 19.3 %collective-permute-start.1 = (bf16[384,1024]{1,0:T(8,128)(2,1)}, bf16[384,1024]{1,0:T(8,128)(2,1)}, u32[]{:S(2)}, u32[]{:S(2)}) collective-permute-start(bf16[384,1024]{1,0:T(8,128)(2,1)} %param.11), channel_id=1, source_target_pairs={{0,4},{4,0},{8,12},{12,8},{16,20},{20,16},{24,28},{28,24},{1,5},{5... | collective-permute-start | bytes 2359304 | tf_op jit(solution)/shard_map/ppermute | solution.py:21
  9.6 19.0 %collective-permute-start.2 = (bf16[384,1024]{1,0:T(8,128)(2,1)}, bf16[384,1024]{1,0:T(8,128)(2,1)}, u32[]{:S(2)}, u32[]{:S(2)}) collective-permute-start(bf16[384,1024]{1,0:T(8,128)(2,1)} %param.11), channel_id=1, source_target_pairs={{0,8},{4,12},{8,0},{12,4},{16,24},{20,28},{24,16},{28,20},{1,9},{5... | collective-permute-start | bytes 2359304 | tf_op jit(solution)/shard_map/ppermute | solution.py:21
  10.0 21.6 %collective-permute-start.3 = (bf16[384,1024]{1,0:T(8,128)(2,1)}, bf16[384,1024]{1,0:T(8,128)(2,1)}, u32[]{:S(2)}, u32[]{:S(2)}) collective-permute-start(bf16[384,1024]{1,0:T(8,128)(2,1)} %param.11), channel_id=1, source_target_pairs={{8,16},{12,20},{16,8},{20,12},{9,17},{13,21},{17,9},{21,13},{10,18... | collective-permute-start | bytes 2359304 | tf_op jit(solution)/shard_map/ppermute | solution.py:365
  34.2 163.8 %all-gather.23.cloned.1.call-start = ((), (), s32[]{:S(2)}) async-start(), calls=%async_computation.4 | async-start | bytes 4718592 | tf_op jit(solution)/shard_map/all_gather | solution.py:374
  34.5 18.1 %collective-permute-start.4 = (bf16[384,1024]{1,0:T(8,128)(2,1)}, bf16[384,1024]{1,0:T(8,128)(2,1)S(1)}, u32[]{:S(2)}, u32[]{:S(2)}) collective-permute-start(bf16[384,1024]{1,0:T(8,128)(2,1)} %collective-permute-done.1), channel_id=1, source_target_pairs={{0,2},{1,3},{2,0},{3,1},{4,6},{5,7},{6,4},{7,5},{8,10},{9,11},{10,... | collective-permute-start | bytes 2359304 | tf_op jit(solution)/shard_map/ppermute | solution.py:21
  35.6 19.4 %collective-permute-start.6 = (bf16[384,1024]{1,0:T(8,128)(2,1)}, bf16[384,1024]{1,0:T(8,128)(2,1)}, u32[]{:S(2)}, u32[]{:S(2)}) collective-permute-start(bf16[384,1024]{1,0:T(8,128)(2,1)} %collective-permute-done.2), channel_id=1, source_target_pairs={{8,16},{12,20},{16,8},{20,12},{9,17},{13,21},{17,9},{21,13},{10,18... | collective-permute-start | bytes 2359304 | tf_op jit(solution)/shard_map/ppermute | solution.py:365
  59.7 138.4 %all-gather.17.cloned.1.call-start = ((), (), s32[]{:S(2)}) async-start(), calls=%async_computation.1 | async-start | bytes 4718592 | tf_op jit(solution)/shard_map/all_gather | solution.py:374
  64.5 133.6 %all-gather.19.cloned.1.call-start = ((), (), s32[]{:S(2)}) async-start(), calls=%async_computation.2 | async-start | bytes 4718592 | tf_op jit(solution)/shard_map/all_gather | solution.py:374
  64.5 39.1 %collective-permute-start.8 = (bf16[768,1024]{1,0:T(8,128)(2,1)}, bf16[768,1024]{1,0:T(8,128)(2,1)}, u32[]{:S(2)}, u32[]{:S(2)}) collective-permute-start(bf16[768,1024]{1,0:T(8,128)(2,1)} %copy-done.4), channel_id=1, source_target_pairs={{0,2},{1,3},{2,0},{3,1},{4,6},{5,7},{6,4},{7,5},{8,10},{9,11},{10,... | collective-permute-start | bytes 4718600 | tf_op jit(solution)/shard_map/ppermute | solution.py:21
  66.1 36.7 %collective-permute-start.10 = (bf16[384,1024]{1,0:T(8,128)(2,1)S(1)}, bf16[384,1024]{1,0:T(8,128)(2,1)}, u32[]{:S(2)}, u32[]{:S(2)}) collective-permute-start(bf16[384,1024]{1,0:T(8,128)(2,1)S(1)} %broadcast_select_fusion.1), channel_id=1, source_target_pairs={{0,4},{4,0},{8,12},{12,8},{16,20},{20,16},{24,28},{28,24},{1,5},{5... | collective-permute-start | bytes 2359304 | tf_op jit(solution)/shard_map/ppermute | solution.py:21
  67.6 35.2 %collective-permute-start.11 = (bf16[384,1024]{1,0:T(8,128)(2,1)}, bf16[384,1024]{1,0:T(8,128)(2,1)S(1)}, u32[]{:S(2)}, u32[]{:S(2)}) collective-permute-start(bf16[384,1024]{1,0:T(8,128)(2,1)} %collective-permute-done.6), channel_id=1, source_target_pairs={{8,0},{12,4},{16,24},{20,28},{9,1},{13,5},{17,25},{21,29},{10,2},{... | collective-permute-start | bytes 2359304 | tf_op jit(solution)/shard_map/ppermute | solution.py:365
  72.1 30.8 %collective-permute-start.9 = (bf16[512,512]{1,0:T(8,128)(2,1)}, bf16[512,512]{1,0:T(8,128)(2,1)S(1)}, u32[]{:S(2)}, u32[]{:S(2)}) collective-permute-start(bf16[512,512]{1,0:T(8,128)(2,1)} %get-tuple-element.78), channel_id=1, source_target_pairs={{0,28},{4,24},{8,20},{12,16},{16,12},{20,8},{24,4},{28,0},{1,29},{... | collective-permute-start | bytes 1572872 | tf_op jit(solution)/shard_map/ppermute | solution.py:21
  72.6 30.2 %collective-permute-start.12 = (bf16[544,256]{1,0:T(8,128)(2,1)S(1)}, bf16[544,256]{1,0:T(8,128)(2,1)S(1)}, u32[]{:S(2)}, u32[]{:S(2)}) collective-permute-start(bf16[544,256]{1,0:T(8,128)(2,1)S(1)} %pad_maximum_fusion.14), channel_id=1, source_target_pairs={{0,16},{4,20},{8,24},{12,28},{16,0},{20,4},{24,8},{28,12},{1,17},{... | collective-permute-start | bytes 835592 | tf_op jit(solution)/shard_map/ppermute | solution.py:21
  107.4 90.7 %all-gather.25.cloned.1.call-start = ((), (), s32[]{:S(2)}) async-start(), calls=%async_computation.5 | async-start | bytes 4718592 | tf_op jit(solution)/shard_map/all_gather | solution.py:374
  108.0 101.0 %all-gather.21.cloned.1.call-start = ((), (), s32[]{:S(2)}) async-start(), calls=%async_computation.3 | async-start | bytes 4718592 | tf_op jit(solution)/shard_map/all_gather | solution.py:374
  108.8 40.2 %collective-permute-start.13 = (bf16[768,1024]{1,0:T(8,128)(2,1)S(1)}, bf16[768,1024]{1,0:T(8,128)(2,1)}, u32[]{:S(2)}, u32[]{:S(2)}) collective-permute-start(bf16[768,1024]{1,0:T(8,128)(2,1)S(1)} %copy-done.2), channel_id=1, source_target_pairs={{0,2},{1,3},{2,0},{3,1},{4,6},{5,7},{6,4},{7,5},{8,10},{9,11},{10,... | collective-permute-start | bytes 4718600 | tf_op jit(solution)/shard_map/ppermute | solution.py:21
  109.3 38.6 %collective-permute-start.16 = (bf16[384,1024]{1,0:T(8,128)(2,1)S(1)}, bf16[384,1024]{1,0:T(8,128)(2,1)}, u32[]{:S(2)}, u32[]{:S(2)}) collective-permute-start(bf16[384,1024]{1,0:T(8,128)(2,1)S(1)} %broadcast_select_fusion), channel_id=1, source_target_pairs={{0,4},{4,0},{8,12},{12,8},{16,20},{20,16},{24,28},{28,24},{1,5},{5... | collective-permute-start | bytes 2359304 | tf_op jit(solution)/shard_map/ppermute | solution.py:21
  110.8 37.1 %collective-permute-start.17 = (bf16[1088,256]{1,0:T(8,128)(2,1)S(1)}, bf16[1088,256]{1,0:T(8,128)(2,1)S(1)}, u32[]{:S(2)}, u32[]{:S(2)}) collective-permute-start(bf16[1088,256]{1,0:T(8,128)(2,1)S(1)} %pad_maximum_fusion.5), channel_id=1, source_target_pairs={{0,8},{4,12},{8,0},{12,4},{16,24},{20,28},{24,16},{28,20},{1,9},{5... | collective-permute-start | bytes 1671176 | tf_op jit(solution)/shard_map/ppermute | solution.py:21
  112.8 35.2 %collective-permute-start.14 = (bf16[512,512]{1,0:T(8,128)(2,1)S(1)}, bf16[512,512]{1,0:T(8,128)(2,1)S(1)}, u32[]{:S(2)}, u32[]{:S(2)}) collective-permute-start(bf16[512,512]{1,0:T(8,128)(2,1)S(1)} %copy-done.11), channel_id=1, source_target_pairs={{0,20},{4,16},{8,28},{12,24},{16,4},{20,0},{24,12},{28,8},{1,21},{... | collective-permute-start | bytes 1572872 | tf_op jit(solution)/shard_map/ppermute | solution.py:21
  113.4 34.6 %collective-permute-start.15 = (bf16[256,512]{1,0:T(8,128)(2,1)}, bf16[256,512]{1,0:T(8,128)(2,1)S(1)}, u32[]{:S(2)}, u32[]{:S(2)}) collective-permute-start(bf16[256,512]{1,0:T(8,128)(2,1)} %get-tuple-element.90), channel_id=1, source_target_pairs={{0,24},{4,28},{8,16},{12,20},{16,8},{20,12},{24,0},{28,4},{1,25},{... | collective-permute-start | bytes 786440 | tf_op jit(solution)/shard_map/ppermute | solution.py:21
  152.8 56.2 %all-gather.27.cloned.1.call-start = ((), (), s32[]{:S(2)}) async-start(), calls=%async_computation.6 | async-start | bytes 4718592 | tf_op jit(solution)/shard_map/all_gather | solution.py:374
  153.1 37.5 %collective-permute-start.18 = (bf16[768,1024]{1,0:T(8,128)(2,1)S(1)}, bf16[768,1024]{1,0:T(8,128)(2,1)}, u32[]{:S(2)}, u32[]{:S(2)}) collective-permute-start(bf16[768,1024]{1,0:T(8,128)(2,1)S(1)} %copy-done.3), channel_id=1, source_target_pairs={{0,2},{1,3},{2,0},{3,1},{4,6},{5,7},{6,4},{7,5},{8,10},{9,11},{10,... | collective-permute-start | bytes 4718600 | tf_op jit(solution)/shard_map/ppermute | solution.py:21
  154.6 35.9 %collective-permute-start.21 = (bf16[2176,256]{1,0:T(8,128)(2,1)S(1)}, bf16[2176,256]{1,0:T(8,128)(2,1)S(1)}, u32[]{:S(2)}, u32[]{:S(2)}) collective-permute-start(bf16[2176,256]{1,0:T(8,128)(2,1)S(1)} %pad_maximum_fusion.4.refs_18_), channel_id=1, source_target_pairs={{0,4},{4,0},{8,12},{12,8},{16,20},{20,16},{24,28},{28,24},{1,5},{5... | collective-permute-start | bytes 3342344 | tf_op jit(solution)/shard_map/ppermute | solution.py:21
  156.2 33.5 %collective-permute-start.19 = (bf16[512,512]{1,0:T(8,128)(2,1)}, bf16[512,512]{1,0:T(8,128)(2,1)S(1)}, u32[]{:S(2)}, u32[]{:S(2)}) collective-permute-start(bf16[512,512]{1,0:T(8,128)(2,1)} %pad_maximum_fusion.11), channel_id=1, source_target_pairs={{0,16},{4,20},{8,24},{12,28},{16,0},{20,4},{24,8},{28,12},{1,17},{... | collective-permute-start | bytes 1572872 | tf_op jit(solution)/shard_map/ppermute | solution.py:21
  156.2 33.5 %collective-permute-start.22 = (bf16[512,512]{1,0:T(8,128)(2,1)}, bf16[512,512]{1,0:T(8,128)(2,1)S(1)}, u32[]{:S(2)}, u32[]{:S(2)}) collective-permute-start(bf16[512,512]{1,0:T(8,128)(2,1)} %pad_maximum_fusion.12), channel_id=1, source_target_pairs={{0,12},{4,8},{8,4},{12,0},{16,28},{20,24},{24,20},{28,16},{1,13},{... | collective-permute-start | bytes 1572872 | tf_op jit(solution)/shard_map/ppermute | solution.py:21
  158.6 31.1 %collective-permute-start.20 = (bf16[256,512]{1,0:T(8,128)(2,1)S(1)}, bf16[256,512]{1,0:T(8,128)(2,1)S(1)}, u32[]{:S(2)}, u32[]{:S(2)}) collective-permute-start(bf16[256,512]{1,0:T(8,128)(2,1)S(1)} %copy-done.12), channel_id=1, source_target_pairs={{0,24},{4,28},{8,16},{12,20},{16,8},{20,12},{24,0},{28,4},{1,25},{... | collective-permute-start | bytes 786440 | tf_op jit(solution)/shard_map/ppermute | solution.py:21
  269.1 26.4 %collective-permute-start.30 = (bf16[384,256]{1,0:T(8,128)(2,1)S(1)}, bf16[384,256]{1,0:T(8,128)(2,1)S(1)}, u32[]{:S(2)}, u32[]{:S(2)}) collective-permute-start(bf16[384,256]{1,0:T(8,128)(2,1)S(1)} %get-tuple-element.146), channel_id=1, source_target_pairs={{0,20},{4,16},{8,28},{12,24},{16,4},{20,0},{24,12},{28,8},{1,21},{... | collective-permute-start | bytes 589832 | tf_op jit(solution)/shard_map/ppermute | solution.py:21
  272.0 29.4 %collective-permute-start.31 = (bf16[384,256]{1,0:T(8,128)(2,1)S(1)}, bf16[384,256]{1,0:T(8,128)(2,1)S(1)}, u32[]{:S(2)}, u32[]{:S(2)}) collective-permute-start(bf16[384,256]{1,0:T(8,128)(2,1)S(1)} %get-tuple-element.145), channel_id=1, source_target_pairs={{0,24},{4,28},{8,16},{12,20},{16,8},{20,12},{24,0},{28,4},{1,25},{... | collective-permute-start | bytes 589832 | tf_op jit(solution)/shard_map/ppermute | solution.py:21
  277.6 26.0 %collective-permute-start.32 = (bf16[384,256]{1,0:T(8,128)(2,1)S(1)}, bf16[384,256]{1,0:T(8,128)(2,1)S(1)}, u32[]{:S(2)}, u32[]{:S(2)}) collective-permute-start(bf16[384,256]{1,0:T(8,128)(2,1)S(1)} %get-tuple-element.144), channel_id=1, source_target_pairs={{0,28},{4,24},{8,20},{12,16},{16,12},{20,8},{24,4},{28,0},{1,29},{... | collective-permute-start | bytes 589832 | tf_op jit(solution)/shard_map/ppermute | solution.py:21
  327.7 19.5 %collective-permute-start.35 = (bf16[384,1024]{1,0:T(8,128)(2,1)S(1)}, bf16[384,1024]{1,0:T(8,128)(2,1)S(1)}, u32[]{:S(2)}, u32[]{:S(2)}) collective-permute-start(bf16[384,1024]{1,0:T(8,128)(2,1)S(1)} %add_convert_fusion.1), channel_id=1, source_target_pairs={{0,2},{1,3},{2,0},{3,1},{4,6},{5,7},{6,4},{7,5},{8,10},{9,11},{10,... | collective-permute-start | bytes 2359304 | tf_op jit(solution)/shard_map/ppermute | solution.py:21
  (44 other events, 627.7 us)
Sparse Core Ops, SparseCore 0:
  34.3 10.7 all-gather.14
  59.8 13.4 all-gather.22
  74.8 13.2 all-gather.16
  107.5 12.2 all-gather.18
  121.3 13.2 all-gather.24
  152.9 11.9 all-gather.20
  166.4 13.2 all-gather.26

commit v4 on v3

--- a/solution.py
+++ b/solution.py
@@ -131,10 +131,11 @@
     stretches = rows // length
 
     def row_factor():
-        squares = jnp.zeros((rows, 1), jnp.float32)
-        for e in range(blocks):
-            part = xbuf[slot, :, e * feats : (e + 1) * feats].astype(jnp.float32)
-            squares = squares + jnp.sum(part * part, axis=1, keepdims=True)
+        squares = jnp.zeros((rows, LANES), jnp.float32)
+        for lo in range(0, dim, LANES):
+            part = xbuf[slot, :, lo : lo + LANES].astype(jnp.float32)
+            squares = squares + part * part
+        squares = jnp.sum(squares, axis=1, keepdims=True)
         return lax.rsqrt(squares * (1.0 / dim) + EPS)
 
     def project(tile, factor):
@@ -156,7 +157,7 @@
         tri = lax.broadcasted_iota(jnp.int32, (length, length), 0) >= lax.broadcasted_iota(
             jnp.int32, (length, length), 1
         )
-        ones = jnp.where(tri, 1.0, 0.0).astype(jnp.float32)
+        ones = jnp.where(tri, 1.0, 0.0).astype(jnp.bfloat16)
         row = lax.broadcasted_iota(jnp.int32, (2 * LANES, chans), 0) % LANES
         lane = lax.broadcasted_iota(jnp.int32, (2 * LANES, chans), 1) // width
         widen = jnp.where(row == lane, 1.0, 0.0).astype(jnp.bfloat16)
@@ -177,7 +178,12 @@
         raw = pbuf[r0 : r0 + length, chans:] + dt_bias[...]
         step = jnp.maximum(raw, 0.0) + jnp.log1p(jnp.exp(-jnp.abs(raw)))
         logd = neg_rate[...] * step
-        cum = jnp.dot(ones, logd, preferred_element_type=jnp.float32, precision=HIGHEST)
+        term0 = logd.astype(jnp.bfloat16)
+        rest = logd - term0.astype(jnp.float32)
+        term1 = rest.astype(jnp.bfloat16)
+        term2 = (rest - term1.astype(jnp.float32)).astype(jnp.bfloat16)
+        sums = jnp.dot(ones, jnp.concatenate([term0, term1, term2], axis=1), preferred_element_type=jnp.float32)
+        cum = sums[:, :LANES] + (sums[:, LANES : 2 * LANES] + sums[:, 2 * LANES :])
         cum_t = cum.T
         columns = jnp.concatenate([jnp.exp(cum), step, jnp.exp(cum[length - 1 :, :] - cum)], axis=0)
         high = columns.astype(jnp.bfloat16)
@@ -534,13 +540,12 @@
     wide = jnp.float32
     shape = (shards, groups, rows, chans, blocks)
     shape = (shards, groups, rows, chans, blocks)
-    first, flat = out_terms(where, [*arrived, gains], w_flat, shape, (3,), True)
-    via_core = swap(first, "head", 1)
+    first, third, flat = out_terms(where, [*arrived, gains], w_flat, shape, (3, 1), True)
+    via_core, from_core = swap(first, "head", 1), swap(third, "head", 1)
     (second,) = out_terms(where, [flat], w_flat, shape, (2,), False)
     to_pair, flat = together((second.astype(wide) + via_core.astype(wide)).astype(jnp.bfloat16), flat)
     beyond = swap(to_pair, "head", 2)
-    third, own = out_terms(where, [flat], w_flat, shape, (1, 0), False)
-    from_core = swap(third, "head", 1)
+    (own,) = out_terms(where, [flat], w_flat, shape, (0,), False)
     return (own.astype(wide) + from_core.astype(wide) + beyond.astype(wide)).astype(jnp.bfloat16)
 
 

time: 357 us -> 351 us (0.983)
  waiting for transfers between devices: 167 us -> 161 us
    ppermute x32, waiting for transfers between devices: 158 us -> 152 us  [swap(): return lax.ppermute(value, axis, [(i, i ^ bit) for i in range(count)])]
    unnamed x69 -> x71, local copies, waits for them, and re-layouts: 7.83 us -> 7.82 us
  transfers between devices with their start and end apart: 43 -> 43, of which waited for: 22 -> 21; matrix products, arithmetic and copies ran while one was open for 10% -> 11% of each run, Pallas kernels for 2% -> 4%
where the time goes in v4:
time: 351 us; the launch traced here: 350 us
  waiting for transfers between devices  161 us (46%)
  Pallas kernels  74 us (21%)
  starting transfers between devices  49.6 us (14%)
  other arithmetic  26.5 us (8%)
  local copies, waits for them, and re-layouts  25.2 us (7%)
  between operations  14.3 us (4%)
    ppermute x32, waiting for transfers between devices, swap(): return lax.ppermute(value, axis, [(i, i ^ bit) for i in range(count)])  152 us
    pallas_call x1, Pallas kernels, mixer(): pl.pallas_call(partial(mixer_kernel, cfg), out_shape=jax.ShapeDtypeStruct...  52.1 us
    ppermute x32, starting transfers between devices, swap(): return lax.ppermute(value, axis, [(i, i ^ bit) for i in range(count)])  34.3 us
    pallas_call x3, Pallas kernels, out_terms(): pl.pallas_call(partial(terms_kernel, (shards, chans, groups, order, keep)...  21.9 us
    ppermute x4, starting transfers between devices, line(): lax.ppermute(value, 'seq', [(2 * a + y, 2 * b + y) for a, b in pairs for...  14.9 us
    concatenate x6, other arithmetic, stack(): return jnp.concatenate(parts, axis=0)  10.2 us
    ppermute x4, waiting for transfers between devices, line(): lax.ppermute(value, 'seq', [(2 * a + y, 2 * b + y) for a, b in pairs for...  8.32 us
    unnamed x71, local copies, waits for them, and re-layouts  7.82 us
  transfers between devices with their start and end apart: 43, of which 21 were waited for; matrix products, arithmetic and copies ran while one was open for 11% of the time, Pallas kernels for 4%

profile of v4, /device:TPU:8, one launch (start us, length us, event | category | flops | bytes accessed | tf_op | source)
XLA Modules:
  0.0 350.3 jit_solution(5067680755431960468)
XLA Ops:
  10.0 4.6 %collective-permute-start.3 = (bf16[384,1024]{1,0:T(8,128)(2,1)}, bf16[384,1024]{1,0:T(8,128)(2,1)}, u32[]{:S(2)}, u32[]{:S(2)}) collective-permute-start(bf16[384,1024]{1,0:T(8,128)(2,1)} %param.11), channel_id=1, source_target_pairs={{8,16},{12,20},{16,8},{20,12},{9,17},{13,21},{17,9},{21,13},{10,18... | collective-permute-start | bytes 2359304 | tf_op jit(solution)/shard_map/ppermute | solution.py:371
  16.3 5.9 %constant_dynamic-slice_fusion.10 = (bf16[512,1,256]{2,1,0:T(2,128)(2,1)S(1)}, bf16[512,1,256]{2,1,0:T(2,128)(2,1)S(1)}, bf16[512,1,256]{2,1,0:T(2,128)(2,1)S(1)...) fusion(bf16[512,2,2304]{2,1,0:T(2,128)(2,1)} %param.13, s32[]{:T(128)S(6)} %select_n.248, s32[]{:T(128)S(6)} %select_n.243, ...), kind=kLoop, calls=%fused_computation.77 | loop fusion | bytes 2621468 | tf_op jit(solution)/shard_map/dynamic_slice | solution.py:478
  23.5 2.5 collective-permute-done
  28.6 3.0 collective-permute-done.3
  31.6 2.6 pad_maximum_fusion
  35.6 3.6 %collective-permute-start.6 = (bf16[384,1024]{1,0:T(8,128)(2,1)}, bf16[384,1024]{1,0:T(8,128)(2,1)}, u32[]{:S(2)}, u32[]{:S(2)}) collective-permute-start(bf16[384,1024]{1,0:T(8,128)(2,1)} %collective-permute-done.2), channel_id=1, source_target_pairs={{8,16},{12,20},{16,8},{20,12},{9,17},{13,21},{17,9},{21,13},{10,18... | collective-permute-start | bytes 2359304 | tf_op jit(solution)/shard_map/ppermute | solution.py:371
  39.3 3.5 %copy.35 = bf16[512,2,2304]{2,0,1:T(8,128)(2,1)S(1)} copy(bf16[512,2,2304]{2,1,0:T(2,128)(2,1)} %param.13) | data formatting | bytes 9437184 | tf_op jit(solution)/shard_map/optimization_barrier | solution.py:384
  42.8 2.2 collective-permute-start.7
  50.3 2.3 collective-permute-done.4
  55.0 3.2 collective-permute-done.7
  67.6 4.4 %collective-permute-start.11 = (bf16[384,1024]{1,0:T(8,128)(2,1)}, bf16[384,1024]{1,0:T(8,128)(2,1)S(1)}, u32[]{:S(2)}, u32[]{:S(2)}) collective-permute-start(bf16[384,1024]{1,0:T(8,128)(2,1)} %collective-permute-done.6), channel_id=1, source_target_pairs={{8,0},{12,4},{16,24},{20,28},{9,1},{13,5},{17,25},{21,29},{10,2},{... | collective-permute-start | bytes 2359304 | tf_op jit(solution)/shard_map/ppermute | solution.py:371
  74.6 28.2 %collective-permute-done.12 = bf16[544,256]{1,0:T(8,128)(2,1)S(1)} collective-permute-done((bf16[544,256]{1,0:T(8,128)(2,1)S(1)}, bf16[544,256]{1,0:T(8,128)(2,1)S(1)}, u32[]{:S(2)}, u32[]{:S(2)}) %collective-permute-start.12) | collective-permute-done | bytes 278560 | tf_op jit(solution)/shard_map/ppermute | solution.py:21
  103.6 2.5 pad_maximum_fusion.1
  114.3 33.6 %collective-permute-done.15.refs_15_ = bf16[256,512]{1,0:T(8,128)(2,1)S(1)} collective-permute-done((bf16[256,512]{1,0:T(8,128)(2,1)}, bf16[256,512]{1,0:T(8,128)(2,1)S(1)}, u32[]{:S(2)}, u32[]{:S(2)}) %collective-permute-start.15) | collective-permute-done | bytes 262176 | tf_op jit(solution)/shard_map/ppermute | solution.py:21
  149.0 2.5 pad_maximum_fusion.2
  156.2 2.4 collective-permute-start.22
  159.7 30.0 %collective-permute-done.20.refs_16_ = bf16[256,512]{1,0:T(8,128)(2,1)S(1)} collective-permute-done((bf16[256,512]{1,0:T(8,128)(2,1)S(1)}, bf16[256,512]{1,0:T(8,128)(2,1)S(1)}, u32[]{:S(2)}, u32[]{:S(2)}) %collective-permute-start.20) | collective-permute-done | bytes 262176 | tf_op jit(solution)/shard_map/ppermute | solution.py:21
  198.1 9.8 %collective-permute-done.24.refs_10_ = bf16[512,512]{1,0:T(8,128)(2,1)S(1)} collective-permute-done((bf16[512,512]{1,0:T(8,128)(2,1)}, bf16[512,512]{1,0:T(8,128)(2,1)S(1)}, u32[]{:S(2)}, u32[]{:S(2)}) %collective-permute-start.24) | collective-permute-done | bytes 524320 | tf_op jit(solution)/shard_map/ppermute | solution.py:21
  210.2 52.1 %shard_map.109 = bf16[3072,256]{1,0:T(8,128)(2,1)} custom-call(s32[10]{0:T(128)} %pad_add_fusion.where_ref, bf16[2,768,1024]{2,1,0:T(8,128)(2,1)} %bitcast.99, bf16[2,768,1024]{2,1,0:T(8,128)(2,1)} %bitcast.101, bf16[2,768,1024]{2,1,0:T(8,128)(2,1)} %bitcast.102, bf16[2,768,1024]{2,1,0:T(8,128)(2,1)} %bitcast.104, bf16[2,768,1024]{2,1,0:T(8,128)(2,1)} %bitcast.100, ...), custom_call_target="tpu_custom_call" | custom-call | flops 22548578304 | bytes 25165824 | tf_op jit(solution)/shard_map/pallas_call | solution.py:270
  262.3 2.3 constant_dynamic-slice_fusion
  265.4 2.7 collective-permute-start.28
  268.7 2.4 collective-permute-start.30
  272.4 4.7 %collective-permute-done.27.refs_2_ = bf16[384,256]{1,0:T(8,128)(2,1)S(1)} collective-permute-done((bf16[384,256]{1,0:T(8,128)(2,1)S(1)}, bf16[384,256]{1,0:T(8,128)(2,1)S(1)}, u32[]{:S(2)}, u32[]{:S(2)}) %collective-permute-start.27) | collective-permute-done | bytes 196640 | tf_op jit(solution)/shard_map/ppermute | solution.py:21
  277.1 2.5 collective-permute-start.32
  281.9 13.1 %collective-permute-done.30.refs_5_ = bf16[384,256]{1,0:T(8,128)(2,1)S(1)} collective-permute-done((bf16[384,256]{1,0:T(8,128)(2,1)S(1)}, bf16[384,256]{1,0:T(8,128)(2,1)S(1)}, u32[]{:S(2)}, u32[]{:S(2)}) %collective-permute-start.30) | collective-permute-done | bytes 196640 | tf_op jit(solution)/shard_map/ppermute | solution.py:21
  295.1 5.9 %collective-permute-done.31.refs_6_ = bf16[384,256]{1,0:T(8,128)(2,1)S(1)} collective-permute-done((bf16[384,256]{1,0:T(8,128)(2,1)S(1)}, bf16[384,256]{1,0:T(8,128)(2,1)S(1)}, u32[]{:S(2)}, u32[]{:S(2)}) %collective-permute-start.31) | collective-permute-done | bytes 196640 | tf_op jit(solution)/shard_map/ppermute | solution.py:21
  300.9 2.2 collective-permute-done.32.refs_7_
  303.8 9.2 %shard_map.110 = (bf16[384,1024]{1,0:T(8,128)(2,1)}, bf16[384,1024]{1,0:T(8,128)(2,1)}, bf16[384,2048]{1,0:T(8,128)(2,1)}) custom-call(s32[10]{0:T(128)} %pad_add_fusion.where_ref, bf16[384,256]{1,0:T(8,128)(2,1)} %get-tuple-element.149.refs_0_, bf16[384,256]{1,0:T(8,128)(2,1)} %copy-done.13, bf16[384,256]{1,0:T(8,128)(2,1)} %copy-done.14, ...), custom_call_target="tpu_custom_call" | custom-call | flops 393216 | bytes 393216 | tf_op jit(solution)/shard_map/pallas_call | solution.py:352
  313.1 6.4 %shard_map.111 = bf16[384,1024]{1,0:T(8,128)(2,1)} custom-call(s32[10]{0:T(128)} %pad_add_fusion.where_ref, bf16[384,2048]{1,0:T(8,128)(2,1)} %get-tuple-element.122.refs_0_, bf16[2048,4096]{1,0:T(8,128)(2,1)} %bitcast.92), custom_call_target="tpu_custom_call" | custom-call | flops 393216 | bytes 393216 | tf_op jit(solution)/shard_map/pallas_call | solution.py:352
  322.4 6.3 %shard_map.112 = bf16[384,1024]{1,0:T(8,128)(2,1)} custom-call(s32[10]{0:T(128)} %pad_add_fusion.where_ref, bf16[384,2048]{1,0:T(8,128)(2,1)} %get-tuple-element.122.refs_0_, bf16[2048,4096]{1,0:T(8,128)(2,1)} %bitcast.93), custom_call_target="tpu_custom_call" | custom-call | flops 393216 | bytes 393216 | tf_op jit(solution)/shard_map/pallas_call | solution.py:352
  328.7 12.3 %collective-permute-done.35 = bf16[384,1024]{1,0:T(8,128)(2,1)S(1)} collective-permute-done((bf16[384,1024]{1,0:T(8,128)(2,1)S(1)}, bf16[384,1024]{1,0:T(8,128)(2,1)S(1)}, u32[]{:S(2)}, u32[]{:S(2)}) %collective-permute-start.35) | collective-permute-done | bytes 786464 | tf_op jit(solution)/shard_map/ppermute | solution.py:21
  341.0 2.4 add_convert_fusion
  (181 shorter events, 64.5 us)
Async XLA Ops:
  6.5 191.5 %all-gather.15.cloned.1.call-start = ((), (), s32[]{:S(2)}) async-start(), calls=%async_computation | async-start | bytes 4718592 | tf_op jit(solution)/shard_map/all_gather | solution.py:380
  6.5 19.5 %collective-permute-start = (bf16[384,1024]{1,0:T(8,128)(2,1)}, bf16[384,1024]{1,0:T(8,128)(2,1)S(1)}, u32[]{:S(2)}, u32[]{:S(2)}) collective-permute-start(bf16[384,1024]{1,0:T(8,128)(2,1)} %param.11), channel_id=1, source_target_pairs={{0,2},{1,3},{2,0},{3,1},{4,6},{5,7},{6,4},{7,5},{8,10},{9,11},{10,... | collective-permute-start | bytes 2359304 | tf_op jit(solution)/shard_map/ppermute | solution.py:21
  8.0 19.3 %collective-permute-start.1 = (bf16[384,1024]{1,0:T(8,128)(2,1)}, bf16[384,1024]{1,0:T(8,128)(2,1)}, u32[]{:S(2)}, u32[]{:S(2)}) collective-permute-start(bf16[384,1024]{1,0:T(8,128)(2,1)} %param.11), channel_id=1, source_target_pairs={{0,4},{4,0},{8,12},{12,8},{16,20},{20,16},{24,28},{28,24},{1,5},{5... | collective-permute-start | bytes 2359304 | tf_op jit(solution)/shard_map/ppermute | solution.py:21
  9.6 19.0 %collective-permute-start.2 = (bf16[384,1024]{1,0:T(8,128)(2,1)}, bf16[384,1024]{1,0:T(8,128)(2,1)}, u32[]{:S(2)}, u32[]{:S(2)}) collective-permute-start(bf16[384,1024]{1,0:T(8,128)(2,1)} %param.11), channel_id=1, source_target_pairs={{0,8},{4,12},{8,0},{12,4},{16,24},{20,28},{24,16},{28,20},{1,9},{5... | collective-permute-start | bytes 2359304 | tf_op jit(solution)/shard_map/ppermute | solution.py:21
  10.0 21.6 %collective-permute-start.3 = (bf16[384,1024]{1,0:T(8,128)(2,1)}, bf16[384,1024]{1,0:T(8,128)(2,1)}, u32[]{:S(2)}, u32[]{:S(2)}) collective-permute-start(bf16[384,1024]{1,0:T(8,128)(2,1)} %param.11), channel_id=1, source_target_pairs={{8,16},{12,20},{16,8},{20,12},{9,17},{13,21},{17,9},{21,13},{10,18... | collective-permute-start | bytes 2359304 | tf_op jit(solution)/shard_map/ppermute | solution.py:371
  34.2 163.8 %all-gather.23.cloned.1.call-start = ((), (), s32[]{:S(2)}) async-start(), calls=%async_computation.4 | async-start | bytes 4718592 | tf_op jit(solution)/shard_map/all_gather | solution.py:380
  34.5 18.1 %collective-permute-start.4 = (bf16[384,1024]{1,0:T(8,128)(2,1)}, bf16[384,1024]{1,0:T(8,128)(2,1)S(1)}, u32[]{:S(2)}, u32[]{:S(2)}) collective-permute-start(bf16[384,1024]{1,0:T(8,128)(2,1)} %collective-permute-done.1), channel_id=1, source_target_pairs={{0,2},{1,3},{2,0},{3,1},{4,6},{5,7},{6,4},{7,5},{8,10},{9,11},{10,... | collective-permute-start | bytes 2359304 | tf_op jit(solution)/shard_map/ppermute | solution.py:21
  35.6 19.4 %collective-permute-start.6 = (bf16[384,1024]{1,0:T(8,128)(2,1)}, bf16[384,1024]{1,0:T(8,128)(2,1)}, u32[]{:S(2)}, u32[]{:S(2)}) collective-permute-start(bf16[384,1024]{1,0:T(8,128)(2,1)} %collective-permute-done.2), channel_id=1, source_target_pairs={{8,16},{12,20},{16,8},{20,12},{9,17},{13,21},{17,9},{21,13},{10,18... | collective-permute-start | bytes 2359304 | tf_op jit(solution)/shard_map/ppermute | solution.py:371
  59.7 138.4 %all-gather.17.cloned.1.call-start = ((), (), s32[]{:S(2)}) async-start(), calls=%async_computation.1 | async-start | bytes 4718592 | tf_op jit(solution)/shard_map/all_gather | solution.py:380
  64.5 133.6 %all-gather.19.cloned.1.call-start = ((), (), s32[]{:S(2)}) async-start(), calls=%async_computation.2 | async-start | bytes 4718592 | tf_op jit(solution)/shard_map/all_gather | solution.py:380
  64.5 39.1 %collective-permute-start.8 = (bf16[768,1024]{1,0:T(8,128)(2,1)}, bf16[768,1024]{1,0:T(8,128)(2,1)}, u32[]{:S(2)}, u32[]{:S(2)}) collective-permute-start(bf16[768,1024]{1,0:T(8,128)(2,1)} %copy-done.4), channel_id=1, source_target_pairs={{0,2},{1,3},{2,0},{3,1},{4,6},{5,7},{6,4},{7,5},{8,10},{9,11},{10,... | collective-permute-start | bytes 4718600 | tf_op jit(solution)/shard_map/ppermute | solution.py:21
  66.1 36.7 %collective-permute-start.10 = (bf16[384,1024]{1,0:T(8,128)(2,1)S(1)}, bf16[384,1024]{1,0:T(8,128)(2,1)}, u32[]{:S(2)}, u32[]{:S(2)}) collective-permute-start(bf16[384,1024]{1,0:T(8,128)(2,1)S(1)} %broadcast_select_fusion.1), channel_id=1, source_target_pairs={{0,4},{4,0},{8,12},{12,8},{16,20},{20,16},{24,28},{28,24},{1,5},{5... | collective-permute-start | bytes 2359304 | tf_op jit(solution)/shard_map/ppermute | solution.py:21
  67.6 35.2 %collective-permute-start.11 = (bf16[384,1024]{1,0:T(8,128)(2,1)}, bf16[384,1024]{1,0:T(8,128)(2,1)S(1)}, u32[]{:S(2)}, u32[]{:S(2)}) collective-permute-start(bf16[384,1024]{1,0:T(8,128)(2,1)} %collective-permute-done.6), channel_id=1, source_target_pairs={{8,0},{12,4},{16,24},{20,28},{9,1},{13,5},{17,25},{21,29},{10,2},{... | collective-permute-start | bytes 2359304 | tf_op jit(solution)/shard_map/ppermute | solution.py:371
  72.1 30.8 %collective-permute-start.9 = (bf16[512,512]{1,0:T(8,128)(2,1)}, bf16[512,512]{1,0:T(8,128)(2,1)S(1)}, u32[]{:S(2)}, u32[]{:S(2)}) collective-permute-start(bf16[512,512]{1,0:T(8,128)(2,1)} %get-tuple-element.77), channel_id=1, source_target_pairs={{0,28},{4,24},{8,20},{12,16},{16,12},{20,8},{24,4},{28,0},{1,29},{... | collective-permute-start | bytes 1572872 | tf_op jit(solution)/shard_map/ppermute | solution.py:21
  72.6 30.2 %collective-permute-start.12 = (bf16[544,256]{1,0:T(8,128)(2,1)S(1)}, bf16[544,256]{1,0:T(8,128)(2,1)S(1)}, u32[]{:S(2)}, u32[]{:S(2)}) collective-permute-start(bf16[544,256]{1,0:T(8,128)(2,1)S(1)} %pad_maximum_fusion.14), channel_id=1, source_target_pairs={{0,16},{4,20},{8,24},{12,28},{16,0},{20,4},{24,8},{28,12},{1,17},{... | collective-permute-start | bytes 835592 | tf_op jit(solution)/shard_map/ppermute | solution.py:21
  107.4 90.7 %all-gather.25.cloned.1.call-start = ((), (), s32[]{:S(2)}) async-start(), calls=%async_computation.5 | async-start | bytes 4718592 | tf_op jit(solution)/shard_map/all_gather | solution.py:380
  108.0 101.0 %all-gather.21.cloned.1.call-start = ((), (), s32[]{:S(2)}) async-start(), calls=%async_computation.3 | async-start | bytes 4718592 | tf_op jit(solution)/shard_map/all_gather | solution.py:380
  108.8 40.2 %collective-permute-start.13 = (bf16[768,1024]{1,0:T(8,128)(2,1)S(1)}, bf16[768,1024]{1,0:T(8,128)(2,1)}, u32[]{:S(2)}, u32[]{:S(2)}) collective-permute-start(bf16[768,1024]{1,0:T(8,128)(2,1)S(1)} %copy-done.2), channel_id=1, source_target_pairs={{0,2},{1,3},{2,0},{3,1},{4,6},{5,7},{6,4},{7,5},{8,10},{9,11},{10,... | collective-permute-start | bytes 4718600 | tf_op jit(solution)/shard_map/ppermute | solution.py:21
  109.3 38.6 %collective-permute-start.16 = (bf16[384,1024]{1,0:T(8,128)(2,1)S(1)}, bf16[384,1024]{1,0:T(8,128)(2,1)}, u32[]{:S(2)}, u32[]{:S(2)}) collective-permute-start(bf16[384,1024]{1,0:T(8,128)(2,1)S(1)} %broadcast_select_fusion), channel_id=1, source_target_pairs={{0,4},{4,0},{8,12},{12,8},{16,20},{20,16},{24,28},{28,24},{1,5},{5... | collective-permute-start | bytes 2359304 | tf_op jit(solution)/shard_map/ppermute | solution.py:21
  110.8 37.1 %collective-permute-start.17 = (bf16[1088,256]{1,0:T(8,128)(2,1)S(1)}, bf16[1088,256]{1,0:T(8,128)(2,1)S(1)}, u32[]{:S(2)}, u32[]{:S(2)}) collective-permute-start(bf16[1088,256]{1,0:T(8,128)(2,1)S(1)} %pad_maximum_fusion.5), channel_id=1, source_target_pairs={{0,8},{4,12},{8,0},{12,4},{16,24},{20,28},{24,16},{28,20},{1,9},{5... | collective-permute-start | bytes 1671176 | tf_op jit(solution)/shard_map/ppermute | solution.py:21
  112.8 35.2 %collective-permute-start.14 = (bf16[512,512]{1,0:T(8,128)(2,1)S(1)}, bf16[512,512]{1,0:T(8,128)(2,1)S(1)}, u32[]{:S(2)}, u32[]{:S(2)}) collective-permute-start(bf16[512,512]{1,0:T(8,128)(2,1)S(1)} %copy-done.11), channel_id=1, source_target_pairs={{0,20},{4,16},{8,28},{12,24},{16,4},{20,0},{24,12},{28,8},{1,21},{... | collective-permute-start | bytes 1572872 | tf_op jit(solution)/shard_map/ppermute | solution.py:21
  113.4 34.6 %collective-permute-start.15 = (bf16[256,512]{1,0:T(8,128)(2,1)}, bf16[256,512]{1,0:T(8,128)(2,1)S(1)}, u32[]{:S(2)}, u32[]{:S(2)}) collective-permute-start(bf16[256,512]{1,0:T(8,128)(2,1)} %get-tuple-element.89), channel_id=1, source_target_pairs={{0,24},{4,28},{8,16},{12,20},{16,8},{20,12},{24,0},{28,4},{1,25},{... | collective-permute-start | bytes 786440 | tf_op jit(solution)/shard_map/ppermute | solution.py:21
  152.8 56.2 %all-gather.27.cloned.1.call-start = ((), (), s32[]{:S(2)}) async-start(), calls=%async_computation.6 | async-start | bytes 4718592 | tf_op jit(solution)/shard_map/all_gather | solution.py:380
  153.1 37.5 %collective-permute-start.18 = (bf16[768,1024]{1,0:T(8,128)(2,1)S(1)}, bf16[768,1024]{1,0:T(8,128)(2,1)}, u32[]{:S(2)}, u32[]{:S(2)}) collective-permute-start(bf16[768,1024]{1,0:T(8,128)(2,1)S(1)} %copy-done.3), channel_id=1, source_target_pairs={{0,2},{1,3},{2,0},{3,1},{4,6},{5,7},{6,4},{7,5},{8,10},{9,11},{10,... | collective-permute-start | bytes 4718600 | tf_op jit(solution)/shard_map/ppermute | solution.py:21
  154.6 35.9 %collective-permute-start.21 = (bf16[2176,256]{1,0:T(8,128)(2,1)S(1)}, bf16[2176,256]{1,0:T(8,128)(2,1)S(1)}, u32[]{:S(2)}, u32[]{:S(2)}) collective-permute-start(bf16[2176,256]{1,0:T(8,128)(2,1)S(1)} %pad_maximum_fusion.4.refs_18_), channel_id=1, source_target_pairs={{0,4},{4,0},{8,12},{12,8},{16,20},{20,16},{24,28},{28,24},{1,5},{5... | collective-permute-start | bytes 3342344 | tf_op jit(solution)/shard_map/ppermute | solution.py:21
  156.2 33.5 %collective-permute-start.19 = (bf16[512,512]{1,0:T(8,128)(2,1)}, bf16[512,512]{1,0:T(8,128)(2,1)S(1)}, u32[]{:S(2)}, u32[]{:S(2)}) collective-permute-start(bf16[512,512]{1,0:T(8,128)(2,1)} %pad_maximum_fusion.11), channel_id=1, source_target_pairs={{0,16},{4,20},{8,24},{12,28},{16,0},{20,4},{24,8},{28,12},{1,17},{... | collective-permute-start | bytes 1572872 | tf_op jit(solution)/shard_map/ppermute | solution.py:21
  156.2 33.5 %collective-permute-start.22 = (bf16[512,512]{1,0:T(8,128)(2,1)}, bf16[512,512]{1,0:T(8,128)(2,1)S(1)}, u32[]{:S(2)}, u32[]{:S(2)}) collective-permute-start(bf16[512,512]{1,0:T(8,128)(2,1)} %pad_maximum_fusion.12), channel_id=1, source_target_pairs={{0,12},{4,8},{8,4},{12,0},{16,28},{20,24},{24,20},{28,16},{1,13},{... | collective-permute-start | bytes 1572872 | tf_op jit(solution)/shard_map/ppermute | solution.py:21
  158.6 31.1 %collective-permute-start.20 = (bf16[256,512]{1,0:T(8,128)(2,1)S(1)}, bf16[256,512]{1,0:T(8,128)(2,1)S(1)}, u32[]{:S(2)}, u32[]{:S(2)}) collective-permute-start(bf16[256,512]{1,0:T(8,128)(2,1)S(1)} %copy-done.12), channel_id=1, source_target_pairs={{0,24},{4,28},{8,16},{12,20},{16,8},{20,12},{24,0},{28,4},{1,25},{... | collective-permute-start | bytes 786440 | tf_op jit(solution)/shard_map/ppermute | solution.py:21
  268.7 26.4 %collective-permute-start.30 = (bf16[384,256]{1,0:T(8,128)(2,1)S(1)}, bf16[384,256]{1,0:T(8,128)(2,1)S(1)}, u32[]{:S(2)}, u32[]{:S(2)}) collective-permute-start(bf16[384,256]{1,0:T(8,128)(2,1)S(1)} %get-tuple-element.144), channel_id=1, source_target_pairs={{0,20},{4,16},{8,28},{12,24},{16,4},{20,0},{24,12},{28,8},{1,21},{... | collective-permute-start | bytes 589832 | tf_op jit(solution)/shard_map/ppermute | solution.py:21
  271.5 29.4 %collective-permute-start.31 = (bf16[384,256]{1,0:T(8,128)(2,1)S(1)}, bf16[384,256]{1,0:T(8,128)(2,1)S(1)}, u32[]{:S(2)}, u32[]{:S(2)}) collective-permute-start(bf16[384,256]{1,0:T(8,128)(2,1)S(1)} %get-tuple-element.143), channel_id=1, source_target_pairs={{0,24},{4,28},{8,16},{12,20},{16,8},{20,12},{24,0},{28,4},{1,25},{... | collective-permute-start | bytes 589832 | tf_op jit(solution)/shard_map/ppermute | solution.py:21
  277.1 26.0 %collective-permute-start.32 = (bf16[384,256]{1,0:T(8,128)(2,1)S(1)}, bf16[384,256]{1,0:T(8,128)(2,1)S(1)}, u32[]{:S(2)}, u32[]{:S(2)}) collective-permute-start(bf16[384,256]{1,0:T(8,128)(2,1)S(1)} %get-tuple-element.142), channel_id=1, source_target_pairs={{0,28},{4,24},{8,20},{12,16},{16,12},{20,8},{24,4},{28,0},{1,29},{... | collective-permute-start | bytes 589832 | tf_op jit(solution)/shard_map/ppermute | solution.py:21
  321.5 19.5 %collective-permute-start.35 = (bf16[384,1024]{1,0:T(8,128)(2,1)S(1)}, bf16[384,1024]{1,0:T(8,128)(2,1)S(1)}, u32[]{:S(2)}, u32[]{:S(2)}) collective-permute-start(bf16[384,1024]{1,0:T(8,128)(2,1)S(1)} %add_convert_fusion.1), channel_id=1, source_target_pairs={{0,2},{1,3},{2,0},{3,1},{4,6},{5,7},{6,4},{7,5},{8,10},{9,11},{10,... | collective-permute-start | bytes 2359304 | tf_op jit(solution)/shard_map/ppermute | solution.py:21
  (45 other events, 659.8 us)
Sparse Core Ops, SparseCore 0:
  34.3 10.7 all-gather.14
  59.8 13.4 all-gather.22
  74.8 13.2 all-gather.16
  107.5 12.2 all-gather.18
  121.3 13.2 all-gather.24
  152.9 11.9 all-gather.20
  166.4 13.2 all-gather.26

commit v5 on v4

--- a/solution.py
+++ b/solution.py
@@ -297,8 +297,8 @@
 
 
 def terms_kernel(cfg, where_ref, *refs):
-    shards, chans, groups, order, keep = cfg
-    count = shards + 1 if keep else 1
+    shards, chans, groups, order, keep, added = cfg
+    count = shards + 1 if keep else 1 + added
     values, w_hbm, outs = refs[:count], refs[count], refs[count + 1 : count + 1 + len(order)]
     w_buf, sem = refs[-2], refs[-1]
     flat = refs[count + 1 + len(order)] if keep else values[0]
@@ -337,20 +337,22 @@
             copy(block, n).wait()
         for lo in range(0, feats, 256):
             cols = min(256, feats - lo)
-            out_ref[:, lo : lo + cols] = jnp.dot(
-                flat[...], w_buf[block, :, lo : lo + cols], preferred_element_type=jnp.float32
-            ).astype(jnp.bfloat16)
-
-
-def out_terms(where, values, w_flat, shape, order, keep):
+            part = jnp.dot(flat[...], w_buf[block, :, lo : lo + cols], preferred_element_type=jnp.float32)
+            if added:
+                part = part + values[1][:, lo : lo + cols].astype(jnp.float32)
+            out_ref[:, lo : lo + cols] = part.astype(out_ref.dtype)
+
+
+def out_terms(where, values, w_flat, shape, order, keep=False, kind=jnp.bfloat16):
     shards, groups, rows, chans, blocks = shape
     depth, dim = w_flat.shape
     feats = dim // blocks
     vmem = pl.BlockSpec(memory_space=pltpu.VMEM)
     widths = [feats] * len(order) + ([depth] if keep else [])
-    out_shape = tuple(jax.ShapeDtypeStruct((rows, n), jnp.bfloat16) for n in widths)
+    added = 0 if keep else len(values) - 1
+    out_shape = tuple(jax.ShapeDtypeStruct((rows, n), kind) for n in widths)
     return pl.pallas_call(
-        partial(terms_kernel, (shards, chans, groups, order, keep)),
+        partial(terms_kernel, (shards, chans, groups, order, keep, added)),
         out_shape=out_shape,
         in_specs=[pl.BlockSpec(memory_space=pltpu.SMEM)] + [vmem] * len(values) + [pl.BlockSpec(memory_space=pl.ANY)],
         out_specs=(vmem,) * len(widths),
@@ -412,28 +414,26 @@
     )
     q1 = jnp.where(middle, c0, o0)
     q1, z1, yz1, c1, m7, far_map = together(q1, z1, yz1, c1, m7, far_map)
-    a1 = stack(z1, yz1)
-    xa1, w7, yq1, o1, far_map = together(
-        x_swap(a1), s_swap(m7, 7), s_swap(q1, 1), line(c1, outward), s_swap(far_map, 4)
-    )
-    own = [stack(tokens, y0), a1]
-    across = [stack(xp, xy), xa1]
+    xz1, xyz1, w7, yq1, o1, far_map = together(
+        x_swap(z1), x_swap(yz1), s_swap(m7, 7), s_swap(q1, 1), line(c1, outward), s_swap(far_map, 4)
+    )
+    own = [stack(tokens, y0), stack(z1, yz1)]
+    across = [stack(xp, xy), stack(xz1, xyz1)]
     q2 = jnp.where(middle, c1, o1)
-    a2 = stack(q1, yq1)
     maps = stack(own_map, far_map)
     half = m6.shape[0] // 2
-    q2, a2, maps, m5, m6a, m6b = together(q2, a2, maps, m5, m6[:half], m6[half:])
-    xa2, w5, w6a, yq2, maps_z = together(
-        x_swap(a2), s_swap(m5, 5), s_swap(m6a, 6), s_swap(q2, 1), s_swap(maps, 2)
-    )
-    a3 = stack(q2, yq2)
+    q2, q1, yq1, maps, m5, m6a, m6b = together(q2, q1, yq1, maps, m5, m6[:half], m6[half:])
+    xq1, xyq1, w5, w6a, yq2, maps_z = together(
+        x_swap(q1), x_swap(yq1), s_swap(m5, 5), s_swap(m6a, 6), s_swap(q2, 1), s_swap(maps, 2)
+    )
     maps = stack(maps, maps_z)
-    a3, maps, m4, m6b, m3 = together(a3, maps, m4, m6b, m3)
-    xa3, w4, w6b, maps_y, w3 = together(
-        x_swap(a3), s_swap(m4, 4), s_swap(m6b, 6), s_swap(maps, 1), s_swap(m3, 3)
-    )
-    own += [a2, a3]
-    across += [xa2]
+    q2, yq2, maps, m4, m6b, m3 = together(q2, yq2, maps, m4, m6b, m3)
+    xq2, xyq2, w4, w6b, maps_y, w3 = together(
+        x_swap(q2), x_swap(yq2), s_swap(m4, 4), s_swap(m6b, 6), s_swap(maps, 1), s_swap(m3, 3)
+    )
+    own += [stack(q1, yq1), stack(q2, yq2)]
+    across += [stack(xq1, xyq1)]
+    xa3 = stack(xq2, xyq2)
     gathered = [both_cores(v) for v in own + across]
     m1, m2, xa3, w3 = together(m1, m2, xa3, w3)
     w1, w2 = s_swap(m1, 1), s_swap(m2, 2)
@@ -537,16 +537,15 @@
 
     gains = gate_gain.reshape(shards, chans)
     w_flat = w_out.reshape(groups * group_width, w_out.shape[2])
-    wide = jnp.float32
     shape = (shards, groups, rows, chans, blocks)
     shape = (shards, groups, rows, chans, blocks)
     first, third, flat = out_terms(where, [*arrived, gains], w_flat, shape, (3, 1), True)
     via_core, from_core = swap(first, "head", 1), swap(third, "head", 1)
-    (second,) = out_terms(where, [flat], w_flat, shape, (2,), False)
-    to_pair, flat = together((second.astype(wide) + via_core.astype(wide)).astype(jnp.bfloat16), flat)
+    (to_pair,) = out_terms(where, [flat, via_core], w_flat, shape, (2,))
+    to_pair, flat = together(to_pair, flat)
     beyond = swap(to_pair, "head", 2)
-    (own,) = out_terms(where, [flat], w_flat, shape, (0,), False)
-    return (own.astype(wide) + from_core.astype(wide) + beyond.astype(wide)).astype(jnp.bfloat16)
+    (own,) = out_terms(where, [flat, from_core], w_flat, shape, (0,), kind=jnp.float32)
+    return (own + beyond.astype(jnp.float32)).astype(jnp.bfloat16)
 
 
 def fits_head_split(mesh, w_in, gate_gain, dt_bias):

time: 351 us -> 346 us (0.986)
  waiting for transfers between devices: 161 us -> 151 us
  starting transfers between devices: 49.6 us -> 54.7 us
    ppermute x32 -> x35, waiting for transfers between devices: 152 us -> 143 us  [swap(): return lax.ppermute(value, axis, [(i, i ^ bit) for i in range(count)])]
    ppermute x32 -> x35, starting transfers between devices: 34.3 us -> 42.7 us  [swap(): return lax.ppermute(value, axis, [(i, i ^ bit) for i in range(count)])]
    concatenate x6 -> x10, other arithmetic: 10.2 us -> 13.7 us  [stack(): return jnp.concatenate(parts, axis=0)]
    unnamed x71 -> x84, local copies, waits for them, and re-layouts: 7.82 us -> 7.77 us
  transfers between devices with their start and end apart: 43 -> 46, of which waited for: 21 -> 28; matrix products, arithmetic and copies ran while one was open for 11% -> 10% of each run, Pallas kernels for 4% -> 4%
where the time goes in v5:
time: 346 us; the launch traced here: 345 us
  waiting for transfers between devices  151 us (44%)
  Pallas kernels  74.6 us (22%)
  starting transfers between devices  54.7 us (16%)
  other arithmetic  25.8 us (7%)
  local copies, waits for them, and re-layouts  23.9 us (7%)
  between operations  14.4 us (4%)
    ppermute x35, waiting for transfers between devices, swap(): return lax.ppermute(value, axis, [(i, i ^ bit) for i in range(count)])  143 us
    pallas_call x1, Pallas kernels, mixer(): pl.pallas_call(partial(mixer_kernel, cfg), out_shape=jax.ShapeDtypeStruct...  52.1 us
    ppermute x35, starting transfers between devices, swap(): return lax.ppermute(value, axis, [(i, i ^ bit) for i in range(count)])  42.7 us
    pallas_call x3, Pallas kernels, out_terms(): pl.pallas_call(partial(terms_kernel, (shards, chans, groups, order, keep,...  22.5 us
    concatenate x10, other arithmetic, stack(): return jnp.concatenate(parts, axis=0)  13.7 us
    ppermute x4, starting transfers between devices, line(): lax.ppermute(value, 'seq', [(2 * a + y, 2 * b + y) for a, b in pairs for...  11.6 us
    ppermute x4, waiting for transfers between devices, line(): lax.ppermute(value, 'seq', [(2 * a + y, 2 * b + y) for a, b in pairs for...  8.51 us
    unnamed x84, local copies, waits for them, and re-layouts  7.77 us
  transfers between devices with their start and end apart: 46, of which 28 were waited for; matrix products, arithmetic and copies ran while one was open for 10% of the time, Pallas kernels for 4%

profile of v5, /device:TPU:8, one launch (start us, length us, event | category | flops | bytes accessed | tf_op | source)
XLA Modules:
  0.0 344.7 jit_solution(6908596311470559188)
XLA Ops:
  10.0 4.6 %collective-permute-start.3 = (bf16[384,1024]{1,0:T(8,128)(2,1)}, bf16[384,1024]{1,0:T(8,128)(2,1)S(1)}, u32[]{:S(2)}, u32[]{:S(2)}) collective-permute-start(bf16[384,1024]{1,0:T(8,128)(2,1)} %param.11), channel_id=1, source_target_pairs={{8,16},{12,20},{16,8},{20,12},{9,17},{13,21},{17,9},{21,13},{10,18... | collective-permute-start | bytes 2359304 | tf_op jit(solution)/shard_map/ppermute | solution.py:373
  16.3 5.9 %constant_dynamic-slice_fusion.10 = (bf16[512,1,256]{2,1,0:T(2,128)(2,1)S(1)}, bf16[512,1,256]{2,1,0:T(2,128)(2,1)S(1)}, bf16[512,1,256]{2,1,0:T(2,128)(2,1)S(1)...) fusion(bf16[512,2,2304]{2,1,0:T(2,128)(2,1)} %param.13, s32[]{:T(128)S(6)} %select_n.248, s32[]{:T(128)S(6)} %select_n.243, ...), kind=kLoop, calls=%fused_computation.80 | loop fusion | bytes 2621468 | tf_op jit(solution)/shard_map/dynamic_slice | solution.py:478
  23.6 2.5 collective-permute-done
  28.6 2.9 collective-permute-done.3
  31.5 2.6 pad_maximum_fusion
  35.5 3.6 %collective-permute-start.6 = (bf16[384,1024]{1,0:T(8,128)(2,1)}, bf16[384,1024]{1,0:T(8,128)(2,1)S(1)}, u32[]{:S(2)}, u32[]{:S(2)}) collective-permute-start(bf16[384,1024]{1,0:T(8,128)(2,1)} %collective-permute-done.2), channel_id=1, source_target_pairs={{8,16},{12,20},{16,8},{20,12},{9,17},{13,21},{17,9},{21,13},{10,18... | collective-permute-start | bytes 2359304 | tf_op jit(solution)/shard_map/ppermute | solution.py:373
  39.2 3.5 %copy.35 = bf16[512,2,2304]{2,0,1:T(8,128)(2,1)S(1)} copy(bf16[512,2,2304]{2,1,0:T(2,128)(2,1)} %param.13) | data formatting | bytes 9437184 | tf_op jit(solution)/shard_map/optimization_barrier | solution.py:386
  49.4 3.1 collective-permute-done.4
  54.9 3.0 collective-permute-done.7
  60.5 2.6 pad_maximum_fusion.1
  63.2 2.8 collective-permute-start.13
  76.0 22.7 %collective-permute-done.10.refs_17_ = bf16[512,512]{1,0:T(8,128)(2,1)S(1)} collective-permute-done((bf16[512,512]{1,0:T(8,128)(2,1)}, bf16[512,512]{1,0:T(8,128)(2,1)S(1)}, u32[]{:S(2)}, u32[]{:S(2)}) %collective-permute-start.10) | collective-permute-done | bytes 524320 | tf_op jit(solution)/shard_map/ppermute | solution.py:21
  111.3 5.6 %collective-permute-done.17.refs_15_ = bf16[256,512]{1,0:T(8,128)(2,1)} collective-permute-done((bf16[256,512]{1,0:T(8,128)(2,1)}, bf16[256,512]{1,0:T(8,128)(2,1)}, u32[]{:S(2)}, u32[]{:S(2)}) %collective-permute-start.17) | collective-permute-done | bytes 262176 | tf_op jit(solution)/shard_map/ppermute | solution.py:21
  118.6 19.1 %collective-permute-done.16.refs_14_ = bf16[512,512]{1,0:T(8,128)(2,1)S(1)} collective-permute-done((bf16[512,512]{1,0:T(8,128)(2,1)S(1)}, bf16[512,512]{1,0:T(8,128)(2,1)S(1)}, u32[]{:S(2)}, u32[]{:S(2)}) %collective-permute-start.16) | collective-permute-done | bytes 524320 | tf_op jit(solution)/shard_map/ppermute | solution.py:21
  142.2 2.9 pad_maximum_fusion.3
  148.7 3.9 %collective-permute-start.22 = (bf16[512,512]{1,0:T(8,128)(2,1)}, bf16[512,512]{1,0:T(8,128)(2,1)S(1)}, u32[]{:S(2)}, u32[]{:S(2)}) collective-permute-start(bf16[512,512]{1,0:T(8,128)(2,1)} %pad_maximum_fusion.15), channel_id=1, source_target_pairs={{0,16},{4,20},{8,24},{12,28},{16,0},{20,4},{24,8},{28,12},{1,17},{... | collective-permute-start | bytes 1572872 | tf_op jit(solution)/shard_map/ppermute | solution.py:21
  152.6 16.4 %collective-permute-done.23.refs_16_ = bf16[256,512]{1,0:T(8,128)(2,1)} collective-permute-done((bf16[256,512]{1,0:T(8,128)(2,1)S(1)}, bf16[256,512]{1,0:T(8,128)(2,1)}, u32[]{:S(2)}, u32[]{:S(2)}) %collective-permute-start.23) | collective-permute-done | bytes 262176 | tf_op jit(solution)/shard_map/ppermute | solution.py:21
  169.1 7.3 %collective-permute-done.22.refs_13_ = bf16[512,512]{1,0:T(8,128)(2,1)S(1)} collective-permute-done((bf16[512,512]{1,0:T(8,128)(2,1)}, bf16[512,512]{1,0:T(8,128)(2,1)S(1)}, u32[]{:S(2)}, u32[]{:S(2)}) %collective-permute-start.22) | collective-permute-done | bytes 524320 | tf_op jit(solution)/shard_map/ppermute | solution.py:21
  176.4 5.8 %collective-permute-done.25.refs_12_ = bf16[512,512]{1,0:T(8,128)(2,1)S(1)} collective-permute-done((bf16[512,512]{1,0:T(8,128)(2,1)S(1)}, bf16[512,512]{1,0:T(8,128)(2,1)S(1)}, u32[]{:S(2)}, u32[]{:S(2)}) %collective-permute-start.25) | collective-permute-done | bytes 524320 | tf_op jit(solution)/shard_map/ppermute | solution.py:21
  185.3 3.0 collective-permute-start.28
  191.3 7.5 %collective-permute-done.27.refs_10_ = bf16[512,512]{1,0:T(8,128)(2,1)S(1)} collective-permute-done((bf16[512,512]{1,0:T(8,128)(2,1)}, bf16[512,512]{1,0:T(8,128)(2,1)S(1)}, u32[]{:S(2)}, u32[]{:S(2)}) %collective-permute-start.27) | collective-permute-done | bytes 524320 | tf_op jit(solution)/shard_map/ppermute | solution.py:21
  201.3 52.1 %shard_map.109 = bf16[3072,256]{1,0:T(8,128)(2,1)} custom-call(s32[10]{0:T(128)} %pad_add_fusion.where_ref, bf16[2,768,1024]{2,1,0:T(8,128)(2,1)} %bitcast.99, bf16[2,768,1024]{2,1,0:T(8,128)(2,1)} %bitcast.101, bf16[2,768,1024]{2,1,0:T(8,128)(2,1)} %bitcast.103, bf16[2,768,1024]{2,1,0:T(8,128)(2,1)} %bitcast.105, bf16[2,768,1024]{2,1,0:T(8,128)(2,1)} %bitcast.100, ...), custom_call_target="tpu_custom_call" | custom-call | flops 22548578304 | bytes 25165824 | tf_op jit(solution)/shard_map/pallas_call | solution.py:270
  263.8 6.0 %collective-permute-done.30.refs_2_ = bf16[384,256]{1,0:T(8,128)(2,1)S(1)} collective-permute-done((bf16[384,256]{1,0:T(8,128)(2,1)S(1)}, bf16[384,256]{1,0:T(8,128)(2,1)S(1)}, u32[]{:S(2)}, u32[]{:S(2)}) %collective-permute-start.30) | collective-permute-done | bytes 196640 | tf_op jit(solution)/shard_map/ppermute | solution.py:21
  272.1 11.7 %collective-permute-done.32.refs_4_ = bf16[384,256]{1,0:T(8,128)(2,1)S(1)} collective-permute-done((bf16[384,256]{1,0:T(8,128)(2,1)S(1)}, bf16[384,256]{1,0:T(8,128)(2,1)S(1)}, u32[]{:S(2)}, u32[]{:S(2)}) %collective-permute-start.32) | collective-permute-done | bytes 196640 | tf_op jit(solution)/shard_map/ppermute | solution.py:21
  283.8 4.2 %collective-permute-done.33.refs_5_ = bf16[384,256]{1,0:T(8,128)(2,1)S(1)} collective-permute-done((bf16[384,256]{1,0:T(8,128)(2,1)S(1)}, bf16[384,256]{1,0:T(8,128)(2,1)S(1)}, u32[]{:S(2)}, u32[]{:S(2)}) %collective-permute-start.33) | collective-permute-done | bytes 196640 | tf_op jit(solution)/shard_map/ppermute | solution.py:21
  288.0 5.1 %collective-permute-done.34.refs_6_ = bf16[384,256]{1,0:T(8,128)(2,1)S(1)} collective-permute-done((bf16[384,256]{1,0:T(8,128)(2,1)S(1)}, bf16[384,256]{1,0:T(8,128)(2,1)S(1)}, u32[]{:S(2)}, u32[]{:S(2)}) %collective-permute-start.34) | collective-permute-done | bytes 196640 | tf_op jit(solution)/shard_map/ppermute | solution.py:21
  293.0 2.5 collective-permute-done.35.refs_7_
  296.2 9.2 %shard_map.110 = (bf16[384,1024]{1,0:T(8,128)(2,1)}, bf16[384,1024]{1,0:T(8,128)(2,1)}, bf16[384,2048]{1,0:T(8,128)(2,1)}) custom-call(s32[10]{0:T(128)} %pad_add_fusion.where_ref, bf16[384,256]{1,0:T(8,128)(2,1)} %get-tuple-element.159.refs_0_, bf16[384,256]{1,0:T(8,128)(2,1)} %copy-done.24, bf16[384,256]{1,0:T(8,128)(2,1)} %copy-done.25, ...), custom_call_target="tpu_custom_call" | custom-call | flops 393216 | bytes 393216 | tf_op jit(solution)/shard_map/pallas_call | solution.py:354
  308.9 6.5 %shard_map.111 = bf16[384,1024]{1,0:T(8,128)(2,1)} custom-call(s32[10]{0:T(128)} %pad_add_fusion.where_ref, bf16[384,2048]{1,0:T(8,128)(2,1)} %get-tuple-element.132.refs_0_, bf16[384,1024]{1,0:T(8,128)(2,1)} %copy-done.5, bf16[2048,4096]{1,0:T(8,128)(2,1)} %bitcast.92), custom_call_target="tpu_custom_call" | custom-call | flops 393216 | bytes 393216 | tf_op jit(solution)/shard_map/pallas_call | solution.py:354
  317.9 6.8 %shard_map.112 = f32[384,1024]{1,0:T(8,128)} custom-call(s32[10]{0:T(128)} %pad_add_fusion.where_ref, bf16[384,2048]{1,0:T(8,128)(2,1)} %get-tuple-element.132.refs_0_, bf16[384,1024]{1,0:T(8,128)(2,1)} %copy-done.4, bf16[2048,4096]{1,0:T(8,128)(2,1)} %bitcast.93), custom_call_target="tpu_custom_call" | custom-call | flops 393216 | bytes 393216 | tf_op jit(solution)/shard_map/pallas_call | solution.py:354
  324.7 10.6 %collective-permute-done.38 = bf16[384,1024]{1,0:T(8,128)(2,1)S(1)} collective-permute-done((bf16[384,1024]{1,0:T(8,128)(2,1)}, bf16[384,1024]{1,0:T(8,128)(2,1)S(1)}, u32[]{:S(2)}, u32[]{:S(2)}) %collective-permute-start.38) | collective-permute-done | bytes 786464 | tf_op jit(solution)/shard_map/ppermute | solution.py:21
  335.3 2.6 add_convert_fusion
  (202 shorter events, 81.8 us)
Async XLA Ops:
  6.5 184.8 %all-gather.15.cloned.1.call-start = ((), (), s32[]{:S(2)}) async-start(), calls=%async_computation | async-start | bytes 4718592 | tf_op jit(solution)/shard_map/all_gather | solution.py:382
  6.5 19.5 %collective-permute-start = (bf16[384,1024]{1,0:T(8,128)(2,1)}, bf16[384,1024]{1,0:T(8,128)(2,1)S(1)}, u32[]{:S(2)}, u32[]{:S(2)}) collective-permute-start(bf16[384,1024]{1,0:T(8,128)(2,1)} %param.11), channel_id=1, source_target_pairs={{0,2},{1,3},{2,0},{3,1},{4,6},{5,7},{6,4},{7,5},{8,10},{9,11},{10,... | collective-permute-start | bytes 2359304 | tf_op jit(solution)/shard_map/ppermute | solution.py:21
  8.0 19.3 %collective-permute-start.1 = (bf16[384,1024]{1,0:T(8,128)(2,1)}, bf16[384,1024]{1,0:T(8,128)(2,1)}, u32[]{:S(2)}, u32[]{:S(2)}) collective-permute-start(bf16[384,1024]{1,0:T(8,128)(2,1)} %param.11), channel_id=1, source_target_pairs={{0,4},{4,0},{8,12},{12,8},{16,20},{20,16},{24,28},{28,24},{1,5},{5... | collective-permute-start | bytes 2359304 | tf_op jit(solution)/shard_map/ppermute | solution.py:21
  9.6 19.0 %collective-permute-start.2 = (bf16[384,1024]{1,0:T(8,128)(2,1)}, bf16[384,1024]{1,0:T(8,128)(2,1)}, u32[]{:S(2)}, u32[]{:S(2)}) collective-permute-start(bf16[384,1024]{1,0:T(8,128)(2,1)} %param.11), channel_id=1, source_target_pairs={{0,8},{4,12},{8,0},{12,4},{16,24},{20,28},{24,16},{28,20},{1,9},{5... | collective-permute-start | bytes 2359304 | tf_op jit(solution)/shard_map/ppermute | solution.py:21
  10.0 21.5 %collective-permute-start.3 = (bf16[384,1024]{1,0:T(8,128)(2,1)}, bf16[384,1024]{1,0:T(8,128)(2,1)S(1)}, u32[]{:S(2)}, u32[]{:S(2)}) collective-permute-start(bf16[384,1024]{1,0:T(8,128)(2,1)} %param.11), channel_id=1, source_target_pairs={{8,16},{12,20},{16,8},{20,12},{9,17},{13,21},{17,9},{21,13},{10,18... | collective-permute-start | bytes 2359304 | tf_op jit(solution)/shard_map/ppermute | solution.py:373
  34.1 157.2 %all-gather.23.cloned.1.call-start = ((), (), s32[]{:S(2)}) async-start(), calls=%async_computation.4 | async-start | bytes 4718592 | tf_op jit(solution)/shard_map/all_gather | solution.py:382
  35.5 19.3 %collective-permute-start.6 = (bf16[384,1024]{1,0:T(8,128)(2,1)}, bf16[384,1024]{1,0:T(8,128)(2,1)S(1)}, u32[]{:S(2)}, u32[]{:S(2)}) collective-permute-start(bf16[384,1024]{1,0:T(8,128)(2,1)} %collective-permute-done.2), channel_id=1, source_target_pairs={{8,16},{12,20},{16,8},{20,12},{9,17},{13,21},{17,9},{21,13},{10,18... | collective-permute-start | bytes 2359304 | tf_op jit(solution)/shard_map/ppermute | solution.py:373
  59.3 132.0 %all-gather.17.cloned.1.call-start = ((), (), s32[]{:S(2)}) async-start(), calls=%async_computation.1 | async-start | bytes 4718592 | tf_op jit(solution)/shard_map/all_gather | solution.py:382
  63.1 137.4 %all-gather.25.cloned.1.call-start = ((), (), s32[]{:S(2)}) async-start(), calls=%async_computation.5 | async-start | bytes 4718592 | tf_op jit(solution)/shard_map/all_gather | solution.py:382
  66.0 32.7 %collective-permute-start.11 = (bf16[384,1024]{1,0:T(8,128)(2,1)S(1)}, bf16[384,1024]{1,0:T(8,128)(2,1)S(1)}, u32[]{:S(2)}, u32[]{:S(2)}) collective-permute-start(bf16[384,1024]{1,0:T(8,128)(2,1)S(1)} %broadcast_select_fusion.1), channel_id=1, source_target_pairs={{0,4},{4,0},{8,12},{12,8},{16,20},{20,16},{24,28},{28,24},{1,5},{5... | collective-permute-start | bytes 2359304 | tf_op jit(solution)/shard_map/ppermute | solution.py:21
  67.5 31.7 %collective-permute-start.12 = (bf16[384,1024]{1,0:T(8,128)(2,1)S(1)}, bf16[384,1024]{1,0:T(8,128)(2,1)S(1)}, u32[]{:S(2)}, u32[]{:S(2)}) collective-permute-start(bf16[384,1024]{1,0:T(8,128)(2,1)S(1)} %collective-permute-done.6), channel_id=1, source_target_pairs={{8,0},{12,4},{16,24},{20,28},{9,1},{13,5},{17,25},{21,29},{10,2},{... | collective-permute-start | bytes 2359304 | tf_op jit(solution)/shard_map/ppermute | solution.py:373
  69.5 30.1 %collective-permute-start.8 = (bf16[384,1024]{1,0:T(8,128)(2,1)}, bf16[384,1024]{1,0:T(8,128)(2,1)S(1)}, u32[]{:S(2)}, u32[]{:S(2)}) collective-permute-start(bf16[384,1024]{1,0:T(8,128)(2,1)} %collective-permute-done.2), channel_id=1, source_target_pairs={{0,2},{1,3},{2,0},{3,1},{4,6},{5,7},{6,4},{7,5},{8,10},{9,11},{10,... | collective-permute-start | bytes 2359304 | tf_op jit(solution)/shard_map/ppermute | solution.py:21
  71.1 30.4 %collective-permute-start.9 = (bf16[384,1024]{1,0:T(8,128)(2,1)}, bf16[384,1024]{1,0:T(8,128)(2,1)S(1)}, u32[]{:S(2)}, u32[]{:S(2)}) collective-permute-start(bf16[384,1024]{1,0:T(8,128)(2,1)} %copy-done.11), channel_id=1, source_target_pairs={{0,2},{1,3},{2,0},{3,1},{4,6},{5,7},{6,4},{7,5},{8,10},{9,11},{10,... | collective-permute-start | bytes 2359304 | tf_op jit(solution)/shard_map/ppermute | solution.py:21
  73.8 24.8 %collective-permute-start.10 = (bf16[512,512]{1,0:T(8,128)(2,1)}, bf16[512,512]{1,0:T(8,128)(2,1)S(1)}, u32[]{:S(2)}, u32[]{:S(2)}) collective-permute-start(bf16[512,512]{1,0:T(8,128)(2,1)} %get-tuple-element.82), channel_id=1, source_target_pairs={{0,28},{4,24},{8,20},{12,16},{16,12},{20,8},{24,4},{28,0},{1,29},{... | collective-permute-start | bytes 1572872 | tf_op jit(solution)/shard_map/ppermute | solution.py:21
  102.9 97.6 %all-gather.19.cloned.1.call-start = ((), (), s32[]{:S(2)}) async-start(), calls=%async_computation.2 | async-start | bytes 4718592 | tf_op jit(solution)/shard_map/all_gather | solution.py:382
  106.3 94.3 %all-gather.27.cloned.1.call-start = ((), (), s32[]{:S(2)}) async-start(), calls=%async_computation.6 | async-start | bytes 4718592 | tf_op jit(solution)/shard_map/all_gather | solution.py:382
  107.3 30.4 %collective-permute-start.14 = (bf16[384,1024]{1,0:T(8,128)(2,1)S(1)}, bf16[384,1024]{1,0:T(8,128)(2,1)S(1)}, u32[]{:S(2)}, u32[]{:S(2)}) collective-permute-start(bf16[384,1024]{1,0:T(8,128)(2,1)S(1)} %broadcast_select_fusion.1), channel_id=1, source_target_pairs={{0,2},{1,3},{2,0},{3,1},{4,6},{5,7},{6,4},{7,5},{8,10},{9,11},{10,... | collective-permute-start | bytes 2359304 | tf_op jit(solution)/shard_map/ppermute | solution.py:21
  108.8 30.9 %collective-permute-start.15 = (bf16[384,1024]{1,0:T(8,128)(2,1)S(1)}, bf16[384,1024]{1,0:T(8,128)(2,1)S(1)}, u32[]{:S(2)}, u32[]{:S(2)}) collective-permute-start(bf16[384,1024]{1,0:T(8,128)(2,1)S(1)} %copy-done.15), channel_id=1, source_target_pairs={{0,2},{1,3},{2,0},{3,1},{4,6},{5,7},{6,4},{7,5},{8,10},{9,11},{10,... | collective-permute-start | bytes 2359304 | tf_op jit(solution)/shard_map/ppermute | solution.py:21
  109.3 30.4 %collective-permute-start.18 = (bf16[384,1024]{1,0:T(8,128)(2,1)S(1)}, bf16[384,1024]{1,0:T(8,128)(2,1)}, u32[]{:S(2)}, u32[]{:S(2)}) collective-permute-start(bf16[384,1024]{1,0:T(8,128)(2,1)S(1)} %broadcast_select_fusion), channel_id=1, source_target_pairs={{0,4},{4,0},{8,12},{12,8},{16,20},{20,16},{24,28},{28,24},{1,5},{5... | collective-permute-start | bytes 2359304 | tf_op jit(solution)/shard_map/ppermute | solution.py:21
  109.8 27.9 %collective-permute-start.19 = (bf16[1088,256]{1,0:T(8,128)(2,1)S(1)}, bf16[1088,256]{1,0:T(8,128)(2,1)S(1)}, u32[]{:S(2)}, u32[]{:S(2)}) collective-permute-start(bf16[1088,256]{1,0:T(8,128)(2,1)S(1)} %pad_maximum_fusion.9), channel_id=1, source_target_pairs={{0,8},{4,12},{8,0},{12,4},{16,24},{20,28},{24,16},{28,20},{1,9},{5... | collective-permute-start | bytes 1671176 | tf_op jit(solution)/shard_map/ppermute | solution.py:21
  116.9 20.8 %collective-permute-start.16 = (bf16[512,512]{1,0:T(8,128)(2,1)S(1)}, bf16[512,512]{1,0:T(8,128)(2,1)S(1)}, u32[]{:S(2)}, u32[]{:S(2)}) collective-permute-start(bf16[512,512]{1,0:T(8,128)(2,1)S(1)} %copy-done.20), channel_id=1, source_target_pairs={{0,20},{4,16},{8,28},{12,24},{16,4},{20,0},{24,12},{28,8},{1,21},{... | collective-permute-start | bytes 1572872 | tf_op jit(solution)/shard_map/ppermute | solution.py:21
  141.0 59.5 %all-gather.21.cloned.1.call-start = ((), (), s32[]{:S(2)}) async-start(), calls=%async_computation.3 | async-start | bytes 4718592 | tf_op jit(solution)/shard_map/all_gather | solution.py:382
  145.2 37.8 %collective-permute-start.24 = (bf16[2176,256]{1,0:T(8,128)(2,1)S(1)}, bf16[2176,256]{1,0:T(8,128)(2,1)}, u32[]{:S(2)}, u32[]{:S(2)}) collective-permute-start(bf16[2176,256]{1,0:T(8,128)(2,1)S(1)} %pad_maximum_fusion.8.refs_18_), channel_id=1, source_target_pairs={{0,4},{4,0},{8,12},{12,8},{16,20},{20,16},{24,28},{28,24},{1,5},{5... | collective-permute-start | bytes 3342344 | tf_op jit(solution)/shard_map/ppermute | solution.py:21
  146.0 23.1 %collective-permute-start.23 = (bf16[256,512]{1,0:T(8,128)(2,1)S(1)}, bf16[256,512]{1,0:T(8,128)(2,1)}, u32[]{:S(2)}, u32[]{:S(2)}) collective-permute-start(bf16[256,512]{1,0:T(8,128)(2,1)S(1)} %copy-done.23), channel_id=1, source_target_pairs={{0,24},{4,28},{8,16},{12,20},{16,8},{20,12},{24,0},{28,4},{1,25},{... | collective-permute-start | bytes 786440 | tf_op jit(solution)/shard_map/ppermute | solution.py:21
  146.7 35.4 %collective-permute-start.20 = (bf16[384,1024]{1,0:T(8,128)(2,1)S(1)}, bf16[384,1024]{1,0:T(8,128)(2,1)S(1)}, u32[]{:S(2)}, u32[]{:S(2)}) collective-permute-start(bf16[384,1024]{1,0:T(8,128)(2,1)S(1)} %broadcast_select_fusion), channel_id=1, source_target_pairs={{0,2},{1,3},{2,0},{3,1},{4,6},{5,7},{6,4},{7,5},{8,10},{9,11},{10,... | collective-permute-start | bytes 2359304 | tf_op jit(solution)/shard_map/ppermute | solution.py:21
  148.2 33.9 %collective-permute-start.21 = (bf16[384,1024]{1,0:T(8,128)(2,1)}, bf16[384,1024]{1,0:T(8,128)(2,1)S(1)}, u32[]{:S(2)}, u32[]{:S(2)}) collective-permute-start(bf16[384,1024]{1,0:T(8,128)(2,1)} %collective-permute-done.18), channel_id=1, source_target_pairs={{0,2},{1,3},{2,0},{3,1},{4,6},{5,7},{6,4},{7,5},{8,10},{9,11},{10,... | collective-permute-start | bytes 2359304 | tf_op jit(solution)/shard_map/ppermute | solution.py:21
  148.7 27.6 %collective-permute-start.22 = (bf16[512,512]{1,0:T(8,128)(2,1)}, bf16[512,512]{1,0:T(8,128)(2,1)S(1)}, u32[]{:S(2)}, u32[]{:S(2)}) collective-permute-start(bf16[512,512]{1,0:T(8,128)(2,1)} %pad_maximum_fusion.15), channel_id=1, source_target_pairs={{0,16},{4,20},{8,24},{12,28},{16,0},{20,4},{24,8},{28,12},{1,17},{... | collective-permute-start | bytes 1572872 | tf_op jit(solution)/shard_map/ppermute | solution.py:21
  259.1 24.6 %collective-permute-start.32 = (bf16[384,256]{1,0:T(8,128)(2,1)S(1)}, bf16[384,256]{1,0:T(8,128)(2,1)S(1)}, u32[]{:S(2)}, u32[]{:S(2)}) collective-permute-start(bf16[384,256]{1,0:T(8,128)(2,1)S(1)} %get-tuple-element.155), channel_id=1, source_target_pairs={{0,16},{4,20},{8,24},{12,28},{16,0},{20,4},{24,8},{28,12},{1,17},{... | collective-permute-start | bytes 589832 | tf_op jit(solution)/shard_map/ppermute | solution.py:21
  261.6 26.4 %collective-permute-start.33 = (bf16[384,256]{1,0:T(8,128)(2,1)S(1)}, bf16[384,256]{1,0:T(8,128)(2,1)S(1)}, u32[]{:S(2)}, u32[]{:S(2)}) collective-permute-start(bf16[384,256]{1,0:T(8,128)(2,1)S(1)} %get-tuple-element.154), channel_id=1, source_target_pairs={{0,20},{4,16},{8,28},{12,24},{16,4},{20,0},{24,12},{28,8},{1,21},{... | collective-permute-start | bytes 589832 | tf_op jit(solution)/shard_map/ppermute | solution.py:21
  262.6 30.5 %collective-permute-start.34 = (bf16[384,256]{1,0:T(8,128)(2,1)S(1)}, bf16[384,256]{1,0:T(8,128)(2,1)S(1)}, u32[]{:S(2)}, u32[]{:S(2)}) collective-permute-start(bf16[384,256]{1,0:T(8,128)(2,1)S(1)} %get-tuple-element.153), channel_id=1, source_target_pairs={{0,24},{4,28},{8,16},{12,20},{16,8},{20,12},{24,0},{28,4},{1,25},{... | collective-permute-start | bytes 589832 | tf_op jit(solution)/shard_map/ppermute | solution.py:21
  269.8 25.8 %collective-permute-start.35 = (bf16[384,256]{1,0:T(8,128)(2,1)S(1)}, bf16[384,256]{1,0:T(8,128)(2,1)S(1)}, u32[]{:S(2)}, u32[]{:S(2)}) collective-permute-start(bf16[384,256]{1,0:T(8,128)(2,1)S(1)} %get-tuple-element.152), channel_id=1, source_target_pairs={{0,28},{4,24},{8,20},{12,16},{16,12},{20,8},{24,4},{28,0},{1,29},{... | collective-permute-start | bytes 589832 | tf_op jit(solution)/shard_map/ppermute | solution.py:21
  315.4 19.9 %collective-permute-start.38 = (bf16[384,1024]{1,0:T(8,128)(2,1)}, bf16[384,1024]{1,0:T(8,128)(2,1)S(1)}, u32[]{:S(2)}, u32[]{:S(2)}) collective-permute-start(bf16[384,1024]{1,0:T(8,128)(2,1)} %shard_map.111), channel_id=1, source_target_pairs={{0,2},{1,3},{2,0},{3,1},{4,6},{5,7},{6,4},{7,5},{8,10},{9,11},{10,... | collective-permute-start | bytes 2359304 | tf_op jit(solution)/shard_map/ppermute | solution.py:21
  (55 other events, 797.8 us)
Sparse Core Ops, SparseCore 0:
  34.3 10.7 all-gather.14
  59.4 13.4 all-gather.22
  74.5 13.2 all-gather.16
  103.0 10.8 all-gather.24
  115.3 13.2 all-gather.18
  141.2 13.2 all-gather.26
  156.0 13.2 all-gather.20

commit v6 on v5

--- a/solution.py
+++ b/solution.py
@@ -413,18 +413,18 @@
         weights_of(w_in, (2, 6, 5, 4, 3, 0, "own")),
     )
     q1 = jnp.where(middle, c0, o0)
-    q1, z1, yz1, c1, m7, far_map = together(q1, z1, yz1, c1, m7, far_map)
-    xz1, xyz1, w7, yq1, o1, far_map = together(
-        x_swap(z1), x_swap(yz1), s_swap(m7, 7), s_swap(q1, 1), line(c1, outward), s_swap(far_map, 4)
+    q1, z1, yz1, c1, m7, far_map, m1 = together(q1, z1, yz1, c1, m7, far_map, m1)
+    xz1, xyz1, w1, w7, yq1, o1, far_map = together(
+        x_swap(z1), x_swap(yz1), s_swap(m1, 1), s_swap(m7, 7), s_swap(q1, 1), line(c1, outward), s_swap(far_map, 4)
     )
     own = [stack(tokens, y0), stack(z1, yz1)]
     across = [stack(xp, xy), stack(xz1, xyz1)]
     q2 = jnp.where(middle, c1, o1)
     maps = stack(own_map, far_map)
     half = m6.shape[0] // 2
-    q2, q1, yq1, maps, m5, m6a, m6b = together(q2, q1, yq1, maps, m5, m6[:half], m6[half:])
-    xq1, xyq1, w5, w6a, yq2, maps_z = together(
-        x_swap(q1), x_swap(yq1), s_swap(m5, 5), s_swap(m6a, 6), s_swap(q2, 1), s_swap(maps, 2)
+    q2, q1, yq1, maps, m5, m6a, m6b, m2 = together(q2, q1, yq1, maps, m5, m6[:half], m6[half:], m2)
+    xq1, xyq1, w2, w5, w6a, yq2, maps_z = together(
+        x_swap(q1), x_swap(yq1), s_swap(m2, 2), s_swap(m5, 5), s_swap(m6a, 6), s_swap(q2, 1), s_swap(maps, 2)
     )
     maps = stack(maps, maps_z)
     q2, yq2, maps, m4, m6b, m3 = together(q2, yq2, maps, m4, m6b, m3)
@@ -435,8 +435,6 @@
     across += [stack(xq1, xyq1)]
     xa3 = stack(xq2, xyq2)
     gathered = [both_cores(v) for v in own + across]
-    m1, m2, xa3, w3 = together(m1, m2, xa3, w3)
-    w1, w2 = s_swap(m1, 1), s_swap(m2, 2)
     last = (xa3, swap(xa3, "head", 1))
     mains = [m0, w1, w2, w3, w4, w5, (w6a, w6b), w7]
     place = {0: 0, 4: 1, 2: 2, 6: 3}

time: 346 us -> 342 us (0.988)
  waiting for transfers between devices: 151 us -> 135 us
  starting transfers between devices: 54.7 us -> 67.1 us
    ppermute x35, waiting for transfers between devices: 143 us -> 127 us  [swap(): return lax.ppermute(value, axis, [(i, i ^ bit) for i in range(count)])]
    ppermute x35, starting transfers between devices: 42.7 us -> 55.1 us  [swap(): return lax.ppermute(value, axis, [(i, i ^ bit) for i in range(count)])]
    unnamed x84 -> x81, local copies, waits for them, and re-layouts: 7.77 us -> 8 us
    concatenate x10 -> x9, other arithmetic: 13.7 us -> 13.7 us  [stack(): return jnp.concatenate(parts, axis=0)]
  transfers between devices with their start and end apart: 46 -> 46, of which waited for: 28 -> 25; matrix products, arithmetic and copies ran while one was open for 10% -> 10% of each run, Pallas kernels for 4% -> 4%
where the time goes in v6:
time: 342 us; the launch traced here: 341 us
  waiting for transfers between devices  135 us (39%)
  Pallas kernels  74.7 us (22%)
  starting transfers between devices  67.1 us (20%)
  other arithmetic  25.8 us (8%)
  local copies, waits for them, and re-layouts  24.2 us (7%)
  between operations  14.4 us (4%)
    ppermute x35, waiting for transfers between devices, swap(): return lax.ppermute(value, axis, [(i, i ^ bit) for i in range(count)])  127 us
    ppermute x35, starting transfers between devices, swap(): return lax.ppermute(value, axis, [(i, i ^ bit) for i in range(count)])  55.1 us
    pallas_call x1, Pallas kernels, mixer(): pl.pallas_call(partial(mixer_kernel, cfg), out_shape=jax.ShapeDtypeStruct...  52.1 us
    pallas_call x3, Pallas kernels, out_terms(): pl.pallas_call(partial(terms_kernel, (shards, chans, groups, order, keep,...  22.5 us
    concatenate x9, other arithmetic, stack(): return jnp.concatenate(parts, axis=0)  13.7 us
    ppermute x4, starting transfers between devices, line(): lax.ppermute(value, 'seq', [(2 * a + y, 2 * b + y) for a, b in pairs for...  11.6 us
    unnamed x81, local copies, waits for them, and re-layouts  8 us
    ppermute x4, waiting for transfers between devices, line(): lax.ppermute(value, 'seq', [(2 * a + y, 2 * b + y) for a, b in pairs for...  8 us
  transfers between devices with their start and end apart: 46, of which 25 were waited for; matrix products, arithmetic and copies ran while one was open for 10% of the time, Pallas kernels for 4%

profile of v6, /device:TPU:8, one launch (start us, length us, event | category | flops | bytes accessed | tf_op | source)
XLA Modules:
  0.0 341.4 jit_solution(15375362757052937487)
XLA Ops:
  10.0 4.6 %collective-permute-start.3 = (bf16[384,1024]{1,0:T(8,128)(2,1)}, bf16[384,1024]{1,0:T(8,128)(2,1)S(1)}, u32[]{:S(2)}, u32[]{:S(2)}) collective-permute-start(bf16[384,1024]{1,0:T(8,128)(2,1)} %param.11), channel_id=1, source_target_pairs={{8,16},{12,20},{16,8},{20,12},{9,17},{13,21},{17,9},{21,13},{10,18... | collective-permute-start | bytes 2359304 | tf_op jit(solution)/shard_map/ppermute | solution.py:373
  16.3 5.9 %constant_dynamic-slice_fusion.10 = (bf16[512,1,256]{2,1,0:T(2,128)(2,1)S(1)}, bf16[512,1,256]{2,1,0:T(2,128)(2,1)S(1)}, bf16[512,1,256]{2,1,0:T(2,128)(2,1)S(1)...) fusion(bf16[512,2,2304]{2,1,0:T(2,128)(2,1)} %param.13, s32[]{:T(128)S(6)} %select_n.248, s32[]{:T(128)S(6)} %select_n.243, ...), kind=kLoop, calls=%fused_computation.79 | loop fusion | bytes 2621468 | tf_op jit(solution)/shard_map/dynamic_slice | solution.py:476
  28.6 2.9 collective-permute-done.3
  35.5 3.6 %collective-permute-start.6 = (bf16[384,1024]{1,0:T(8,128)(2,1)}, bf16[384,1024]{1,0:T(8,128)(2,1)S(1)}, u32[]{:S(2)}, u32[]{:S(2)}) collective-permute-start(bf16[384,1024]{1,0:T(8,128)(2,1)} %collective-permute-done.2), channel_id=1, source_target_pairs={{8,16},{12,20},{16,8},{20,12},{9,17},{13,21},{17,9},{21,13},{10,18... | collective-permute-start | bytes 2359304 | tf_op jit(solution)/shard_map/ppermute | solution.py:373
  39.2 3.5 %copy.35 = bf16[512,2,2304]{2,0,1:T(8,128)(2,1)S(1)} copy(bf16[512,2,2304]{2,1,0:T(2,128)(2,1)} %param.13) | data formatting | bytes 9437184 | tf_op jit(solution)/shard_map/optimization_barrier | solution.py:386
  49.4 3.1 collective-permute-done.4
  54.8 3.0 collective-permute-done.7
  63.1 2.8 collective-permute-start.14
  75.2 9.2 %collective-permute-done.10.refs_10_ = bf16[512,512]{1,0:T(8,128)(2,1)S(1)} collective-permute-done((bf16[512,512]{1,0:T(8,128)(2,1)}, bf16[512,512]{1,0:T(8,128)(2,1)S(1)}, u32[]{:S(2)}, u32[]{:S(2)}) %collective-permute-start.10) | collective-permute-done | bytes 524320 | tf_op jit(solution)/shard_map/ppermute | solution.py:21
  86.7 12.8 %collective-permute-done.11.refs_17_ = bf16[512,512]{1,0:T(8,128)(2,1)S(1)} collective-permute-done((bf16[512,512]{1,0:T(8,128)(2,1)}, bf16[512,512]{1,0:T(8,128)(2,1)S(1)}, u32[]{:S(2)}, u32[]{:S(2)}) %collective-permute-start.11) | collective-permute-done | bytes 524320 | tf_op jit(solution)/shard_map/ppermute | solution.py:21
  99.5 4.6 %collective-permute-done.12 = bf16[384,1024]{1,0:T(8,128)(2,1)S(1)} collective-permute-done((bf16[384,1024]{1,0:T(8,128)(2,1)S(1)}, bf16[384,1024]{1,0:T(8,128)(2,1)S(1)}, u32[]{:S(2)}, u32[]{:S(2)}) %collective-permute-start.12) | collective-permute-done | bytes 786464 | tf_op jit(solution)/shard_map/ppermute | solution.py:21
  114.7 3.6 %collective-permute-done.19.refs_15_ = bf16[256,512]{1,0:T(8,128)(2,1)} collective-permute-done((bf16[256,512]{1,0:T(8,128)(2,1)}, bf16[256,512]{1,0:T(8,128)(2,1)}, u32[]{:S(2)}, u32[]{:S(2)}) %collective-permute-start.19) | collective-permute-done | bytes 262176 | tf_op jit(solution)/shard_map/ppermute | solution.py:21
  118.3 11.9 %collective-permute-start.21 = (bf16[1088,256]{1,0:T(8,128)(2,1)S(1)}, bf16[1088,256]{1,0:T(8,128)(2,1)S(1)}, u32[]{:S(2)}, u32[]{:S(2)}) collective-permute-start(bf16[1088,256]{1,0:T(8,128)(2,1)S(1)} %pad_maximum_fusion.8), channel_id=1, source_target_pairs={{0,8},{4,12},{8,0},{12,4},{16,24},{20,28},{24,16},{28,20},{1,9},{5... | collective-permute-start | bytes 1671176 | tf_op jit(solution)/shard_map/ppermute | solution.py:21
  130.5 3.7 %collective-permute-start.18 = (bf16[512,512]{1,0:T(8,128)(2,1)S(1)}, bf16[512,512]{1,0:T(8,128)(2,1)S(1)}, u32[]{:S(2)}, u32[]{:S(2)}) collective-permute-start(bf16[512,512]{1,0:T(8,128)(2,1)S(1)} %copy-done.18), channel_id=1, source_target_pairs={{0,20},{4,16},{8,28},{12,24},{16,4},{20,0},{24,12},{28,8},{1,21},{... | collective-permute-start | bytes 1572872 | tf_op jit(solution)/shard_map/ppermute | solution.py:21
  134.2 13.8 %collective-permute-done.18.refs_14_ = bf16[512,512]{1,0:T(8,128)(2,1)S(1)} collective-permute-done((bf16[512,512]{1,0:T(8,128)(2,1)S(1)}, bf16[512,512]{1,0:T(8,128)(2,1)S(1)}, u32[]{:S(2)}, u32[]{:S(2)}) %collective-permute-start.18) | collective-permute-done | bytes 524320 | tf_op jit(solution)/shard_map/ppermute | solution.py:21
  151.5 2.9 pad_maximum_fusion.3
  158.3 4.7 %collective-permute-start.24 = (bf16[512,512]{1,0:T(8,128)(2,1)}, bf16[512,512]{1,0:T(8,128)(2,1)S(1)}, u32[]{:S(2)}, u32[]{:S(2)}) collective-permute-start(bf16[512,512]{1,0:T(8,128)(2,1)} %pad_maximum_fusion.14), channel_id=1, source_target_pairs={{0,16},{4,20},{8,24},{12,28},{16,0},{20,4},{24,8},{28,12},{1,17},{... | collective-permute-start | bytes 1572872 | tf_op jit(solution)/shard_map/ppermute | solution.py:21
  163.0 14.4 %collective-permute-done.25.refs_16_ = bf16[256,512]{1,0:T(8,128)(2,1)} collective-permute-done((bf16[256,512]{1,0:T(8,128)(2,1)}, bf16[256,512]{1,0:T(8,128)(2,1)}, u32[]{:S(2)}, u32[]{:S(2)}) %collective-permute-start.25) | collective-permute-done | bytes 262176 | tf_op jit(solution)/shard_map/ppermute | solution.py:21
  177.4 7.3 %collective-permute-done.24.refs_13_ = bf16[512,512]{1,0:T(8,128)(2,1)S(1)} collective-permute-done((bf16[512,512]{1,0:T(8,128)(2,1)}, bf16[512,512]{1,0:T(8,128)(2,1)S(1)}, u32[]{:S(2)}, u32[]{:S(2)}) %collective-permute-start.24) | collective-permute-done | bytes 524320 | tf_op jit(solution)/shard_map/ppermute | solution.py:21
  184.7 5.5 %collective-permute-done.27.refs_12_ = bf16[512,512]{1,0:T(8,128)(2,1)S(1)} collective-permute-done((bf16[512,512]{1,0:T(8,128)(2,1)S(1)}, bf16[512,512]{1,0:T(8,128)(2,1)S(1)}, u32[]{:S(2)}, u32[]{:S(2)}) %collective-permute-start.27) | collective-permute-done | bytes 524320 | tf_op jit(solution)/shard_map/ppermute | solution.py:21
  195.6 52.1 %shard_map.109 = bf16[3072,256]{1,0:T(8,128)(2,1)} custom-call(s32[10]{0:T(128)} %pad_add_fusion.where_ref, bf16[2,768,1024]{2,1,0:T(8,128)(2,1)} %bitcast.99, bf16[2,768,1024]{2,1,0:T(8,128)(2,1)} %bitcast.101, bf16[2,768,1024]{2,1,0:T(8,128)(2,1)} %bitcast.103, bf16[2,768,1024]{2,1,0:T(8,128)(2,1)} %bitcast.105, bf16[2,768,1024]{2,1,0:T(8,128)(2,1)} %bitcast.100, ...), custom_call_target="tpu_custom_call" | custom-call | flops 22548578304 | bytes 25165824 | tf_op jit(solution)/shard_map/pallas_call | solution.py:270
  250.4 3.5 %collective-permute-start.30 = (bf16[384,256]{1,0:T(8,128)(2,1)S(1)}, bf16[384,256]{1,0:T(8,128)(2,1)S(1)}, u32[]{:S(2)}, u32[]{:S(2)}) collective-permute-start(bf16[384,256]{1,0:T(8,128)(2,1)S(1)} %get-tuple-element.157), channel_id=1, source_target_pairs={{0,8},{4,12},{8,0},{12,4},{16,24},{20,28},{24,16},{28,20},{1,9},{5... | collective-permute-start | bytes 589832 | tf_op jit(solution)/shard_map/ppermute | solution.py:21
  253.9 2.7 collective-permute-start.32
  259.3 6.9 %collective-permute-done.30.refs_2_ = bf16[384,256]{1,0:T(8,128)(2,1)S(1)} collective-permute-done((bf16[384,256]{1,0:T(8,128)(2,1)S(1)}, bf16[384,256]{1,0:T(8,128)(2,1)S(1)}, u32[]{:S(2)}, u32[]{:S(2)}) %collective-permute-start.30) | collective-permute-done | bytes 196640 | tf_op jit(solution)/shard_map/ppermute | solution.py:21
  266.9 2.7 collective-permute-done.31.refs_3_
  269.6 13.4 %collective-permute-done.33.refs_5_ = bf16[384,256]{1,0:T(8,128)(2,1)S(1)} collective-permute-done((bf16[384,256]{1,0:T(8,128)(2,1)S(1)}, bf16[384,256]{1,0:T(8,128)(2,1)S(1)}, u32[]{:S(2)}, u32[]{:S(2)}) %collective-permute-start.33) | collective-permute-done | bytes 196640 | tf_op jit(solution)/shard_map/ppermute | solution.py:21
  283.1 5.2 %collective-permute-done.34.refs_6_ = bf16[384,256]{1,0:T(8,128)(2,1)S(1)} collective-permute-done((bf16[384,256]{1,0:T(8,128)(2,1)S(1)}, bf16[384,256]{1,0:T(8,128)(2,1)S(1)}, u32[]{:S(2)}, u32[]{:S(2)}) %collective-permute-start.34) | collective-permute-done | bytes 196640 | tf_op jit(solution)/shard_map/ppermute | solution.py:21
  288.3 3.9 %collective-permute-done.35.refs_7_ = bf16[384,256]{1,0:T(8,128)(2,1)S(1)} collective-permute-done((bf16[384,256]{1,0:T(8,128)(2,1)S(1)}, bf16[384,256]{1,0:T(8,128)(2,1)S(1)}, u32[]{:S(2)}, u32[]{:S(2)}) %collective-permute-start.35) | collective-permute-done | bytes 196640 | tf_op jit(solution)/shard_map/ppermute | solution.py:21
  292.9 9.2 %shard_map.110 = (bf16[384,1024]{1,0:T(8,128)(2,1)}, bf16[384,1024]{1,0:T(8,128)(2,1)}, bf16[384,2048]{1,0:T(8,128)(2,1)}) custom-call(s32[10]{0:T(128)} %pad_add_fusion.where_ref, bf16[384,256]{1,0:T(8,128)(2,1)} %get-tuple-element.159.refs_0_, bf16[384,256]{1,0:T(8,128)(2,1)} %copy-done.22, bf16[384,256]{1,0:T(8,128)(2,1)} %copy-done.23, ...), custom_call_target="tpu_custom_call" | custom-call | flops 393216 | bytes 393216 | tf_op jit(solution)/shard_map/pallas_call | solution.py:354
  305.6 6.5 %shard_map.111 = bf16[384,1024]{1,0:T(8,128)(2,1)} custom-call(s32[10]{0:T(128)} %pad_add_fusion.where_ref, bf16[384,2048]{1,0:T(8,128)(2,1)} %get-tuple-element.132.refs_0_, bf16[384,1024]{1,0:T(8,128)(2,1)} %copy-done.4, bf16[2048,4096]{1,0:T(8,128)(2,1)} %bitcast.92), custom_call_target="tpu_custom_call" | custom-call | flops 393216 | bytes 393216 | tf_op jit(solution)/shard_map/pallas_call | solution.py:354
  314.6 6.8 %shard_map.112 = f32[384,1024]{1,0:T(8,128)} custom-call(s32[10]{0:T(128)} %pad_add_fusion.where_ref, bf16[384,2048]{1,0:T(8,128)(2,1)} %get-tuple-element.132.refs_0_, bf16[384,1024]{1,0:T(8,128)(2,1)} %copy-done.3, bf16[2048,4096]{1,0:T(8,128)(2,1)} %bitcast.93), custom_call_target="tpu_custom_call" | custom-call | flops 393216 | bytes 393216 | tf_op jit(solution)/shard_map/pallas_call | solution.py:354
  321.4 10.6 %collective-permute-done.38 = bf16[384,1024]{1,0:T(8,128)(2,1)S(1)} collective-permute-done((bf16[384,1024]{1,0:T(8,128)(2,1)}, bf16[384,1024]{1,0:T(8,128)(2,1)S(1)}, u32[]{:S(2)}, u32[]{:S(2)}) %collective-permute-start.38) | collective-permute-done | bytes 786464 | tf_op jit(solution)/shard_map/ppermute | solution.py:21
  (199 shorter events, 79.2 us)
Async XLA Ops:
  6.5 189.0 %all-gather.15.cloned.1.call-start = ((), (), s32[]{:S(2)}) async-start(), calls=%async_computation | async-start | bytes 4718592 | tf_op jit(solution)/shard_map/all_gather | solution.py:382
  6.5 19.5 %collective-permute-start = (bf16[384,1024]{1,0:T(8,128)(2,1)}, bf16[384,1024]{1,0:T(8,128)(2,1)S(1)}, u32[]{:S(2)}, u32[]{:S(2)}) collective-permute-start(bf16[384,1024]{1,0:T(8,128)(2,1)} %param.11), channel_id=1, source_target_pairs={{0,2},{1,3},{2,0},{3,1},{4,6},{5,7},{6,4},{7,5},{8,10},{9,11},{10,... | collective-permute-start | bytes 2359304 | tf_op jit(solution)/shard_map/ppermute | solution.py:21
  8.0 19.3 %collective-permute-start.1 = (bf16[384,1024]{1,0:T(8,128)(2,1)}, bf16[384,1024]{1,0:T(8,128)(2,1)}, u32[]{:S(2)}, u32[]{:S(2)}) collective-permute-start(bf16[384,1024]{1,0:T(8,128)(2,1)} %param.11), channel_id=1, source_target_pairs={{0,4},{4,0},{8,12},{12,8},{16,20},{20,16},{24,28},{28,24},{1,5},{5... | collective-permute-start | bytes 2359304 | tf_op jit(solution)/shard_map/ppermute | solution.py:21
  9.6 19.0 %collective-permute-start.2 = (bf16[384,1024]{1,0:T(8,128)(2,1)}, bf16[384,1024]{1,0:T(8,128)(2,1)}, u32[]{:S(2)}, u32[]{:S(2)}) collective-permute-start(bf16[384,1024]{1,0:T(8,128)(2,1)} %param.11), channel_id=1, source_target_pairs={{0,8},{4,12},{8,0},{12,4},{16,24},{20,28},{24,16},{28,20},{1,9},{5... | collective-permute-start | bytes 2359304 | tf_op jit(solution)/shard_map/ppermute | solution.py:21
  10.0 21.5 %collective-permute-start.3 = (bf16[384,1024]{1,0:T(8,128)(2,1)}, bf16[384,1024]{1,0:T(8,128)(2,1)S(1)}, u32[]{:S(2)}, u32[]{:S(2)}) collective-permute-start(bf16[384,1024]{1,0:T(8,128)(2,1)} %param.11), channel_id=1, source_target_pairs={{8,16},{12,20},{16,8},{20,12},{9,17},{13,21},{17,9},{21,13},{10,18... | collective-permute-start | bytes 2359304 | tf_op jit(solution)/shard_map/ppermute | solution.py:373
  34.1 161.4 %all-gather.23.cloned.1.call-start = ((), (), s32[]{:S(2)}) async-start(), calls=%async_computation.4 | async-start | bytes 4718592 | tf_op jit(solution)/shard_map/all_gather | solution.py:382
  34.4 18.1 %collective-permute-start.4 = (bf16[384,1024]{1,0:T(8,128)(2,1)}, bf16[384,1024]{1,0:T(8,128)(2,1)S(1)}, u32[]{:S(2)}, u32[]{:S(2)}) collective-permute-start(bf16[384,1024]{1,0:T(8,128)(2,1)} %collective-permute-done.1), channel_id=1, source_target_pairs={{0,2},{1,3},{2,0},{3,1},{4,6},{5,7},{6,4},{7,5},{8,10},{9,11},{10,... | collective-permute-start | bytes 2359304 | tf_op jit(solution)/shard_map/ppermute | solution.py:21
  35.5 19.3 %collective-permute-start.6 = (bf16[384,1024]{1,0:T(8,128)(2,1)}, bf16[384,1024]{1,0:T(8,128)(2,1)S(1)}, u32[]{:S(2)}, u32[]{:S(2)}) collective-permute-start(bf16[384,1024]{1,0:T(8,128)(2,1)} %collective-permute-done.2), channel_id=1, source_target_pairs={{8,16},{12,20},{16,8},{20,12},{9,17},{13,21},{17,9},{21,13},{10,18... | collective-permute-start | bytes 2359304 | tf_op jit(solution)/shard_map/ppermute | solution.py:373
  59.3 136.2 %all-gather.17.cloned.1.call-start = ((), (), s32[]{:S(2)}) async-start(), calls=%async_computation.1 | async-start | bytes 4718592 | tf_op jit(solution)/shard_map/all_gather | solution.py:382
  63.1 132.4 %all-gather.25.cloned.1.call-start = ((), (), s32[]{:S(2)}) async-start(), calls=%async_computation.5 | async-start | bytes 4718592 | tf_op jit(solution)/shard_map/all_gather | solution.py:382
  65.9 18.4 %collective-permute-start.10 = (bf16[512,512]{1,0:T(8,128)(2,1)}, bf16[512,512]{1,0:T(8,128)(2,1)S(1)}, u32[]{:S(2)}, u32[]{:S(2)}) collective-permute-start(bf16[512,512]{1,0:T(8,128)(2,1)} %get-tuple-element.83), channel_id=1, source_target_pairs={{0,4},{4,0},{8,12},{12,8},{16,20},{20,16},{24,28},{28,24},{1,5},{5... | collective-permute-start | bytes 1572872 | tf_op jit(solution)/shard_map/ppermute | solution.py:21
  67.5 37.6 %collective-permute-start.8 = (bf16[384,1024]{1,0:T(8,128)(2,1)}, bf16[384,1024]{1,0:T(8,128)(2,1)S(1)}, u32[]{:S(2)}, u32[]{:S(2)}) collective-permute-start(bf16[384,1024]{1,0:T(8,128)(2,1)} %collective-permute-done.2), channel_id=1, source_target_pairs={{0,2},{1,3},{2,0},{3,1},{4,6},{5,7},{6,4},{7,5},{8,10},{9,11},{10,... | collective-permute-start | bytes 2359304 | tf_op jit(solution)/shard_map/ppermute | solution.py:21
  68.9 35.2 %collective-permute-start.12 = (bf16[384,1024]{1,0:T(8,128)(2,1)S(1)}, bf16[384,1024]{1,0:T(8,128)(2,1)S(1)}, u32[]{:S(2)}, u32[]{:S(2)}) collective-permute-start(bf16[384,1024]{1,0:T(8,128)(2,1)S(1)} %broadcast_select_fusion.1), channel_id=1, source_target_pairs={{0,4},{4,0},{8,12},{12,8},{16,20},{20,16},{24,28},{28,24},{1,5},{5... | collective-permute-start | bytes 2359304 | tf_op jit(solution)/shard_map/ppermute | solution.py:21
  69.5 34.7 %collective-permute-start.13 = (bf16[384,1024]{1,0:T(8,128)(2,1)S(1)}, bf16[384,1024]{1,0:T(8,128)(2,1)S(1)}, u32[]{:S(2)}, u32[]{:S(2)}) collective-permute-start(bf16[384,1024]{1,0:T(8,128)(2,1)S(1)} %collective-permute-done.6), channel_id=1, source_target_pairs={{8,0},{12,4},{16,24},{20,28},{9,1},{13,5},{17,25},{21,29},{10,2},{... | collective-permute-start | bytes 2359304 | tf_op jit(solution)/shard_map/ppermute | solution.py:373
  73.7 31.3 %collective-permute-start.9 = (bf16[384,1024]{1,0:T(8,128)(2,1)}, bf16[384,1024]{1,0:T(8,128)(2,1)S(1)}, u32[]{:S(2)}, u32[]{:S(2)}) collective-permute-start(bf16[384,1024]{1,0:T(8,128)(2,1)} %copy-done.10), channel_id=1, source_target_pairs={{0,2},{1,3},{2,0},{3,1},{4,6},{5,7},{6,4},{7,5},{8,10},{9,11},{10,... | collective-permute-start | bytes 2359304 | tf_op jit(solution)/shard_map/ppermute | solution.py:21
  106.5 89.0 %all-gather.19.cloned.1.call-start = ((), (), s32[]{:S(2)}) async-start(), calls=%async_computation.2 | async-start | bytes 4718592 | tf_op jit(solution)/shard_map/all_gather | solution.py:382
  109.9 85.7 %all-gather.27.cloned.1.call-start = ((), (), s32[]{:S(2)}) async-start(), calls=%async_computation.6 | async-start | bytes 4718592 | tf_op jit(solution)/shard_map/all_gather | solution.py:382
  109.9 20.6 %collective-permute-start.17 = (bf16[512,512]{1,0:T(8,128)(2,1)}, bf16[512,512]{1,0:T(8,128)(2,1)S(1)}, u32[]{:S(2)}, u32[]{:S(2)}) collective-permute-start(bf16[512,512]{1,0:T(8,128)(2,1)} %pad_maximum_fusion.11), channel_id=1, source_target_pairs={{0,8},{4,12},{8,0},{12,4},{16,24},{20,28},{24,16},{28,20},{1,9},{5... | collective-permute-start | bytes 1572872 | tf_op jit(solution)/shard_map/ppermute | solution.py:21
  111.2 36.9 %collective-permute-start.15 = (bf16[384,1024]{1,0:T(8,128)(2,1)S(1)}, bf16[384,1024]{1,0:T(8,128)(2,1)S(1)}, u32[]{:S(2)}, u32[]{:S(2)}) collective-permute-start(bf16[384,1024]{1,0:T(8,128)(2,1)S(1)} %broadcast_select_fusion.1), channel_id=1, source_target_pairs={{0,2},{1,3},{2,0},{3,1},{4,6},{5,7},{6,4},{7,5},{8,10},{9,11},{10,... | collective-permute-start | bytes 2359304 | tf_op jit(solution)/shard_map/ppermute | solution.py:21
  112.7 35.4 %collective-permute-start.16 = (bf16[384,1024]{1,0:T(8,128)(2,1)S(1)}, bf16[384,1024]{1,0:T(8,128)(2,1)S(1)}, u32[]{:S(2)}, u32[]{:S(2)}) collective-permute-start(bf16[384,1024]{1,0:T(8,128)(2,1)S(1)} %copy-done.14), channel_id=1, source_target_pairs={{0,2},{1,3},{2,0},{3,1},{4,6},{5,7},{6,4},{7,5},{8,10},{9,11},{10,... | collective-permute-start | bytes 2359304 | tf_op jit(solution)/shard_map/ppermute | solution.py:21
  113.2 35.8 %collective-permute-start.20 = (bf16[384,1024]{1,0:T(8,128)(2,1)S(1)}, bf16[384,1024]{1,0:T(8,128)(2,1)}, u32[]{:S(2)}, u32[]{:S(2)}) collective-permute-start(bf16[384,1024]{1,0:T(8,128)(2,1)S(1)} %broadcast_select_fusion), channel_id=1, source_target_pairs={{0,4},{4,0},{8,12},{12,8},{16,20},{20,16},{24,28},{28,24},{1,5},{5... | collective-permute-start | bytes 2359304 | tf_op jit(solution)/shard_map/ppermute | solution.py:21
  118.3 29.7 %collective-permute-start.21 = (bf16[1088,256]{1,0:T(8,128)(2,1)S(1)}, bf16[1088,256]{1,0:T(8,128)(2,1)S(1)}, u32[]{:S(2)}, u32[]{:S(2)}) collective-permute-start(bf16[1088,256]{1,0:T(8,128)(2,1)S(1)} %pad_maximum_fusion.8), channel_id=1, source_target_pairs={{0,8},{4,12},{8,0},{12,4},{16,24},{20,28},{24,16},{28,20},{1,9},{5... | collective-permute-start | bytes 1671176 | tf_op jit(solution)/shard_map/ppermute | solution.py:21
  150.4 45.2 %all-gather.21.cloned.1.call-start = ((), (), s32[]{:S(2)}) async-start(), calls=%async_computation.3 | async-start | bytes 4718592 | tf_op jit(solution)/shard_map/all_gather | solution.py:382
  154.5 36.6 %collective-permute-start.26 = (bf16[2176,256]{1,0:T(8,128)(2,1)S(1)}, bf16[2176,256]{1,0:T(8,128)(2,1)}, u32[]{:S(2)}, u32[]{:S(2)}) collective-permute-start(bf16[2176,256]{1,0:T(8,128)(2,1)S(1)} %pad_maximum_fusion.7.refs_18_), channel_id=1, source_target_pairs={{0,4},{4,0},{8,12},{12,8},{16,20},{20,16},{24,28},{28,24},{1,5},{5... | collective-permute-start | bytes 3342344 | tf_op jit(solution)/shard_map/ppermute | solution.py:21
  155.0 22.4 %collective-permute-start.25 = (bf16[256,512]{1,0:T(8,128)(2,1)}, bf16[256,512]{1,0:T(8,128)(2,1)}, u32[]{:S(2)}, u32[]{:S(2)}) collective-permute-start(bf16[256,512]{1,0:T(8,128)(2,1)} %get-tuple-element.115), channel_id=1, source_target_pairs={{0,24},{4,28},{8,16},{12,20},{16,8},{20,12},{24,0},{28,4},{1,25},{... | collective-permute-start | bytes 786440 | tf_op jit(solution)/shard_map/ppermute | solution.py:21
  156.2 34.0 %collective-permute-start.22 = (bf16[384,1024]{1,0:T(8,128)(2,1)S(1)}, bf16[384,1024]{1,0:T(8,128)(2,1)S(1)}, u32[]{:S(2)}, u32[]{:S(2)}) collective-permute-start(bf16[384,1024]{1,0:T(8,128)(2,1)S(1)} %broadcast_select_fusion), channel_id=1, source_target_pairs={{0,2},{1,3},{2,0},{3,1},{4,6},{5,7},{6,4},{7,5},{8,10},{9,11},{10,... | collective-permute-start | bytes 2359304 | tf_op jit(solution)/shard_map/ppermute | solution.py:21
  157.7 32.6 %collective-permute-start.23 = (bf16[384,1024]{1,0:T(8,128)(2,1)}, bf16[384,1024]{1,0:T(8,128)(2,1)S(1)}, u32[]{:S(2)}, u32[]{:S(2)}) collective-permute-start(bf16[384,1024]{1,0:T(8,128)(2,1)} %collective-permute-done.20), channel_id=1, source_target_pairs={{0,2},{1,3},{2,0},{3,1},{4,6},{5,7},{6,4},{7,5},{8,10},{9,11},{10,... | collective-permute-start | bytes 2359304 | tf_op jit(solution)/shard_map/ppermute | solution.py:21
  158.3 26.5 %collective-permute-start.24 = (bf16[512,512]{1,0:T(8,128)(2,1)}, bf16[512,512]{1,0:T(8,128)(2,1)S(1)}, u32[]{:S(2)}, u32[]{:S(2)}) collective-permute-start(bf16[512,512]{1,0:T(8,128)(2,1)} %pad_maximum_fusion.14), channel_id=1, source_target_pairs={{0,16},{4,20},{8,24},{12,28},{16,0},{20,4},{24,8},{28,12},{1,17},{... | collective-permute-start | bytes 1572872 | tf_op jit(solution)/shard_map/ppermute | solution.py:21
  256.7 26.4 %collective-permute-start.33 = (bf16[384,256]{1,0:T(8,128)(2,1)S(1)}, bf16[384,256]{1,0:T(8,128)(2,1)S(1)}, u32[]{:S(2)}, u32[]{:S(2)}) collective-permute-start(bf16[384,256]{1,0:T(8,128)(2,1)S(1)} %get-tuple-element.154), channel_id=1, source_target_pairs={{0,20},{4,16},{8,28},{12,24},{16,4},{20,0},{24,12},{28,8},{1,21},{... | collective-permute-start | bytes 589832 | tf_op jit(solution)/shard_map/ppermute | solution.py:21
  257.8 30.5 %collective-permute-start.34 = (bf16[384,256]{1,0:T(8,128)(2,1)S(1)}, bf16[384,256]{1,0:T(8,128)(2,1)S(1)}, u32[]{:S(2)}, u32[]{:S(2)}) collective-permute-start(bf16[384,256]{1,0:T(8,128)(2,1)S(1)} %get-tuple-element.153), channel_id=1, source_target_pairs={{0,24},{4,28},{8,16},{12,20},{16,8},{20,12},{24,0},{28,4},{1,25},{... | collective-permute-start | bytes 589832 | tf_op jit(solution)/shard_map/ppermute | solution.py:21
  266.2 26.0 %collective-permute-start.35 = (bf16[384,256]{1,0:T(8,128)(2,1)S(1)}, bf16[384,256]{1,0:T(8,128)(2,1)S(1)}, u32[]{:S(2)}, u32[]{:S(2)}) collective-permute-start(bf16[384,256]{1,0:T(8,128)(2,1)S(1)} %get-tuple-element.152), channel_id=1, source_target_pairs={{0,28},{4,24},{8,20},{12,16},{16,12},{20,8},{24,4},{28,0},{1,29},{... | collective-permute-start | bytes 589832 | tf_op jit(solution)/shard_map/ppermute | solution.py:21
  312.1 19.9 %collective-permute-start.38 = (bf16[384,1024]{1,0:T(8,128)(2,1)}, bf16[384,1024]{1,0:T(8,128)(2,1)S(1)}, u32[]{:S(2)}, u32[]{:S(2)}) collective-permute-start(bf16[384,1024]{1,0:T(8,128)(2,1)} %shard_map.111), channel_id=1, source_target_pairs={{0,2},{1,3},{2,0},{3,1},{4,6},{5,7},{6,4},{7,5},{8,10},{9,11},{10,... | collective-permute-start | bytes 2359304 | tf_op jit(solution)/shard_map/ppermute | solution.py:21
  (53 other events, 803.9 us)
Sparse Core Ops, SparseCore 0:
  34.2 10.7 all-gather.14
  59.4 13.4 all-gather.22
  74.4 13.2 all-gather.16
  106.6 12.0 all-gather.24
  120.1 13.2 all-gather.18
  150.5 13.5 all-gather.26
  165.6 13.2 all-gather.20
